TPU v7x, 128 devices: a whole 4x4x4 slice. The times are simulated.
128 devices in a mesh: ctx: 16 (over x, z), tp: 8 (over y, core).
Axes of the slice: x: 4, y: 4, z: 4, core: 2. Of those that a mesh axis runs over, the one named last changes fastest.
Arguments:
- tokens: bfloat16 [8192, 4096], P('ctx', 'tp'), may hold values from -6 to 6
- w_query: bfloat16 [4096, 2048], P(None, 'tp'), may hold values from -0.09375 to 0.09375
- w_key: bfloat16 [4096, 2048], P(None, 'tp'), may hold values from -0.09375 to 0.09375
- w_value: bfloat16 [4096, 4096], P(None, 'tp'), may hold values from -0.09375 to 0.09375
- w_gate: bfloat16 [4096, 4096], P(None, 'tp'), may hold values from -0.09375 to 0.09375
- w_out: bfloat16 [4096, 4096], P('tp'), may hold values from -0.125 to 0.125
- log_decay: float32 [8, 8192], P('tp', 'ctx'), may hold values from -0.7 to 0
Outputs:
- mixed: bfloat16 [8192, 4096], P('ctx', 'tp')
All inputs are finite; a program needn't handle non-finite values.
Results may differ from a plain program's by a relative error of at most 0.023.
Values may be sent and summed in bfloat16 or wider, within the bound.
No kernel may reach another device: no remote copies, remote signals or barrier semaphores. Data moves between devices by JAX's collectives and lax.ppermute only.
A program may use at most 128 MiB of HBM per device.

v0:
```python
import jax
import jax.numpy as jnp
from jax import lax
from jax.sharding import PartitionSpec as P

DK = 256
DV = 512


def entering_2(shard, axis, combine, identity):
    count, position = (lax.axis_size(axis), lax.axis_index(axis))
    everything = jax.tree.map(
        lambda part, kind: lax.all_gather(part.astype(kind), axis),
        shard,
        (jnp.bfloat16, jnp.bfloat16),
    )
    start = jax.tree.map(
        lambda part, zero: jnp.broadcast_to(jnp.asarray(zero, part.dtype), part.shape),
        shard,
        identity,
    )

    def turn(k, before):
        reached = k < position
        new = combine(
            before, jax.tree.map(lambda part, own: part[k].astype(own.dtype), everything, shard)
        )
        return jax.tree.map(lambda a, b: jnp.where(reached, a, b), new, before)

    return lax.fori_loop(0, count, turn, start)


def block_terms(query_block, key_block, value_block, rate_block, state):
    length = query_block.shape[0]
    cumulative = jnp.cumsum(rate_block)
    spread = cumulative[:, None] - cumulative[None, :]
    lower_mask = jnp.arange(length)[:, None] >= jnp.arange(length)[None, :]
    weights = jnp.exp(jnp.where(lower_mask, spread, -1e30))
    scores = jnp.dot(query_block, key_block.T, preferred_element_type=jnp.float32) * weights
    scores = scores.astype(jnp.bfloat16)
    inner_part = jnp.dot(scores, value_block, preferred_element_type=jnp.float32)
    carried = jnp.exp(cumulative)[:, None] * jnp.dot(
        query_block.astype(jnp.float32), state, precision=lax.Precision.HIGHEST
    )
    remain = jnp.exp(cumulative[-1] - cumulative)
    weighted_keys = key_block.astype(jnp.float32) * remain[:, None]
    new_state = jnp.exp(cumulative[-1]) * state + jnp.dot(
        weighted_keys.T, value_block.astype(jnp.float32), precision=lax.Precision.HIGHEST
    )
    return (inner_part + carried, new_state)


def group_norm(output):
    center = output - jnp.mean(output, axis=-1, keepdims=True)
    variance = jnp.mean(center * center, axis=-1, keepdims=True)
    return center * lax.rsqrt(variance + 1e-05)


def combine(earlier, latter):
    return (earlier[0] * latter[0], latter[0][:, None, None] * earlier[1] + latter[1])


def shards(tokens, w_query, w_key, w_value, w_gate, w_out, log_decay):
    row_count = tokens.shape[0]
    matrices = (w_query, w_key, w_value, w_gate)
    piece = lax.all_gather(tokens, "tp", axis=1, tiled=True)
    projected = tuple(
        (jnp.dot(piece, matrix, preferred_element_type=jnp.float32) for matrix in matrices)
    )
    queries = projected[0].astype(jnp.bfloat16)
    keys = (projected[1] * DK ** (-0.5)).astype(jnp.bfloat16)
    values = projected[2].astype(jnp.bfloat16)
    gates = projected[3].astype(jnp.bfloat16)
    block_size = min(512, row_count)
    block_count = row_count // block_size
    head_index = 0
    query_head = queries.reshape(block_count, block_size, DK)
    key_head = keys.reshape(block_count, block_size, DK)
    value_head = values.reshape(block_count, block_size, DV)
    rate_head = log_decay[head_index].reshape(block_count, block_size)

    def advance(state, inputs):
        output, new_state = block_terms(inputs[0], inputs[1], inputs[2], inputs[3], state)
        return (new_state, output)

    final_state, outputs = lax.scan(
        advance, jnp.zeros((DK, DV), jnp.float32), (query_head, key_head, value_head, rate_head)
    )
    local_outputs = [outputs.reshape(row_count, DV)]
    local_states = [final_state]
    shard_cumuls = [jnp.cumsum(log_decay[head_index])]
    factors = jnp.exp(jnp.stack([cumul_row[-1] for cumul_row in shard_cumuls]))
    states = jnp.stack(local_states)
    entering = entering_2(
        (factors, states), "ctx", combine, (jnp.ones_like(factors), jnp.zeros_like(states))
    )[1]
    head_index = 0
    query_rows = queries.astype(jnp.float32)
    incoming = jnp.exp(shard_cumuls[head_index])[:, None] * jnp.dot(
        query_rows, entering[head_index], precision=lax.Precision.HIGHEST
    )
    normed = group_norm(local_outputs[head_index] + incoming)
    gate_head = gates.astype(jnp.float32)
    pieces = jax.nn.silu(gate_head) * normed
    hidden = pieces.astype(jnp.bfloat16)
    partial_terms = jnp.dot(hidden, w_out, preferred_element_type=jnp.float32)
    return lax.psum_scatter(
        partial_terms.astype(jnp.bfloat16), "tp", scatter_dimension=1, tiled=True
    )


def solution(mesh):
    in_specs = (
        P("ctx", "tp"),
        P(None, "tp"),
        P(None, "tp"),
        P(None, "tp"),
        P(None, "tp"),
        P("tp", None),
        P("tp", "ctx"),
    )
    out_specs = P("ctx", "tp")
    return jax.shard_map(shards, mesh=mesh, in_specs=in_specs, out_specs=out_specs, check_vma=False)
```

profile of v0, /device:TPU:0, one launch (start us, length us, event | category | flops | bytes accessed | tf_op | source)
XLA Modules:
  0.0 203.8 jit_solution(2281712014715713913)
XLA Ops:
  10.5 33.1 %all-gather.5.cloned.1.call-done = bf16[512,4096]{1,0:T(8,128)(2,1)} async-done(((bf16[512,512]{1,0:T(8,128)(2,1)}), bf16[512,4096]{1,0:T(8,128)(2,1)}) %all-gather.5.cloned.1.call-update) | async-done | bytes 4194320 | tf_op jit(solution)/shard_map/all_gather | solution.py:66
  43.7 5.9 %convolution_convert_fusion.1 = bf16[512,512]{1,0:T(8,128)(2,1)S(1)} fusion(bf16[512,4096]{1,0:T(8,128)(2,1)} %all-gather.5.cloned.1.call-done, bf16[4096,512]{1,0:T(8,128)(2,1)} %param.12), kind=kOutput, calls=%fused_computation.11 | convolution fusion | flops 2147745792 | bytes 8912896 | tf_op jit(solution)/shard_map/dot_general | solution.py:68
  49.6 1.3 fusion.5
  50.9 1.4 fusion.6
  53.1 1.3 dynamic-update-slice
  54.4 40.8 %all-reduce = bf16[16]{0:T(256)(128)(2,1)S(1)} all-reduce(bf16[16]{0:T(256)(128)(2,1)S(1)} %dynamic-update-slice), channel_id=2, replica_groups=mesh['ctx'=16,'tp'=8] {'ctx'}, use_global_device_ids=true, to_apply=%add | all-reduce | flops 16 | bytes 64
  95.1 4.2 %convolution_convert_fusion.3 = bf16[512,256]{1,0:T(8,128)(2,1)S(1)} fusion(bf16[512,4096]{1,0:T(8,128)(2,1)} %all-gather.5.cloned.1.call-done, bf16[4096,256]{1,0:T(8,128)(2,1)} %param.10), kind=kOutput, calls=%fused_computation.19 | convolution fusion | flops 1073872896 | bytes 6553600 | tf_op jit(solution)/shard_map/dot_general | solution.py:68
  99.4 2.6 %fusion.4 = f32[512,512]{1,0:T(8,128)} fusion(bf16[512,512]{1,0:T(8,128)(2,1)S(1)} %convolution_convert_fusion.1, bf16[512,256]{1,0:T(8,128)(2,1)S(1)} %convolution_convert_fusion.3, bf16[512,256]{1,0:T(8,128)(2,1)} %copy-done.4, f32[512]{0:T(512)S(1)} %get-tuple-element.160), kind=kOutput, calls=%fused_computation.14 | convolution fusion | flops 403963904 | bytes 2099200 | tf_op jit(solution)/shard_map/while/body/eval_jaxpr/dot_general | solution.py:41
  102.0 2.8 %fusion.2 = f32[512,512]{1,0:T(8,128)} fusion(f32[512,512]{1,0:T(8,128)} %fusion.4, bf16[512,256]{1,0:T(8,128)(2,1)S(1)} %convolution_convert_fusion.3, f32[512]{0:T(512)S(1)} %get-tuple-element.159), kind=kOutput, calls=%fused_computation.7 | convolution fusion | flops 805830656 | bytes 2361344 | tf_op jit(solution)/shard_map/while/body/eval_jaxpr/dot_general | solution.py:42
  104.9 40.5 %while.9 = (s32[]{:T(128)}, f32[1,256,512]{2,1,0:T(8,128)S(1)}, s32[]{:T(128)}, bf16[16,1]{0,1:T(2,128)(2,1)S(1)}, bf16[16,1,256,512]{3,2,1,0:T(8,128)(2,1)}, /*index=5*/s32[]{:T(128)}, s32[]{:T(128)}) while((s32[]{:T(128)}, f32[1,256,512]{2,1,0:T(8,128)S(1)}, s32[]{:T(128)}, bf16[16,1]{0,1:T(2,128)(2,1)S(1)}, ...), condition=%wide.region_3.4_spmd.clone, body=%wide.region_2.3_spmd.clone.sunk | while | flops 655365 | bytes 1310839 | solution.py:30
  106.1 1.3 fusion.48
  108.6 1.3 fusion.48
  111.2 1.3 fusion.48
  113.7 1.3 fusion.48
  116.2 1.3 fusion.48
  118.8 1.3 fusion.48
  121.3 1.3 fusion.48
  123.8 1.3 fusion.48
  126.4 1.3 fusion.48
  128.9 1.3 fusion.48
  131.4 1.3 fusion.48
  145.4 2.0 fusion.31
  148.7 11.6 %convolution_convert_fusion = bf16[512,4096]{1,0:T(8,128)(2,1)} fusion(bf16[512,4096]{1,0:T(8,128)(2,1)} %param.14, bf16[512,4096]{1,0:T(8,128)(2,1)} %all-gather.5.cloned.1.call-done, bf16[4096,512]{1,0:T(8,128)(2,1)} %param.13, f32[512,512]{1,0:T(8,128)} %copy-done.1, f32[512]{0:T(512)S(1)} %add_rsqrt_fusion, f32[512]{0:T(512)S(1)} %broadcast_multiply_fusion), kind=kOutput, calls=%fused_computation.3 | convolution fusion | flops 4299685888 | bytes 17829888 | tf_op jit(solution)/shard_map/dot_general | solution.py:106
  160.3 36.9 %reduce-scatter.2.cloned.1.call-done = bf16[512,512]{1,0:T(8,128)(2,1)} async-done(((bf16[512,4096]{1,0:T(8,128)(2,1)}), bf16[512,512]{1,0:T(8,128)(2,1)}) %reduce-scatter.2.cloned.1.call-update) | async-done | bytes 524304 | tf_op jit(solution)/shard_map/reduce_scatter | solution.py:107
  (51 shorter events, 21.0 us)
Async XLA Ops:
  6.5 43.1 %copy-start = (bf16[4096,256]{1,0:T(8,128)(2,1)S(1)}, bf16[4096,256]{1,0:T(8,128)(2,1)}, u32[]{:S(2)}) copy-start(bf16[4096,256]{1,0:T(8,128)(2,1)} %param.11) | copy-start | bytes 6291460
  6.5 37.1 %all-gather.5.cloned.1.call-start = ((), (), s32[]{:S(2)}) async-start(), calls=%async_computation.1 | async-start | bytes 4718592 | tf_op jit(solution)/shard_map/all_gather | solution.py:66
  7.3 97.6 %all-gather.7.cloned.1.call-start = ((), (), s32[]{:S(2)}) async-start(), calls=%async_computation.3 | async-start | bytes 4456448 | tf_op jit(solution)/shard_map/all_gather | solution.py:13
  43.7 5.9 %copy-start.2 = (bf16[512,4096]{1,0:T(8,128)(2,1)S(1)}, bf16[512,4096]{1,0:T(8,128)(2,1)}, u32[]{:S(2)}) copy-start(bf16[512,4096]{1,0:T(8,128)(2,1)} %all-gather.5.cloned.1.call-done) | copy-start | bytes 12582916
  49.6 2.8 %copy-start.3 = (u32[128]{0:T(128)S(1)}, u32[128]{0:T(128)}, u32[]{:S(2)}) copy-start(u32[128]{0:T(128)} %constant.70) | copy-start | bytes 1540
  50.9 3.5 %copy-start.4 = (bf16[512,256]{1,0:T(8,128)(2,1)}, bf16[512,256]{1,0:T(8,128)(2,1)S(1)}, u32[]{:S(2)}) copy-start(bf16[512,256]{1,0:T(8,128)(2,1)S(1)} %fusion.5) | copy-start | bytes 786436
  52.4 144.9 %reduce-scatter.2.cloned.1.call-start = ((), (), s32[]{:S(2)}) async-start(), calls=%async_computation.2 | async-start | bytes 4718592 | tf_op jit(solution)/shard_map/reduce_scatter | solution.py:107
  147.4 1.1 copy-start.1
Sparse Core Ops, SparseCore 0:
  9.1 34.5 all-gather.4
  52.5 51.7 all-gather.6
  160.5 36.7 reduce-scatter.1
where the time goes:
time: 205 us; the launch traced here: 204 us
  waiting for transfers between devices  70.8 us (35%)
  blocking collectives  40.8 us (20%)
  matrix products  31.9 us (16%)
  other arithmetic  22.9 us (11%)
  between operations  13.9 us (7%)
  local copies, waits for them, and re-layouts  12.5 us (6%)
  loops' own time  10.9 us (5%)
    unnamed x1, blocking collectives  40.8 us
    reduce_scatter x1, waiting for transfers between devices, shards(): lax.psum_scatter(partial_terms.astype(jnp.bfloat16), 'tp', scatter_dimens...  36.9 us
    all_gather x1, waiting for transfers between devices, shards(): piece = lax.all_gather(tokens, 'tp', axis=1, tiled=True)  33.1 us
    select_n x16, other arithmetic, turn(): return jax.tree.map(lambda a, b: jnp.where(reached, a, b), new, before)  20.3 us
    dot_general x1, matrix products, shards(): partial_terms = jnp.dot(hidden, w_out, preferred_element_type=jnp.float32)  11.6 us
    dot_general x3, matrix products, shards(): jnp.dot(piece, matrix, preferred_element_type=jnp.float32)  11.4 us
    another operation x1, loops' own time, entering_2(): return lax.fori_loop(0, count, turn, start)  10.9 us
    dynamic_slice x16, local copies, waits for them, and re-layouts, turn(): part[k].astype(own.dtype)  9.37 us
  transfers between devices with their start and end apart: 3, of which 2 were waited for; matrix products, arithmetic and copies ran while one was open for 7% of the time, Pallas kernels for 0%

commit v1 on v0

v1 whole, which is shorter than its diff:
```python
import jax
import jax.numpy as jnp
from jax import lax
from jax.sharding import PartitionSpec as P

DK = 256
DV = 512
BF, F32 = jnp.bfloat16, jnp.float32
SIDE = 4


def tp_shift(value, step):
    pairs = [(i, (i + 2 * step) % 8) for i in range(8)]
    return lax.ppermute(value, "tp", pairs)


def tp_swap(value):
    return lax.ppermute(value, "tp", [(i, i ^ 1) for i in range(8)])


def z_flip(value, k):
    return lax.ppermute(value, "ctx", [(i, i ^ k) for i in range(16)])


def x_flip(value, k):
    return lax.ppermute(value, "ctx", [(i, i ^ (4 * k)) for i in range(16)])


def dot(a, b):
    return jnp.dot(a, b, preferred_element_type=F32)


def packed(piece, factor):
    high = lax.reduce_precision(factor, 8, 7)
    rows = jnp.concatenate([jnp.full((8, DV), high, F32), jnp.full((8, DV), factor - high, F32)])
    return jnp.concatenate([piece.astype(BF), rows.astype(BF)])


def unpacked(message):
    factor = message[64, 0].astype(F32) + message[72, 0].astype(F32)
    return message[:64].astype(F32), factor


def between(factors, sources, low, high):
    product = jnp.float32(1.0)
    for factor, source in zip(factors, sources):
        product = product * jnp.where((source > low) & (source < high), factor, 1.0)
    return product


def prefix(pieces, factors, sources, target):
    total = jnp.zeros_like(pieces[0])
    for piece, source in zip(pieces, sources):
        weight = jnp.where(source < target, between(factors, sources, source, target), 0.0)
        total = total + weight * piece
    return total


def shards(tokens, w_query, w_key, w_value, w_gate, w_out, log_decay):
    ctx, tp = lax.axis_index("ctx"), lax.axis_index("tp")
    x, z, y, core = ctx // SIDE, ctx % SIDE, tp // 2, tp % 2

    top, low = tokens[:256], tokens[256:]
    a_right, a_left = tp_shift(top, 1), tp_shift(low, -1)
    b_right, b_left = tp_shift(low, 1), tp_shift(top, -1)
    c_right, c_left = tp_shift(a_right, 1), tp_shift(a_left, -1)
    before = jnp.concatenate([a_right, b_right])
    after = jnp.concatenate([b_left, a_left])
    across = jnp.concatenate([c_right, c_left])
    parts = []
    for block, step in ((tokens, 0), (before, -1), (after, 1), (across, 2)):
        owner = (y + step) % SIDE
        parts.append((block, 2 * owner + core))
        parts.append((tp_swap(block), 2 * owner + 1 - core))

    w_out_blocks = w_out.reshape(DV, SIDE, 2, DV)
    w_own = lax.dynamic_index_in_dim(w_out_blocks, core, 2, keepdims=False)
    w_other = tp_swap(lax.dynamic_index_in_dim(w_out_blocks, 1 - core, 2, keepdims=False))

    def project(weight):
        total = 0.0
        for block, owner in parts:
            total = total + dot(block, lax.dynamic_slice_in_dim(weight, owner * 512, 512))
        return total

    keys = (project(w_key) * DK ** (-0.5)).astype(BF)
    values = project(w_value).astype(BF)
    cumul = jnp.cumsum(log_decay[0])
    remain = jnp.exp(cumul[-1] - cumul)
    factor = jnp.exp(cumul[-1])
    weighted = (keys.astype(F32) * remain[:, None]).astype(BF)
    state = lax.dot_general(weighted, values, (((0,), (0,)), ((), ())), preferred_element_type=F32)

    def cut(whole, k):
        return lax.dynamic_slice_in_dim(whole, (z ^ k) * 64, 64)

    near = [z ^ k for k in range(SIDE)]
    got = [unpacked(z_flip(packed(cut(state, k), factor), k)) for k in range(1, SIDE)]
    pieces = [cut(state, 0)] + [piece for piece, _ in got]
    factors = [factor] + [f for _, f in got]
    line = prefix(pieces, factors, near, SIDE)
    line_factor = between(factors, near, -1, SIDE)
    far = [x ^ k for k in range(1, SIDE)]
    lines = [unpacked(x_flip(packed(line, line_factor), k)) for k in range(1, SIDE)]
    entry = prefix([p for p, _ in lines], [f for _, f in lines], far, x)

    def entering(target):
        return prefix(pieces, factors, near, target) + between(factors, near, -1, target) * entry

    slices = [entering(z)] + [z_flip(entering(z ^ k).astype(BF), k) for k in range(1, SIDE)]

    queries = project(w_query).astype(BF)
    gates = project(w_gate).astype(BF).astype(F32)
    spread = cumul[:, None] - cumul[None, :]
    mask = jnp.arange(512)[:, None] >= jnp.arange(512)[None, :]
    weights = jnp.exp(jnp.where(mask, spread, -1e30))
    scores = lax.dot_general(queries, keys, (((1,), (1,)), ((), ())), preferred_element_type=F32)
    local = dot((scores * weights).astype(BF), values)

    whole = jnp.zeros((DK, DV), BF)
    for k in range(SIDE):
        whole = lax.dynamic_update_slice_in_dim(whole, slices[k].astype(BF), (z ^ k) * 64, 0)
    retained = local + jnp.exp(cumul)[:, None] * dot(queries, whole)
    center = retained - jnp.mean(retained, axis=-1, keepdims=True)
    variance = jnp.mean(center * center, axis=-1, keepdims=True)
    normed = center * lax.rsqrt(variance + 1e-5)
    hidden = (jax.nn.silu(gates) * normed).astype(BF)
    other = tp_swap(hidden)

    def partial(step):
        owner = (y + step) % SIDE
        mine = lax.dynamic_index_in_dim(w_own, owner, 1, keepdims=False)
        theirs = lax.dynamic_index_in_dim(w_other, owner, 1, keepdims=False)
        return dot(hidden, mine) + dot(other, theirs)

    opposite = partial(2).astype(BF)
    via_right, via_left = tp_shift(opposite[:256], 1), tp_shift(opposite[256:], -1)
    right, left = partial(1), partial(-1)
    low_right, top_left = tp_shift(right[256:].astype(BF), 1), tp_shift(left[:256].astype(BF), -1)
    top_right = tp_shift((right[:256] + via_right.astype(F32)).astype(BF), 1)
    low_left = tp_shift((left[256:] + via_left.astype(F32)).astype(BF), -1)
    own = partial(0)
    out_top = own[:256] + top_right.astype(F32) + top_left.astype(F32)
    out_low = own[256:] + low_right.astype(F32) + low_left.astype(F32)
    return jnp.concatenate([out_top, out_low]).astype(BF)


def solution(mesh):
    in_specs = (P("ctx", "tp"),) + (P(None, "tp"),) * 4 + (P("tp", None), P("tp", "ctx"))
    return jax.shard_map(
        shards, mesh=mesh, in_specs=in_specs, out_specs=P("ctx", "tp"), check_vma=False
    )
```

time: 205 us -> 136 us (0.66)
  waiting for transfers between devices: 70.8 us -> 20.1 us
  blocking collectives: 40.8 us -> 0 us
  starting transfers between devices: 0.08 us -> 34.3 us
  other arithmetic: 22.9 us -> 3.12 us
  local copies, waits for them, and re-layouts: 12.5 us -> 24.5 us
  loops' own time: 10.9 us -> 0 us
  matrix products: 31.9 us -> 39.8 us
    unnamed x1 -> x0, blocking collectives: 40.8 us -> none
    reduce_scatter x1 -> x0, waiting for transfers between devices: 36.9 us -> none  [shards(): lax.psum_scatter(partial_terms.astype(jnp.bfloat16), 'tp', scatter_dimens...]
    ppermute x0 -> x27, starting transfers between devices: none -> 34.3 us  [the longest x12 19.8 us: tp_shift(): return lax.ppermute(value, 'tp', pairs)]
    all_gather x2 -> x0, waiting for transfers between devices: 33.1 us -> none  [the longest x1 33.1 us: shards(): piece = lax.all_gather(tokens, 'tp', axis=1, tiled=True)]
    select_n x16 -> x0, other arithmetic: 20.3 us -> none  [turn(): return jax.tree.map(lambda a, b: jnp.where(reached, a, b), new, before)]
    ppermute x0 -> x27, waiting for transfers between devices: none -> 20.1 us  [the longest x12 12.8 us: tp_shift(): return lax.ppermute(value, 'tp', pairs)]
    another operation x1 -> x0, loops' own time: 10.9 us -> none  [entering_2(): return lax.fori_loop(0, count, turn, start)]
    dot_general x8 -> x43, matrix products: 31.9 us -> 39.8 us  [the longest x42 39.4 us: dot(): return jnp.dot(a, b, preferred_element_type=F32)]
  transfers between devices with their start and end apart: 3 -> 27, of which waited for: 2 -> 10; matrix products, arithmetic and copies ran while one was open for 7% -> 47% of each run, Pallas kernels for 0% -> 0%
where the time goes in v1:
time: 136 us; the launch traced here: 135 us
  matrix products  39.8 us (29%)
  starting transfers between devices  34.3 us (25%)
  local copies, waits for them, and re-layouts  24.5 us (18%)
  waiting for transfers between devices  20.1 us (15%)
  between operations  12.7 us (9%)
  other arithmetic  3.12 us (2%)
    dot_general x42, matrix products, dot(): return jnp.dot(a, b, preferred_element_type=F32)  39.4 us
    ppermute x12, starting transfers between devices, tp_shift(): return lax.ppermute(value, 'tp', pairs)  19.8 us
    ppermute x12, waiting for transfers between devices, tp_shift(): return lax.ppermute(value, 'tp', pairs)  12.8 us
    unnamed x36, local copies, waits for them, and re-layouts  9.85 us
    ppermute x6, starting transfers between devices, z_flip(): return lax.ppermute(value, 'ctx', [(i, i ^ k) for i in range(16)])  9.72 us
    dynamic_slice x2, local copies, waits for them, and re-layouts, shards(): lax.dynamic_index_in_dim(w_out_blocks, 1 - core, 2, keepdims=False)  7.31 us
    ppermute x6, waiting for transfers between devices, z_flip(): return lax.ppermute(value, 'ctx', [(i, i ^ k) for i in range(16)])  4.44 us
    ppermute x3, starting transfers between devices, x_flip(): return lax.ppermute(value, 'ctx', [(i, i ^ 4 * k) for i in range(16)])  4.17 us
  transfers between devices with their start and end apart: 27, of which 10 were waited for; matrix products, arithmetic and copies ran while one was open for 47% of the time, Pallas kernels for 0%

profile of v1, /device:TPU:0, one launch (start us, length us, event | category | flops | bytes accessed | tf_op | source)
XLA Modules:
  0.0 134.5 jit_solution(8784474108831150924)
XLA Ops:
  0.0 2.0 %fusion.188 = (bf16[256,512]{1,0:T(8,128)(2,1)}, bf16[256,512]{1,0:T(8,128)(2,1)}) fusion(bf16[512,512]{1,0:T(8,128)(2,1)} %param.7), kind=kLoop, calls=%fused_computation.258 | loop fusion | bytes 1048576 | tf_op jit(solution)/shard_map/slice | solution.py:63
  2.0 1.8 %collective-permute-start.2 = (bf16[256,512]{1,0:T(8,128)(2,1)}, bf16[256,512]{1,0:T(8,128)(2,1)}, u32[]{:S(2)}, u32[]{:S(2)}) collective-permute-start(bf16[256,512]{1,0:T(8,128)(2,1)} %get-tuple-element.14), channel_id=1, source_target_pairs={{0,2},{1,3},{2,4},{3,5},{4,6},{5,7},{6,0},{7,1},{8,10},{9,11},{10,... | collective-permute-start | bytes 786440 | tf_op jit(solution)/shard_map/ppermute | solution.py:14
  5.8 2.7 %collective-permute-start.4 = (bf16[256,512]{1,0:T(8,128)(2,1)}, bf16[256,512]{1,0:T(8,128)(2,1)}, u32[]{:S(2)}, u32[]{:S(2)}) collective-permute-start(bf16[256,512]{1,0:T(8,128)(2,1)} %get-tuple-element.15), channel_id=1, source_target_pairs={{0,6},{1,7},{2,0},{3,1},{4,2},{5,3},{6,4},{7,5},{8,14},{9,15},{10,... | collective-permute-start | bytes 786440 | tf_op jit(solution)/shard_map/ppermute | solution.py:14
  8.5 2.2 %fusion.105 = f32[256,512]{1,0:T(8,128)} fusion(bf16[512,512]{1,0:T(8,128)(2,1)} %param.7, bf16[4096,256]{1,0:T(8,128)(2,1)S(1)} %copy-done, s32[]{:T(128)S(6)} %select_n.434), kind=kOutput, calls=%fused_computation.150 | convolution fusion | flops 134217728 | bytes 1310724 | tf_op jit(solution)/shard_map/dot_general | solution.py:30
  10.7 2.5 %fusion.74 = f32[512,512]{1,0:T(8,128)} fusion(bf16[512,512]{1,0:T(8,128)(2,1)S(1)} %copy-done.3, bf16[4096,512]{1,0:T(8,128)(2,1)} %param.10, s32[]{:T(128)S(6)} %select_n.434), kind=kOutput, calls=%fused_computation.104 | convolution fusion | flops 268435456 | bytes 2097156 | tf_op jit(solution)/shard_map/dot_general | solution.py:30
  14.9 2.1 %fusion.118 = f32[256,512]{1,0:T(8,128)} fusion(bf16[512,512]{1,0:T(8,128)(2,1)S(1)} %copy-done.3, bf16[4096,256]{1,0:T(8,128)(2,1)} %param.8, s32[]{:T(128)S(6)} %select_n.434), kind=kOutput, calls=%fused_computation.163 | convolution fusion | flops 134217728 | bytes 1310724 | tf_op jit(solution)/shard_map/dot_general | solution.py:30
  17.0 2.5 %fusion.90 = f32[512,512]{1,0:T(8,128)} fusion(bf16[512,512]{1,0:T(8,128)(2,1)S(1)} %copy-done.3, bf16[4096,512]{1,0:T(8,128)(2,1)} %param.11, s32[]{:T(128)S(6)} %select_n.434), kind=kOutput, calls=%fused_computation.120 | convolution fusion | flops 268435456 | bytes 2097156 | tf_op jit(solution)/shard_map/dot_general | solution.py:30
  19.5 6.5 %copy.80 = bf16[512,4096]{0,1:T(8,128)(2,1)} copy(bf16[512,4096]{1,0:T(8,128)(2,1)} %param.12) | data formatting | bytes 8388608 | tf_op args[5]
  26.0 3.1 %constant_dynamic-slice_fusion = bf16[512,4,1,512]{0,3,2,1:T(8,128)(2,1)} fusion(bf16[512,4,2,512]{0,3,2,1:T(8,128)(2,1)} %bitcast.95, s32[]{:T(128)S(6)} %select_n.533), kind=kLoop, calls=%fused_computation.211 | loop fusion | bytes 4194308 | tf_op jit(solution)/shard_map/jit(dynamic_index_in_dim)/dynamic_slice | solution.py:78
  31.7 4.2 %copy.82 = bf16[512,4,1,512]{3,0,2,1:T(8,128)(2,1)} copy(bf16[512,4,1,512]{0,3,2,1:T(8,128)(2,1)} %constant_dynamic-slice_fusion) | data formatting | bytes 4194304 | tf_op jit(solution)/shard_map/jit(dynamic_index_in_dim)/dynamic_slice | solution.py:78
  41.2 3.0 %collective-permute-start.8 = (bf16[256,512]{1,0:T(8,128)(2,1)S(1)}, bf16[256,512]{1,0:T(8,128)(2,1)S(1)}, u32[]{:S(2)}, u32[]{:S(2)}) collective-permute-start(bf16[256,512]{1,0:T(8,128)(2,1)S(1)} %collective-permute-done.5), channel_id=1, source_target_pairs={{0,6},{1,7},{2,0},{3,1},{4,2},{5,3},{6,4},{7,5},{8,14},{9,15},{10,... | collective-permute-start | bytes 786440 | tf_op jit(solution)/shard_map/ppermute | solution.py:14
  46.3 3.5 %collective-permute-done.7 = bf16[256,512]{1,0:T(8,128)(2,1)S(1)} collective-permute-done((bf16[256,512]{1,0:T(8,128)(2,1)}, bf16[256,512]{1,0:T(8,128)(2,1)S(1)}, u32[]{:S(2)}, u32[]{:S(2)}) %collective-permute-start.7) | collective-permute-done | bytes 262176 | tf_op jit(solution)/shard_map/ppermute | solution.py:14
  61.8 4.2 %collective-permute-start.10 = (bf16[80,512]{1,0:T(8,128)(2,1)S(1)}, bf16[80,512]{1,0:T(8,128)(2,1)S(1)}, u32[]{:S(2)}, u32[]{:S(2)}) collective-permute-start(bf16[80,512]{1,0:T(8,128)(2,1)S(1)} %get-tuple-element.30), channel_id=1, source_target_pairs={{0,16},{8,24},{16,0},{24,8},{32,48},{40,56},{48,32},{56,40},{64,80... | collective-permute-start | bytes 245768 | tf_op jit(solution)/shard_map/ppermute | solution.py:22
  77.0 2.8 %collective-permute-start.14 = (bf16[80,512]{1,0:T(8,128)(2,1)S(1)}, bf16[80,512]{1,0:T(8,128)(2,1)S(1)}, u32[]{:S(2)}, u32[]{:S(2)}) collective-permute-start(bf16[80,512]{1,0:T(8,128)(2,1)S(1)} %pad_maximum_fusion.4), channel_id=1, source_target_pairs={{0,96},{8,104},{16,112},{24,120},{32,64},{40,72},{48,80},{56,88},{... | collective-permute-start | bytes 245768 | tf_op jit(solution)/shard_map/ppermute | solution.py:26
  79.8 2.5 %fusion.79 = f32[512,512]{0,1:T(8,128)} fusion(bf16[512,512]{1,0:T(8,128)(2,1)S(1)} %collective-permute-done.9, bf16[4096,512]{1,0:T(8,128)(2,1)} %param.11, s32[]{:T(128)S(6)} %select_n.444), kind=kOutput, calls=%fused_computation.109 | convolution fusion | flops 268435456 | bytes 2097156 | tf_op jit(solution)/shard_map/dot_general | solution.py:30
  85.6 2.8 %collective-permute-done.13 = bf16[80,512]{1,0:T(8,128)(2,1)S(1)} collective-permute-done((bf16[80,512]{1,0:T(8,128)(2,1)S(1)}, bf16[80,512]{1,0:T(8,128)(2,1)S(1)}, u32[]{:S(2)}, u32[]{:S(2)}) %collective-permute-start.13) | collective-permute-done | bytes 81952 | tf_op jit(solution)/shard_map/ppermute | solution.py:26
  92.4 3.2 %collective-permute-start.18 = (bf16[64,512]{1,0:T(8,128)(2,1)S(1)}, bf16[64,512]{1,0:T(8,128)(2,1)S(1)}, u32[]{:S(2)}, u32[]{:S(2)}) collective-permute-start(bf16[64,512]{1,0:T(8,128)(2,1)S(1)} %fusion.143), channel_id=1, source_target_pairs={{0,24},{8,16},{16,8},{24,0},{32,56},{40,48},{48,40},{56,32},{64,88... | collective-permute-start | bytes 196616 | tf_op jit(solution)/shard_map/ppermute | solution.py:22
  97.3 3.2 %collective-permute-done.16 = bf16[64,512]{1,0:T(8,128)(2,1)S(1)} collective-permute-done((bf16[64,512]{1,0:T(8,128)(2,1)S(1)}, bf16[64,512]{1,0:T(8,128)(2,1)S(1)}, u32[]{:S(2)}, u32[]{:S(2)}) %collective-permute-start.16) | collective-permute-done | bytes 65568 | tf_op jit(solution)/shard_map/ppermute | solution.py:22
  103.4 1.9 %fusion.33 = bf16[512,512]{0,1:T(8,128)(2,1)S(1)} fusion(f32[512,512]{0,1:T(8,128)S(1)} %copy-done.14, f32[512,512]{0,1:T(8,128)S(1)} %copy-done.13, bf16[512,512]{1,0:T(8,128)(2,1)S(1)} %copy-done.5, f32[512,512]{0,1:T(8,128)S(1)} %get-tuple-element.32, f32[512]{0:T(512)S(1)} %add_rsqrt_fusion, f32[512]{0:T(512)S(1)} %broadcast_multiply_fusion, ...), kind=kOutput, calls=%fused_computation.53 | convolution fusion | flops 271581184 | bytes 4722692 | tf_op jit(solution)/shard_map/dot_general | solution.py:30
  109.2 3.6 %collective-permute-start.25 = (bf16[256,512]{1,0:T(8,128)(2,1)S(1)}, bf16[256,512]{1,0:T(8,128)(2,1)S(1)}, u32[]{:S(2)}, u32[]{:S(2)}) collective-permute-start(bf16[256,512]{1,0:T(8,128)(2,1)S(1)} %get-tuple-element.10), channel_id=1, source_target_pairs={{0,6},{1,7},{2,0},{3,1},{4,2},{5,3},{6,4},{7,5},{8,14},{9,15},{10,... | collective-permute-start | bytes 786440 | tf_op jit(solution)/shard_map/ppermute | solution.py:14
  116.1 3.3 %collective-permute-start.23 = (bf16[256,512]{1,0:T(8,128)(2,1)S(1)}, bf16[256,512]{1,0:T(8,128)(2,1)S(1)}, u32[]{:S(2)}, u32[]{:S(2)}) collective-permute-start(bf16[256,512]{1,0:T(8,128)(2,1)S(1)} %slice.216), channel_id=1, source_target_pairs={{0,6},{1,7},{2,0},{3,1},{4,2},{5,3},{6,4},{7,5},{8,14},{9,15},{10,... | collective-permute-start | bytes 786440 | tf_op jit(solution)/shard_map/ppermute | solution.py:14
  119.4 3.2 %collective-permute-start.26 = (bf16[256,512]{1,0:T(8,128)(2,1)S(1)}, bf16[256,512]{1,0:T(8,128)(2,1)S(1)}, u32[]{:S(2)}, u32[]{:S(2)}) collective-permute-start(bf16[256,512]{1,0:T(8,128)(2,1)S(1)} %fusion.37), channel_id=1, source_target_pairs={{0,6},{1,7},{2,0},{3,1},{4,2},{5,3},{6,4},{7,5},{8,14},{9,15},{10,... | collective-permute-start | bytes 786440 | tf_op jit(solution)/shard_map/ppermute | solution.py:14
  125.1 3.8 %collective-permute-done.24 = bf16[256,512]{1,0:T(8,128)(2,1)S(1)} collective-permute-done((bf16[256,512]{1,0:T(8,128)(2,1)S(1)}, bf16[256,512]{1,0:T(8,128)(2,1)S(1)}, u32[]{:S(2)}, u32[]{:S(2)}) %collective-permute-start.24) | collective-permute-done | bytes 262176 | tf_op jit(solution)/shard_map/ppermute | solution.py:14
  130.4 3.1 %collective-permute-done.22 = bf16[256,512]{1,0:T(8,128)(2,1)S(1)} collective-permute-done((bf16[256,512]{1,0:T(8,128)(2,1)S(1)}, bf16[256,512]{1,0:T(8,128)(2,1)S(1)}, u32[]{:S(2)}, u32[]{:S(2)}) %collective-permute-start.22) | collective-permute-done | bytes 262176 | tf_op jit(solution)/shard_map/ppermute | solution.py:14
  (154 shorter events, 48.2 us)
Async XLA Ops:
  0.0 50.6 %collective-permute-start = (bf16[512,512]{1,0:T(8,128)(2,1)}, bf16[512,512]{1,0:T(8,128)(2,1)S(1)}, u32[]{:S(2)}, u32[]{:S(2)}) collective-permute-start(bf16[512,512]{1,0:T(8,128)(2,1)} %param.7), channel_id=1, source_target_pairs={{0,1},{1,0},{2,3},{3,2},{4,5},{5,4},{6,7},{7,6},{8,9},{9,8},{10,11... | collective-permute-start | bytes 1572872 | tf_op jit(solution)/shard_map/ppermute | solution.py:18
  2.0 43.2 %collective-permute-start.2 = (bf16[256,512]{1,0:T(8,128)(2,1)}, bf16[256,512]{1,0:T(8,128)(2,1)}, u32[]{:S(2)}, u32[]{:S(2)}) collective-permute-start(bf16[256,512]{1,0:T(8,128)(2,1)} %get-tuple-element.14), channel_id=1, source_target_pairs={{0,2},{1,3},{2,4},{3,5},{4,6},{5,7},{6,0},{7,1},{8,10},{9,11},{10,... | collective-permute-start | bytes 786440 | tf_op jit(solution)/shard_map/ppermute | solution.py:14
  3.8 33.3 %collective-permute-start.5 = (bf16[256,512]{1,0:T(8,128)(2,1)}, bf16[256,512]{1,0:T(8,128)(2,1)S(1)}, u32[]{:S(2)}, u32[]{:S(2)}) collective-permute-start(bf16[256,512]{1,0:T(8,128)(2,1)} %get-tuple-element.14), channel_id=1, source_target_pairs={{0,6},{1,7},{2,0},{3,1},{4,2},{5,3},{6,4},{7,5},{8,14},{9,15},{10,... | collective-permute-start | bytes 786440 | tf_op jit(solution)/shard_map/ppermute | solution.py:14
  5.2 34.3 %collective-permute-start.1 = (bf16[256,512]{1,0:T(8,128)(2,1)}, bf16[256,512]{1,0:T(8,128)(2,1)}, u32[]{:S(2)}, u32[]{:S(2)}) collective-permute-start(bf16[256,512]{1,0:T(8,128)(2,1)} %get-tuple-element.15), channel_id=1, source_target_pairs={{0,2},{1,3},{2,4},{3,5},{4,6},{5,7},{6,0},{7,1},{8,10},{9,11},{10,... | collective-permute-start | bytes 786440 | tf_op jit(solution)/shard_map/ppermute | solution.py:14
  5.8 30.1 %collective-permute-start.4 = (bf16[256,512]{1,0:T(8,128)(2,1)}, bf16[256,512]{1,0:T(8,128)(2,1)}, u32[]{:S(2)}, u32[]{:S(2)}) collective-permute-start(bf16[256,512]{1,0:T(8,128)(2,1)} %get-tuple-element.15), channel_id=1, source_target_pairs={{0,6},{1,7},{2,0},{3,1},{4,2},{5,3},{6,4},{7,5},{8,14},{9,15},{10,... | collective-permute-start | bytes 786440 | tf_op jit(solution)/shard_map/ppermute | solution.py:14
  35.9 71.7 %collective-permute-start.20 = (bf16[512,4,512]{2,0,1:T(8,128)(2,1)}, bf16[512,4,512]{2,0,1:T(8,128)(2,1)}, u32[]{:S(2)}, u32[]{:S(2)}) collective-permute-start(bf16[512,4,512]{2,0,1:T(8,128)(2,1)} %bitcast.100), channel_id=1, source_target_pairs={{0,1},{1,0},{2,3},{3,2},{4,5},{5,4},{6,7},{7,6},{8,9},{9,8},{10,11... | collective-permute-start | bytes 6291464 | tf_op jit(solution)/shard_map/ppermute | solution.py:18
  39.6 10.2 %collective-permute-start.7 = (bf16[256,512]{1,0:T(8,128)(2,1)}, bf16[256,512]{1,0:T(8,128)(2,1)S(1)}, u32[]{:S(2)}, u32[]{:S(2)}) collective-permute-start(bf16[256,512]{1,0:T(8,128)(2,1)} %collective-permute-done.1), channel_id=1, source_target_pairs={{0,2},{1,3},{2,4},{3,5},{4,6},{5,7},{6,0},{7,1},{8,10},{9,11},{10,... | collective-permute-start | bytes 786440 | tf_op jit(solution)/shard_map/ppermute | solution.py:14
  41.2 8.9 %collective-permute-start.8 = (bf16[256,512]{1,0:T(8,128)(2,1)S(1)}, bf16[256,512]{1,0:T(8,128)(2,1)S(1)}, u32[]{:S(2)}, u32[]{:S(2)}) collective-permute-start(bf16[256,512]{1,0:T(8,128)(2,1)S(1)} %collective-permute-done.5), channel_id=1, source_target_pairs={{0,6},{1,7},{2,0},{3,1},{4,2},{5,3},{6,4},{7,5},{8,14},{9,15},{10,... | collective-permute-start | bytes 786440 | tf_op jit(solution)/shard_map/ppermute | solution.py:14
  45.2 8.5 %collective-permute-start.6 = (bf16[512,512]{1,0:T(8,128)(2,1)S(1)}, bf16[512,512]{1,0:T(8,128)(2,1)S(1)}, u32[]{:S(2)}, u32[]{:S(2)}) collective-permute-start(bf16[512,512]{1,0:T(8,128)(2,1)S(1)} %constant_dynamic-update-slice_fusion.2), channel_id=1, source_target_pairs={{0,1},{1,0},{2,3},{3,2},{4,5},{5,4},{6,7},{7,6},{8,9},{9,8},{10,11... | collective-permute-start | bytes 1572872 | tf_op jit(solution)/shard_map/ppermute | solution.py:18
  50.2 9.4 %collective-permute-start.9 = (bf16[512,512]{1,0:T(8,128)(2,1)S(1)}, bf16[512,512]{1,0:T(8,128)(2,1)S(1)}, u32[]{:S(2)}, u32[]{:S(2)}) collective-permute-start(bf16[512,512]{1,0:T(8,128)(2,1)S(1)} %constant_dynamic-update-slice_fusion.4), channel_id=1, source_target_pairs={{0,1},{1,0},{2,3},{3,2},{4,5},{5,4},{6,7},{7,6},{8,9},{9,8},{10,11... | collective-permute-start | bytes 1572872 | tf_op jit(solution)/shard_map/ppermute | solution.py:18
  61.8 7.7 %collective-permute-start.10 = (bf16[80,512]{1,0:T(8,128)(2,1)S(1)}, bf16[80,512]{1,0:T(8,128)(2,1)S(1)}, u32[]{:S(2)}, u32[]{:S(2)}) collective-permute-start(bf16[80,512]{1,0:T(8,128)(2,1)S(1)} %get-tuple-element.30), channel_id=1, source_target_pairs={{0,16},{8,24},{16,0},{24,8},{32,48},{40,56},{48,32},{56,40},{64,80... | collective-permute-start | bytes 245768 | tf_op jit(solution)/shard_map/ppermute | solution.py:22
  66.0 5.5 %collective-permute-start.12 = (bf16[80,512]{1,0:T(8,128)(2,1)S(1)}, bf16[80,512]{1,0:T(8,128)(2,1)S(1)}, u32[]{:S(2)}, u32[]{:S(2)}) collective-permute-start(bf16[80,512]{1,0:T(8,128)(2,1)S(1)} %get-tuple-element.29), channel_id=1, source_target_pairs={{0,8},{8,0},{16,24},{24,16},{32,40},{40,32},{48,56},{56,48},{64,72... | collective-permute-start | bytes 245768 | tf_op jit(solution)/shard_map/ppermute | solution.py:22
  67.0 6.2 %collective-permute-start.11 = (bf16[80,512]{1,0:T(8,128)(2,1)S(1)}, bf16[80,512]{1,0:T(8,128)(2,1)S(1)}, u32[]{:S(2)}, u32[]{:S(2)}) collective-permute-start(bf16[80,512]{1,0:T(8,128)(2,1)S(1)} %get-tuple-element.28), channel_id=1, source_target_pairs={{0,24},{8,16},{16,8},{24,0},{32,56},{40,48},{48,40},{56,32},{64,88... | collective-permute-start | bytes 245768 | tf_op jit(solution)/shard_map/ppermute | solution.py:22
  77.0 6.7 %collective-permute-start.14 = (bf16[80,512]{1,0:T(8,128)(2,1)S(1)}, bf16[80,512]{1,0:T(8,128)(2,1)S(1)}, u32[]{:S(2)}, u32[]{:S(2)}) collective-permute-start(bf16[80,512]{1,0:T(8,128)(2,1)S(1)} %pad_maximum_fusion.4), channel_id=1, source_target_pairs={{0,96},{8,104},{16,112},{24,120},{32,64},{40,72},{48,80},{56,88},{... | collective-permute-start | bytes 245768 | tf_op jit(solution)/shard_map/ppermute | solution.py:26
  82.3 6.1 %collective-permute-start.13 = (bf16[80,512]{1,0:T(8,128)(2,1)S(1)}, bf16[80,512]{1,0:T(8,128)(2,1)S(1)}, u32[]{:S(2)}, u32[]{:S(2)}) collective-permute-start(bf16[80,512]{1,0:T(8,128)(2,1)S(1)} %pad_maximum_fusion.4), channel_id=1, source_target_pairs={{0,64},{8,72},{16,80},{24,88},{32,96},{40,104},{48,112},{56,120},{... | collective-permute-start | bytes 245768 | tf_op jit(solution)/shard_map/ppermute | solution.py:26
  83.1 7.2 %collective-permute-start.15 = (bf16[80,512]{1,0:T(8,128)(2,1)S(1)}, bf16[80,512]{1,0:T(8,128)(2,1)S(1)}, u32[]{:S(2)}, u32[]{:S(2)}) collective-permute-start(bf16[80,512]{1,0:T(8,128)(2,1)S(1)} %pad_maximum_fusion.4), channel_id=1, source_target_pairs={{0,32},{8,40},{16,48},{24,56},{32,0},{40,8},{48,16},{56,24},{64,96... | collective-permute-start | bytes 245768 | tf_op jit(solution)/shard_map/ppermute | solution.py:26
  92.4 9.2 %collective-permute-start.18 = (bf16[64,512]{1,0:T(8,128)(2,1)S(1)}, bf16[64,512]{1,0:T(8,128)(2,1)S(1)}, u32[]{:S(2)}, u32[]{:S(2)}) collective-permute-start(bf16[64,512]{1,0:T(8,128)(2,1)S(1)} %fusion.143), channel_id=1, source_target_pairs={{0,24},{8,16},{16,8},{24,0},{32,56},{40,48},{48,40},{56,32},{64,88... | collective-permute-start | bytes 196616 | tf_op jit(solution)/shard_map/ppermute | solution.py:22
  95.7 5.8 %collective-permute-start.17 = (bf16[64,512]{1,0:T(8,128)(2,1)S(1)}, bf16[64,512]{1,0:T(8,128)(2,1)S(1)}, u32[]{:S(2)}, u32[]{:S(2)}) collective-permute-start(bf16[64,512]{1,0:T(8,128)(2,1)S(1)} %fusion.138), channel_id=1, source_target_pairs={{0,16},{8,24},{16,0},{24,8},{32,48},{40,56},{48,32},{56,40},{64,80... | collective-permute-start | bytes 196616 | tf_op jit(solution)/shard_map/ppermute | solution.py:22
  109.2 10.1 %collective-permute-start.25 = (bf16[256,512]{1,0:T(8,128)(2,1)S(1)}, bf16[256,512]{1,0:T(8,128)(2,1)S(1)}, u32[]{:S(2)}, u32[]{:S(2)}) collective-permute-start(bf16[256,512]{1,0:T(8,128)(2,1)S(1)} %get-tuple-element.10), channel_id=1, source_target_pairs={{0,6},{1,7},{2,0},{3,1},{4,2},{5,3},{6,4},{7,5},{8,14},{9,15},{10,... | collective-permute-start | bytes 786440 | tf_op jit(solution)/shard_map/ppermute | solution.py:14
  112.9 10.4 %collective-permute-start.21 = (bf16[256,512]{1,0:T(8,128)(2,1)S(1)}, bf16[256,512]{1,0:T(8,128)(2,1)S(1)}, u32[]{:S(2)}, u32[]{:S(2)}) collective-permute-start(bf16[256,512]{1,0:T(8,128)(2,1)S(1)} %get-tuple-element.9), channel_id=1, source_target_pairs={{0,2},{1,3},{2,4},{3,5},{4,6},{5,7},{6,0},{7,1},{8,10},{9,11},{10,... | collective-permute-start | bytes 786440 | tf_op jit(solution)/shard_map/ppermute | solution.py:14
  114.4 14.4 %collective-permute-start.24 = (bf16[256,512]{1,0:T(8,128)(2,1)S(1)}, bf16[256,512]{1,0:T(8,128)(2,1)S(1)}, u32[]{:S(2)}, u32[]{:S(2)}) collective-permute-start(bf16[256,512]{1,0:T(8,128)(2,1)S(1)} %slice.215), channel_id=1, source_target_pairs={{0,2},{1,3},{2,4},{3,5},{4,6},{5,7},{6,0},{7,1},{8,10},{9,11},{10,... | collective-permute-start | bytes 786440 | tf_op jit(solution)/shard_map/ppermute | solution.py:14
  116.1 12.8 %collective-permute-start.23 = (bf16[256,512]{1,0:T(8,128)(2,1)S(1)}, bf16[256,512]{1,0:T(8,128)(2,1)S(1)}, u32[]{:S(2)}, u32[]{:S(2)}) collective-permute-start(bf16[256,512]{1,0:T(8,128)(2,1)S(1)} %slice.216), channel_id=1, source_target_pairs={{0,6},{1,7},{2,0},{3,1},{4,2},{5,3},{6,4},{7,5},{8,14},{9,15},{10,... | collective-permute-start | bytes 786440 | tf_op jit(solution)/shard_map/ppermute | solution.py:14
  119.4 10.9 %collective-permute-start.26 = (bf16[256,512]{1,0:T(8,128)(2,1)S(1)}, bf16[256,512]{1,0:T(8,128)(2,1)S(1)}, u32[]{:S(2)}, u32[]{:S(2)}) collective-permute-start(bf16[256,512]{1,0:T(8,128)(2,1)S(1)} %fusion.37), channel_id=1, source_target_pairs={{0,6},{1,7},{2,0},{3,1},{4,2},{5,3},{6,4},{7,5},{8,14},{9,15},{10,... | collective-permute-start | bytes 786440 | tf_op jit(solution)/shard_map/ppermute | solution.py:14
  123.3 10.1 %collective-permute-start.22 = (bf16[256,512]{1,0:T(8,128)(2,1)S(1)}, bf16[256,512]{1,0:T(8,128)(2,1)S(1)}, u32[]{:S(2)}, u32[]{:S(2)}) collective-permute-start(bf16[256,512]{1,0:T(8,128)(2,1)S(1)} %fusion.40), channel_id=1, source_target_pairs={{0,2},{1,3},{2,4},{3,5},{4,6},{5,7},{6,0},{7,1},{8,10},{9,11},{10,... | collective-permute-start | bytes 786440 | tf_op jit(solution)/shard_map/ppermute | solution.py:14
  (19 other events, 126.8 us)

commit v2 on v1

v2 whole, which is shorter than its diff:
```python
import functools

import jax
import jax.numpy as jnp
from jax import lax
from jax.experimental import pallas as pl
from jax.experimental.pallas import tpu as pltpu
from jax.sharding import PartitionSpec as P

DK = 256
DV = 512
ROWS = 512
HALF = 256
WIDE = 512
SIDE = 4
CUT = DK // SIDE
MSG = CUT + 16
BF, F32 = jnp.bfloat16, jnp.float32
VM = pl.BlockSpec(memory_space=pltpu.VMEM)
SM = pl.BlockSpec(memory_space=pltpu.SMEM)
ANY = pl.BlockSpec(memory_space=pl.ANY)
HBM = pl.BlockSpec(memory_space=pltpu.HBM)


def tp_shift(value, step):
    return lax.ppermute(value, "tp", [(i, (i + 2 * step) % 8) for i in range(8)])


def tp_swap(value):
    return lax.ppermute(value, "tp", [(i, i ^ 1) for i in range(8)])


def z_flip(value, k):
    return lax.ppermute(value, "ctx", [(i, i ^ k) for i in range(16)])


def x_flip(value, k):
    return lax.ppermute(value, "ctx", [(i, i ^ (4 * k)) for i in range(16)])


def dot(a, b):
    return jnp.dot(a, b, preferred_element_type=F32)


def call(body, outs, in_specs, args, name, scratch=(), flops=0, moved=0, limit=16, out_specs=None, after=()):
    shapes = [jax.ShapeDtypeStruct(shape, dtype) for shape, dtype in outs]

    def whole(*refs):
        body(*refs[: len(args)], *refs[len(args) + len(after):])

    return pl.pallas_call(
        whole,
        out_shape=shapes,
        in_specs=list(in_specs) + [ANY] * len(after),
        out_specs=out_specs or [VM] * len(shapes),
        scratch_shapes=list(scratch),
        name=name,
        cost_estimate=pl.CostEstimate(flops=flops, bytes_accessed=moved, transcendentals=0),
        compiler_params=pltpu.CompilerParams(vmem_limit_bytes=limit * 1024 * 1024),
    )(*args, *after)


def project_body(owners, halves, n_weights, started, place, *refs):
    shards = []
    for half in halves:
        shards.append(jnp.concatenate([refs[0][...], refs[1][...]], axis=0) if half else refs[0][...])
        refs = refs[2 if half else 1:]
    weights, refs = refs[:n_weights], refs[n_weights:]
    sums, outs = (refs[:n_weights], refs[n_weights:]) if started else ([None] * n_weights, refs)
    for weight, before, out in zip(weights, sums, outs):
        total = None if before is None else before[...]
        for shard, owner in zip(shards, owners):
            rows = pl.ds(pl.multiple_of(place[owner] * WIDE, WIDE), WIDE)
            new = dot(shard, weight[rows, :])
            total = new if total is None else total + new
        out[...] = total


def project(place, owners, shards, weights, before, name, after=()):
    halves = [isinstance(s, tuple) for s in shards]
    flat = [p for s in shards for p in (s if isinstance(s, tuple) else (s,))]
    n = len(weights)
    widths = [w.shape[1] for w in weights]
    return call(
        functools.partial(project_body, owners, halves, n, before is not None),
        [((ROWS, width), F32) for width in widths],
        [SM] + [VM] * (len(flat) + n + (n if before else 0)),
        [place, *flat, *weights, *(before or [])],
        name,
        flops=2 * ROWS * WIDE * len(owners) * sum(widths),
        moved=WIDE * len(owners) * sum(widths) * 2,
        after=after,
    )


def tie(values, after, name):
    n = len(values)

    def body(*refs):
        pass

    return pl.pallas_call(
        body,
        out_shape=[jax.ShapeDtypeStruct(v.shape, v.dtype) for v in values],
        in_specs=[ANY] * (n + len(after)),
        out_specs=[ANY] * n,
        input_output_aliases={i: i for i in range(n)},
        name=name,
        compiler_params=pltpu.CompilerParams(vmem_limit_bytes=4 * 1024 * 1024),
    )(*values, *after)


def state_body(place, own0, own1, key_sum, value_sum, wk, wv, remain, factor, keys, values, mine, m1, m2, m3, state):
    x = jnp.concatenate([own0[...], own1[...]], axis=0)
    rows = pl.ds(pl.multiple_of(place[7] * WIDE, WIDE), WIDE)
    k = ((key_sum[...] + dot(x, wk[rows, :])) * DK ** (-0.5)).astype(BF)
    v = (value_sum[...] + dot(x, wv[rows, :])).astype(BF)
    keys[...] = k
    values[...] = v
    weighted = (k.astype(F32) * remain[...]).astype(BF)
    state[...] = lax.dot_general(weighted, v, (((0,), (0,)), ((), ())), preferred_element_type=F32)
    z = place[8]
    total = factor[...]
    high = total.astype(BF)
    rest = (total - high.astype(F32)).astype(BF)
    for i, ref in enumerate((mine, m1, m2, m3)):
        piece = state[pl.ds(pl.multiple_of((z ^ i) * CUT, CUT), CUT), :]
        if i == 0:
            ref[...] = piece
        else:
            ref[...] = jnp.concatenate(
                [piece.astype(BF), jnp.broadcast_to(high, (8, DV)), jnp.broadcast_to(rest, (8, DV))], axis=0
            )


def open_message(ref):
    ends = ref[CUT:, :].astype(F32)
    return ref[:CUT, :].astype(F32), ends[0:1] + ends[8:9]


def between(factors, sources, low, high):
    product = jnp.ones_like(factors[0])
    for factor, source in zip(factors, sources):
        product = product * jnp.where((source > low) & (source < high), factor, 1.0)
    return product


def prefix(pieces, factors, sources, target):
    total = jnp.zeros_like(pieces[0])
    for piece, source in zip(pieces, sources):
        weight = between(factors, sources, source, target)
        total = total + jnp.where(source < target, weight, 0.0) * piece
    return total


def line_of(place, mine, factor, messages):
    opened = [open_message(m) for m in messages]
    z = place[8]
    pieces = [mine[...]] + [piece for piece, _ in opened]
    factors = [factor[...]] + [f for _, f in opened]
    return pieces, factors, [z ^ k for k in range(SIDE)]


def line_body(place, mine, factor, m1, m2, m3, out):
    pieces, factors, sources = line_of(place, mine, factor, (m1, m2, m3))
    total = between(factors, sources, -1, SIDE)
    high = total.astype(BF)
    rest = (total - high.astype(F32)).astype(BF)
    piece = prefix(pieces, factors, sources, SIDE)
    out[...] = jnp.concatenate(
        [piece.astype(BF), jnp.broadcast_to(high, (8, DV)), jnp.broadcast_to(rest, (8, DV))], axis=0
    )


def entry_body(place, mine, factor, m1, m2, m3, n1, n2, n3, e0, e1, e2, e3):
    pieces, factors, sources = line_of(place, mine, factor, (m1, m2, m3))
    x, z = place[9], place[8]
    opened = [open_message(n) for n in (n1, n2, n3)]
    entry = prefix([p for p, _ in opened], [f for _, f in opened], [x ^ k for k in range(1, SIDE)], x)
    for k, ref in enumerate((e0, e1, e2, e3)):
        target = z ^ k
        whole = prefix(pieces, factors, sources, target) + between(factors, sources, -1, target) * entry
        ref[...] = whole.astype(BF)


def decay_body(rates, remain, decay, factor, mask):
    rows = lax.broadcasted_iota(jnp.int32, (ROWS, ROWS), 0)
    cols = lax.broadcasted_iota(jnp.int32, (ROWS, ROWS), 1)
    rate_row = jnp.broadcast_to(rates[...], (ROWS, ROWS))
    rate_col = jnp.sum(jnp.where(rows == cols, rate_row, 0.0), axis=1, keepdims=True)
    cumul_col = jnp.sum(jnp.where(rows >= cols, rate_row, 0.0), axis=1, keepdims=True)
    cumul_row = jnp.sum(jnp.where(rows <= cols, rate_col, 0.0), axis=0, keepdims=True)
    total = cumul_col[ROWS - 1:]
    remain[...] = jnp.exp(total - cumul_col)
    decay[...] = jnp.exp(cumul_col)
    factor[...] = jnp.broadcast_to(jnp.exp(total), (1, DV))
    mask[...] = jnp.exp(jnp.where(rows >= cols, cumul_col - cumul_row, -1e30))


def local_body(query_sum, keys, values, mask, queries, local):
    q = query_sum[...].astype(BF)
    queries[...] = q
    scores = lax.dot_general(q, keys[...], (((1,), (1,)), ((), ())), preferred_element_type=F32)
    local[...] = dot((scores * mask[...]).astype(BF), values[...])


def hidden_body(half, place, queries, e0, e1, e2, e3, local, decay, gate_sum, hidden, whole):
    z = place[8]
    rows = pl.ds(half * HALF, HALF)
    for k, ref in enumerate((e0, e1, e2, e3)):
        whole[pl.ds(pl.multiple_of((z ^ k) * CUT, CUT), CUT), :] = ref[...]
    retained = local[rows, :] + decay[rows, :] * dot(queries[rows, :], whole[...])
    center = retained - jnp.mean(retained, axis=-1, keepdims=True)
    variance = jnp.mean(center * center, axis=-1, keepdims=True)
    gate = gate_sum[rows, :].astype(BF).astype(F32)
    hidden[...] = (gate / (1.0 + jnp.exp(-gate)) * (center * lax.rsqrt(variance + 1e-5))).astype(BF)


def halve_body(before, after, top, low):
    top[...] = before[:HALF]
    low[...] = after[HALF:]


STEPS = (2, 1, -1, 0)


def pick_body(place, weight, given_far, given, given_own, kept_far, kept, kept_own, sems):
    core, y = place[10], place[11]
    copies = []
    for i, step in enumerate(STEPS):
        block = (y + step) % SIDE
        for j, (outs, which) in enumerate((((given_far, given, given_own), 1 - core), ((kept_far, kept, kept_own), core))):
            columns = pl.ds(pl.multiple_of((2 * block + which) * DV, DV), DV)
            out = (outs[0], outs[1].at[:, pl.ds(0, DV)], outs[1].at[:, pl.ds(DV, DV)], outs[2])[i]
            copy = pltpu.make_async_copy(weight.at[:, columns], out, sems.at[i, j])
            copy.start()
            copies.append(copy)
    for copy in copies:
        copy.wait()


def partial_body(n, *refs):
    hidden = jnp.concatenate([r[...] for r in refs[:n]], axis=0)
    other = jnp.concatenate([r[...] for r in refs[n: 2 * n]], axis=0)
    mine, theirs, outs = refs[2 * n], refs[2 * n + 1], refs[2 * n + 2:]
    total = dot(hidden, mine[...]) + dot(other, theirs[...])
    for i, out in enumerate(outs):
        rows, columns = (i % n) * HALF, (i // n) * DV
        out[...] = total[rows: rows + HALF, columns: columns + DV].astype(out.dtype)


def partial(hidden, other, mine, theirs, kinds, name, after=()):
    width, n = mine.shape[1], len(hidden)
    return call(
        functools.partial(partial_body, n),
        [((HALF, DV), kind) for kind in kinds],
        [VM] * (2 * n + 2),
        [*hidden, *other, mine, theirs],
        name,
        flops=4 * n * HALF * DV * width,
        moved=4 * DV * width,
        after=after,
    )


def own_body(h0, h1, o0, o1, mine, theirs, top, low, out_top, out_low):
    for h, o, come, out in ((h0, o0, top, out_top), (h1, o1, low, out_low)):
        out[...] = dot(h[...], mine[...]) + dot(o[...], theirs[...]) + come[...].astype(F32)


def final_body(own_top, own_low, top, low, out):
    out[:HALF, :] = (own_top[...] + top[...].astype(F32)).astype(BF)
    out[HALF:, :] = (own_low[...] + low[...].astype(F32)).astype(BF)


def added(mine, come):
    return (mine + come.astype(F32)).astype(BF)


def shards(tokens, w_query, w_key, w_value, w_gate, w_out, log_decay):
    ctx, tp = lax.axis_index("ctx"), lax.axis_index("tp")
    w_out = pltpu.with_memory_space_constraint(w_out, pltpu.HBM)
    x, z, y, core = ctx // SIDE, ctx % SIDE, tp // 2, tp % 2
    owners = [2 * ((y + step) % SIDE) + c for step in (0, -1, 1, 2) for c in (core, 1 - core)]
    place = jnp.stack([jnp.asarray(v, jnp.int32) for v in (*owners, z, x, core, y)])

    own_s = tp_swap(tokens)
    before, after = tp_shift(tokens, 1), tp_shift(tokens, -1)
    remain, decay, factor, mask = call(
        decay_body,
        [((ROWS, 1), F32)] * 2 + [((1, DV), F32), ((ROWS, ROWS), F32)],
        [VM],
        [log_decay],
        "decay",
        flops=ROWS * ROWS * 64,
    )
    given_far, given, given_own, kept_far, kept, kept_own = call(
        pick_body, [((DV, DV), BF), ((DV, 2 * DV), BF), ((DV, DV), BF)] * 2, [SM, HBM], [place, w_out], "pick",
        scratch=[pltpu.SemaphoreType.DMA((SIDE, 2))], moved=8 * DV * DV * 4,
    )
    theirs_far, theirs, theirs_own = tp_swap(given_far), tp_swap(given), tp_swap(given_own)

    kv = (w_key, w_value)
    sums = project(place, (0, 1), (tokens, own_s), kv, None, "kv_own", after=[kept_far])
    before, after = tie((before, after), [sums[0], mask], "tie")
    halves = call(
        halve_body, [((HALF, WIDE), BF)] * 2, [VM] * 2, [before, after], "halve", moved=ROWS * WIDE * 2,
    )
    before_s, after_s = tp_swap(before), tp_swap(after)
    across = (tp_shift(halves[0], 1), tp_shift(halves[1], -1))
    across_s = tuple(tp_swap(p) for p in across)
    sums = project(place, (2, 4, 3, 5), (before, after, before_s, after_s), kv, sums, "kv_near")
    sums = project(place, (6,), (across,), kv, sums, "kv_far")
    keys, values, mine, m1, m2, m3 = call(
        state_body,
        [((ROWS, DK), BF), ((ROWS, DV), BF), ((CUT, DV), F32)] + [((MSG, DV), BF)] * 3,
        [SM] + [VM] * 8,
        [place, *across_s, *sums, w_key, w_value, remain, factor],
        "state",
        scratch=[pltpu.VMEM((DK, DV), F32)],
        flops=2 * ROWS * (WIDE * (DK + DV) + DK * DV),
        moved=WIDE * (DK + DV) * 2,
    )
    messages = [z_flip(m, k + 1) for k, m in enumerate((m1, m2, m3))]

    everything = (tokens, own_s, before, after, before_s, after_s, across, across_s)
    order = (0, 1, 2, 4, 3, 5, 6, 7)
    (query_sum,) = project(place, order, everything, (w_query,), None, "queries", after=[keys])
    (line,) = call(
        line_body, [((MSG, DV), BF)], [SM] + [VM] * 5, [place, mine, factor, *messages], "line", moved=MSG * DV * 8,
        after=[query_sum],
    )
    lines = [x_flip(line, k) for k in range(1, SIDE)]
    (gate_sum,) = project(place, order, everything, (w_gate,), None, "gates", after=[line])
    e0, e1, e2, e3 = call(
        entry_body, [((CUT, DV), BF)] * 4, [SM] + [VM] * 8, [place, mine, factor, *messages, *lines], "entry",
        moved=MSG * DV * 16, after=[gate_sum],
    )
    queries, local = call(
        local_body,
        [((ROWS, DK), BF), ((ROWS, DV), F32)],
        [VM] * 4,
        [query_sum, keys, values, mask],
        "local",
        flops=2 * ROWS * ROWS * (DK + DV),
        moved=ROWS * DV * 4,
        after=[e0],
    )
    e1, e2, e3 = (z_flip(e, k + 1) for k, e in enumerate((e1, e2, e3)))
    hidden, other, far = [], [], []
    for half in range(2):
        (part,) = call(
            functools.partial(hidden_body, half), [((HALF, DV), BF)], [SM] + [VM] * 8,
            [place, queries, e0, e1, e2, e3, local, decay, gate_sum], f"hidden{half}",
            scratch=[pltpu.VMEM((DK, DV), BF)], flops=ROWS * DK * DV, moved=ROWS * DV * 4, after=hidden,
        )
        hidden.append(part)
        other.append(tp_swap(part))
    for half in range(2):
        far += partial(hidden[half: half + 1], other[half: half + 1], kept_far, theirs_far, (BF,), f"far{half}", after=far)
    via_right, via_left = tp_shift(far[0], 1), tp_shift(far[1], -1)
    r_top, r_low, l_top, l_low = partial(hidden, other, kept, theirs, (F32, BF, BF, F32), "beside", after=far)
    low_right, top_left = tp_shift(r_low, 1), tp_shift(l_top, -1)
    top_right, low_left = tp_shift(added(r_top, via_right), 1), tp_shift(added(l_low, via_left), -1)
    own = call(
        own_body, [((HALF, DV), F32)] * 2, [VM] * 8, [*hidden, *other, kept_own, theirs_own, top_left, low_right], "own",
        flops=4 * ROWS * DV * DV, moved=8 * DV * DV,
    )
    (out,) = call(
        final_body, [((ROWS, DV), BF)], [VM] * 4, [*own, top_right, low_left], "final", moved=ROWS * DV * 2,
    )
    return out


def solution(mesh):
    in_specs = (P("ctx", "tp"),) + (P(None, "tp"),) * 4 + (P("tp", None), P("tp", "ctx"))
    return jax.shard_map(
        shards, mesh=mesh, in_specs=in_specs, out_specs=P("ctx", "tp"), check_vma=False
    )
```

time: 136 us -> 92.8 us (0.68)
  matrix products: 39.8 us -> 0 us
  Pallas kernels: 0 us -> 22.6 us
  local copies, waits for them, and re-layouts: 24.5 us -> 2.78 us
  waiting for transfers between devices: 20.1 us -> 32.7 us
  between operations: 12.7 us -> 0.27 us
  other arithmetic: 3.12 us -> 0.14 us
    dot_general x43 -> x0, matrix products: 39.8 us -> none  [the longest x42 39.4 us: dot(): return jnp.dot(a, b, preferred_element_type=F32)]
    pallas_call x0 -> x20, Pallas kernels: none -> 22.6 us  [the longest x19 22.6 us: call(): pl.pallas_call(whole, out_shape=shapes, in_specs=list(in_specs) + [ANY] *...]
    ppermute x12 -> x10, waiting for transfers between devices: 12.8 us -> 23 us  [tp_shift(): lax.ppermute(value, 'tp', [(i, (i + 2 * step) % 8) for i in range(8)])]
    dynamic_slice x2 -> x0, local copies, waits for them, and re-layouts: 7.31 us -> none  [shards(): lax.dynamic_index_in_dim(w_out_blocks, 1 - core, 2, keepdims=False)]
    unnamed x36 -> x16, local copies, waits for them, and re-layouts: 9.85 us -> 2.69 us
    slice x12 -> x0, local copies, waits for them, and re-layouts: 6.12 us -> none  [the longest x6 3.4 us: unpacked(): factor = message[64, 0].astype(F32) + message[72, 0].astype(F32)]
    ppermute x12 -> x10, starting transfers between devices: 19.8 us -> 16.7 us  [tp_shift(): lax.ppermute(value, 'tp', [(i, (i + 2 * step) % 8) for i in range(8)])]
    ppermute x6, waiting for transfers between devices: 4.44 us -> 6.73 us  [z_flip(): return lax.ppermute(value, 'ctx', [(i, i ^ k) for i in range(16)])]
  transfers between devices with their start and end apart: 27 -> 29, of which waited for: 10 -> 12; matrix products, arithmetic and copies ran while one was open for 47% -> 0% of each run, Pallas kernels for 0% -> 24%
where the time goes in v2:
time: 92.8 us; the launch traced here: 92 us
  starting transfers between devices  33.5 us (36%)
  waiting for transfers between devices  32.7 us (35%)
  Pallas kernels  22.6 us (24%)
  local copies, waits for them, and re-layouts  2.78 us (3%)
    ppermute x10, waiting for transfers between devices, tp_shift(): lax.ppermute(value, 'tp', [(i, (i + 2 * step) % 8) for i in range(8)])  23 us
    pallas_call x19, Pallas kernels, call(): pl.pallas_call(whole, out_shape=shapes, in_specs=list(in_specs) + [ANY] *...  22.6 us
    ppermute x10, starting transfers between devices, tp_shift(): lax.ppermute(value, 'tp', [(i, (i + 2 * step) % 8) for i in range(8)])  16.7 us
    ppermute x6, starting transfers between devices, z_flip(): return lax.ppermute(value, 'ctx', [(i, i ^ k) for i in range(16)])  9.76 us
    ppermute x6, waiting for transfers between devices, z_flip(): return lax.ppermute(value, 'ctx', [(i, i ^ k) for i in range(16)])  6.73 us
    ppermute x3, starting transfers between devices, x_flip(): return lax.ppermute(value, 'ctx', [(i, i ^ 4 * k) for i in range(16)])  4.78 us
    unnamed x16, local copies, waits for them, and re-layouts  2.69 us
    ppermute x3, waiting for transfers between devices, x_flip(): return lax.ppermute(value, 'ctx', [(i, i ^ 4 * k) for i in range(16)])  2.29 us
  transfers between devices with their start and end apart: 29, of which 12 were waited for; matrix products, arithmetic and copies ran while one was open for 0% of the time, Pallas kernels for 24%

profile of v2, /device:TPU:0, one launch (start us, length us, event | category | flops | bytes accessed | tf_op | source)
XLA Modules:
  0.0 92.0 jit_solution(671234743373814276)
XLA Ops:
  0.0 1.7 %collective-permute-start.1 = (bf16[512,512]{1,0:T(8,128)(2,1)}, bf16[512,512]{1,0:T(8,128)(2,1)S(1)}, u32[]{:S(2)}, u32[]{:S(2)}) collective-permute-start(bf16[512,512]{1,0:T(8,128)(2,1)} %refs_1_.7), channel_id=1, source_target_pairs={{0,2},{1,3},{2,4},{3,5},{4,6},{5,7},{6,0},{7,1},{8,10},{9,11},{10,... | collective-permute-start | bytes 1572872 | tf_op jit(solution)/shard_map/ppermute | solution.py:26
  3.4 3.1 %pick.1 = (bf16[512,512]{1,0:T(8,128)(2,1)S(1)}, bf16[512,1024]{1,0:T(8,128)(2,1)S(1)}, bf16[512,512]{1,0:T(8,128)(2,1)S(1)}, bf16[512,512]{1,0:T(8,128)(2,1)S(1...) custom-call(s32[12]{0:T(128)S(1)} %stack.51.refs_0_, bf16[512,4096]{1,0:T(8,128)(2,1)} %refs_1_.4), custom_call_target="tpu_custom_call" | custom-call | bytes 8388608 | tf_op jit(solution)/shard_map/pick/pallas_call | solution.py:51
  6.8 1.6 %copy-done.1 = bf16[4096,256]{1,0:T(8,128)(2,1)S(1)} copy-done((bf16[4096,256]{1,0:T(8,128)(2,1)S(1)}, bf16[4096,256]{1,0:T(8,128)(2,1)}, u32[]{:S(2)}) %copy-start.1) | copy-done | bytes 2097176
  11.0 4.9 %collective-permute-done.1.refs_0_ = bf16[512,512]{1,0:T(8,128)(2,1)S(1)} collective-permute-done((bf16[512,512]{1,0:T(8,128)(2,1)}, bf16[512,512]{1,0:T(8,128)(2,1)S(1)}, u32[]{:S(2)}, u32[]{:S(2)}) %collective-permute-start.1) | collective-permute-done | bytes 524320 | tf_op jit(solution)/shard_map/ppermute | solution.py:26
  16.5 1.6 %collective-permute-start.5 = (bf16[256,512]{1,0:T(8,128)(2,1)S(1)}, bf16[256,512]{1,0:T(8,128)(2,1)S(1)}, u32[]{:S(2)}, u32[]{:S(2)}) collective-permute-start(bf16[256,512]{1,0:T(8,128)(2,1)S(1)} %get-tuple-element.48), channel_id=1, source_target_pairs={{0,2},{1,3},{2,4},{3,5},{4,6},{5,7},{6,0},{7,1},{8,10},{9,11},{10,... | collective-permute-start | bytes 786440 | tf_op jit(solution)/shard_map/ppermute | solution.py:26
  18.1 1.7 %collective-permute-start.6 = (bf16[256,512]{1,0:T(8,128)(2,1)S(1)}, bf16[256,512]{1,0:T(8,128)(2,1)S(1)}, u32[]{:S(2)}, u32[]{:S(2)}) collective-permute-start(bf16[256,512]{1,0:T(8,128)(2,1)S(1)} %get-tuple-element.49), channel_id=1, source_target_pairs={{0,6},{1,7},{2,0},{3,1},{4,2},{5,3},{6,4},{7,5},{8,14},{9,15},{10,... | collective-permute-start | bytes 786440 | tf_op jit(solution)/shard_map/ppermute | solution.py:26
  19.8 6.2 %collective-permute-done.5.refs_1_.refs_7_ = bf16[256,512]{1,0:T(8,128)(2,1)S(1)} collective-permute-done((bf16[256,512]{1,0:T(8,128)(2,1)S(1)}, bf16[256,512]{1,0:T(8,128)(2,1)S(1)}, u32[]{:S(2)}, u32[]{:S(2)}) %collective-permute-start.5) | collective-permute-done | bytes 262176 | tf_op jit(solution)/shard_map/ppermute | solution.py:26
  27.1 2.4 %kv_near.1 = (f32[512,256]{1,0:T(8,128)S(1)}, f32[512,512]{1,0:T(8,128)S(1)}) custom-call(s32[12]{0:T(128)S(1)} %stack.51.refs_0_, bf16[512,512]{1,0:T(8,128)(2,1)S(1)} %get-tuple-element.46.refs_0_.refs_1_.refs_3_, bf16[512,512]{1,0:T(8,128)(2,1)S(1)} %get-tuple-element.47.refs_1_.refs_2_.refs_4_, ...), custom_call_target="tpu_custom_call" | custom-call | flops 1610612736 | bytes 3145728 | tf_op jit(solution)/shard_map/kv_near/pallas_call | solution.py:51
  32.1 4.0 %collective-permute-start.10 = (bf16[80,512]{1,0:T(8,128)(2,1)S(1)}, bf16[80,512]{1,0:T(8,128)(2,1)S(1)}, u32[]{:S(2)}, u32[]{:S(2)}) collective-permute-start(bf16[80,512]{1,0:T(8,128)(2,1)S(1)} %get-tuple-element.61), channel_id=1, source_target_pairs={{0,16},{8,24},{16,0},{24,8},{32,48},{40,56},{48,32},{56,40},{64,80... | collective-permute-start | bytes 245768 | tf_op jit(solution)/shard_map/ppermute | solution.py:34
  37.1 1.8 %queries.1.refs_6_.refs_0_ = f32[512,256]{1,0:T(8,128)S(1)} custom-call(s32[12]{0:T(128)S(1)} %stack.51.refs_0_, bf16[512,512]{1,0:T(8,128)(2,1)S(1)} %copy-done.4, bf16[512,512]{1,0:T(8,128)(2,1)S(1)} %collective-permute-done.refs_2_, bf16[512,512]{1,0:T(8,128)(2,1)S(1)} %get-tuple-element.46.refs_0_.refs_1_.refs_3_, ...), custom_call_target="tpu_custom_call" | custom-call | flops 1073741824 | bytes 2097152 | tf_op jit(solution)/shard_map/queries/pallas_call | solution.py:51
  38.9 2.8 %collective-permute-done.11.refs_5_ = bf16[80,512]{1,0:T(8,128)(2,1)S(1)} collective-permute-done((bf16[80,512]{1,0:T(8,128)(2,1)S(1)}, bf16[80,512]{1,0:T(8,128)(2,1)S(1)}, u32[]{:S(2)}, u32[]{:S(2)}) %collective-permute-start.11) | collective-permute-done | bytes 81952 | tf_op jit(solution)/shard_map/ppermute | solution.py:34
  42.4 1.6 %collective-permute-start.12 = (bf16[80,512]{1,0:T(8,128)(2,1)S(1)}, bf16[80,512]{1,0:T(8,128)(2,1)S(1)}, u32[]{:S(2)}, u32[]{:S(2)}) collective-permute-start(bf16[80,512]{1,0:T(8,128)(2,1)S(1)} %line.1.refs_12_), channel_id=1, source_target_pairs={{0,32},{8,40},{16,48},{24,56},{32,0},{40,8},{48,16},{56,24},{64,96... | collective-permute-start | bytes 245768 | tf_op jit(solution)/shard_map/ppermute | solution.py:38
  44.0 2.7 %collective-permute-start.13 = (bf16[80,512]{1,0:T(8,128)(2,1)S(1)}, bf16[80,512]{1,0:T(8,128)(2,1)S(1)}, u32[]{:S(2)}, u32[]{:S(2)}) collective-permute-start(bf16[80,512]{1,0:T(8,128)(2,1)S(1)} %line.1.refs_12_), channel_id=1, source_target_pairs={{0,64},{8,72},{16,80},{24,88},{32,96},{40,104},{48,112},{56,120},{... | collective-permute-start | bytes 245768 | tf_op jit(solution)/shard_map/ppermute | solution.py:38
  47.2 2.9 %gates.1.refs_9_.refs_8_ = f32[512,512]{1,0:T(8,128)S(1)} custom-call(s32[12]{0:T(128)S(1)} %stack.51.refs_0_, bf16[512,512]{1,0:T(8,128)(2,1)S(1)} %copy-done.4, bf16[512,512]{1,0:T(8,128)(2,1)S(1)} %collective-permute-done.refs_2_, bf16[512,512]{1,0:T(8,128)(2,1)S(1)} %get-tuple-element.46.refs_0_.refs_1_.refs_3_, ...), custom_call_target="tpu_custom_call" | custom-call | flops 2147483648 | bytes 4194304 | tf_op jit(solution)/shard_map/gates/pallas_call | solution.py:51
  50.1 2.3 %collective-permute-done.14.refs_8_ = bf16[80,512]{1,0:T(8,128)(2,1)S(1)} collective-permute-done((bf16[80,512]{1,0:T(8,128)(2,1)S(1)}, bf16[80,512]{1,0:T(8,128)(2,1)S(1)}, u32[]{:S(2)}, u32[]{:S(2)}) %collective-permute-start.14) | collective-permute-done | bytes 81952 | tf_op jit(solution)/shard_map/ppermute | solution.py:38
  53.7 3.3 %collective-permute-start.16 = (bf16[64,512]{1,0:T(8,128)(2,1)S(1)}, bf16[64,512]{1,0:T(8,128)(2,1)S(1)}, u32[]{:S(2)}, u32[]{:S(2)}) collective-permute-start(bf16[64,512]{1,0:T(8,128)(2,1)S(1)} %get-tuple-element.66), channel_id=1, source_target_pairs={{0,16},{8,24},{16,0},{24,8},{32,48},{40,56},{48,32},{56,40},{64,80... | collective-permute-start | bytes 196616 | tf_op jit(solution)/shard_map/ppermute | solution.py:34
  60.0 2.5 %collective-permute-done.17.refs_5_ = bf16[64,512]{1,0:T(8,128)(2,1)S(1)} collective-permute-done((bf16[64,512]{1,0:T(8,128)(2,1)S(1)}, bf16[64,512]{1,0:T(8,128)(2,1)S(1)}, u32[]{:S(2)}, u32[]{:S(2)}) %collective-permute-start.17) | collective-permute-done | bytes 65568 | tf_op jit(solution)/shard_map/ppermute | solution.py:34
  66.9 3.0 %collective-permute-start.27 = (bf16[256,512]{1,0:T(8,128)(2,1)S(1)}, bf16[256,512]{1,0:T(8,128)(2,1)S(1)}, u32[]{:S(2)}, u32[]{:S(2)}) collective-permute-start(bf16[256,512]{1,0:T(8,128)(2,1)S(1)} %far1.1.refs_7_), channel_id=1, source_target_pairs={{0,6},{1,7},{2,0},{3,1},{4,2},{5,3},{6,4},{7,5},{8,14},{9,15},{10,... | collective-permute-start | bytes 786440 | tf_op jit(solution)/shard_map/ppermute | solution.py:26
  71.3 3.3 %collective-permute-start.23 = (bf16[256,512]{1,0:T(8,128)(2,1)S(1)}, bf16[256,512]{1,0:T(8,128)(2,1)S(1)}, u32[]{:S(2)}, u32[]{:S(2)}) collective-permute-start(bf16[256,512]{1,0:T(8,128)(2,1)S(1)} %get-tuple-element.75), channel_id=1, source_target_pairs={{0,6},{1,7},{2,0},{3,1},{4,2},{5,3},{6,4},{7,5},{8,14},{9,15},{10,... | collective-permute-start | bytes 786440 | tf_op jit(solution)/shard_map/ppermute | solution.py:26
  74.6 2.0 %collective-permute-done.27 = bf16[256,512]{1,0:T(8,128)(2,1)S(1)} collective-permute-done((bf16[256,512]{1,0:T(8,128)(2,1)S(1)}, bf16[256,512]{1,0:T(8,128)(2,1)S(1)}, u32[]{:S(2)}, u32[]{:S(2)}) %collective-permute-start.27) | collective-permute-done | bytes 262176 | tf_op jit(solution)/shard_map/ppermute | solution.py:26
  76.7 3.8 %collective-permute-start.28 = (bf16[256,512]{1,0:T(8,128)(2,1)S(1)}, bf16[256,512]{1,0:T(8,128)(2,1)S(1)}, u32[]{:S(2)}, u32[]{:S(2)}) collective-permute-start(bf16[256,512]{1,0:T(8,128)(2,1)S(1)} %add_convert_fusion), channel_id=1, source_target_pairs={{0,6},{1,7},{2,0},{3,1},{4,2},{5,3},{6,4},{7,5},{8,14},{9,15},{10,... | collective-permute-start | bytes 786440 | tf_op jit(solution)/shard_map/ppermute | solution.py:26
  80.6 1.6 %collective-permute-done.23.refs_6_ = bf16[256,512]{1,0:T(8,128)(2,1)S(1)} collective-permute-done((bf16[256,512]{1,0:T(8,128)(2,1)S(1)}, bf16[256,512]{1,0:T(8,128)(2,1)S(1)}, u32[]{:S(2)}, u32[]{:S(2)}) %collective-permute-start.23) | collective-permute-done | bytes 262176 | tf_op jit(solution)/shard_map/ppermute | solution.py:26
  82.2 3.8 %collective-permute-done.24.refs_7_ = bf16[256,512]{1,0:T(8,128)(2,1)S(1)} collective-permute-done((bf16[256,512]{1,0:T(8,128)(2,1)S(1)}, bf16[256,512]{1,0:T(8,128)(2,1)S(1)}, u32[]{:S(2)}, u32[]{:S(2)}) %collective-permute-start.24) | collective-permute-done | bytes 262176 | tf_op jit(solution)/shard_map/ppermute | solution.py:26
  87.3 3.9 %collective-permute-done.26.refs_2_ = bf16[256,512]{1,0:T(8,128)(2,1)S(1)} collective-permute-done((bf16[256,512]{1,0:T(8,128)(2,1)S(1)}, bf16[256,512]{1,0:T(8,128)(2,1)S(1)}, u32[]{:S(2)}, u32[]{:S(2)}) %collective-permute-start.26) | collective-permute-done | bytes 262176 | tf_op jit(solution)/shard_map/ppermute | solution.py:26
  (73 shorter events, 23.5 us)
Async XLA Ops:
  0.0 6.8 %collective-permute-start = (bf16[512,512]{1,0:T(8,128)(2,1)}, bf16[512,512]{1,0:T(8,128)(2,1)S(1)}, u32[]{:S(2)}, u32[]{:S(2)}) collective-permute-start(bf16[512,512]{1,0:T(8,128)(2,1)} %refs_1_.7), channel_id=1, source_target_pairs={{0,1},{1,0},{2,3},{3,2},{4,5},{5,4},{6,7},{7,6},{8,9},{9,8},{10,11... | collective-permute-start | bytes 1572872 | tf_op jit(solution)/shard_map/ppermute | solution.py:30
  0.0 15.9 %collective-permute-start.1 = (bf16[512,512]{1,0:T(8,128)(2,1)}, bf16[512,512]{1,0:T(8,128)(2,1)S(1)}, u32[]{:S(2)}, u32[]{:S(2)}) collective-permute-start(bf16[512,512]{1,0:T(8,128)(2,1)} %refs_1_.7), channel_id=1, source_target_pairs={{0,2},{1,3},{2,4},{3,5},{4,6},{5,7},{6,0},{7,1},{8,10},{9,11},{10,... | collective-permute-start | bytes 1572872 | tf_op jit(solution)/shard_map/ppermute | solution.py:26
  1.7 14.2 %collective-permute-start.2 = (bf16[512,512]{1,0:T(8,128)(2,1)}, bf16[512,512]{1,0:T(8,128)(2,1)S(1)}, u32[]{:S(2)}, u32[]{:S(2)}) collective-permute-start(bf16[512,512]{1,0:T(8,128)(2,1)} %refs_1_.7), channel_id=1, source_target_pairs={{0,6},{1,7},{2,0},{3,1},{4,2},{5,3},{6,4},{7,5},{8,14},{9,15},{10,... | collective-permute-start | bytes 1572872 | tf_op jit(solution)/shard_map/ppermute | solution.py:26
  15.9 10.6 %collective-permute-start.3 = (bf16[512,512]{1,0:T(8,128)(2,1)S(1)}, bf16[512,512]{1,0:T(8,128)(2,1)S(1)}, u32[]{:S(2)}, u32[]{:S(2)}) collective-permute-start(bf16[512,512]{1,0:T(8,128)(2,1)S(1)} %get-tuple-element.46.refs_0_.refs_1_.refs_3_), channel_id=1, source_target_pairs={{0,1},{1,0},{2,3},{3,2},{4,5},{5,4},{6,7},{7,6},{8,9},{9,8},{10,11... | collective-permute-start | bytes 1572872 | tf_op jit(solution)/shard_map/ppermute | solution.py:30
  15.9 11.1 %collective-permute-start.4 = (bf16[512,512]{1,0:T(8,128)(2,1)S(1)}, bf16[512,512]{1,0:T(8,128)(2,1)S(1)}, u32[]{:S(2)}, u32[]{:S(2)}) collective-permute-start(bf16[512,512]{1,0:T(8,128)(2,1)S(1)} %get-tuple-element.47.refs_1_.refs_2_.refs_4_), channel_id=1, source_target_pairs={{0,1},{1,0},{2,3},{3,2},{4,5},{5,4},{6,7},{7,6},{8,9},{9,8},{10,11... | collective-permute-start | bytes 1572872 | tf_op jit(solution)/shard_map/ppermute | solution.py:30
  16.5 9.5 %collective-permute-start.5 = (bf16[256,512]{1,0:T(8,128)(2,1)S(1)}, bf16[256,512]{1,0:T(8,128)(2,1)S(1)}, u32[]{:S(2)}, u32[]{:S(2)}) collective-permute-start(bf16[256,512]{1,0:T(8,128)(2,1)S(1)} %get-tuple-element.48), channel_id=1, source_target_pairs={{0,2},{1,3},{2,4},{3,5},{4,6},{5,7},{6,0},{7,1},{8,10},{9,11},{10,... | collective-permute-start | bytes 786440 | tf_op jit(solution)/shard_map/ppermute | solution.py:26
  18.1 7.9 %collective-permute-start.6 = (bf16[256,512]{1,0:T(8,128)(2,1)S(1)}, bf16[256,512]{1,0:T(8,128)(2,1)S(1)}, u32[]{:S(2)}, u32[]{:S(2)}) collective-permute-start(bf16[256,512]{1,0:T(8,128)(2,1)S(1)} %get-tuple-element.49), channel_id=1, source_target_pairs={{0,6},{1,7},{2,0},{3,1},{4,2},{5,3},{6,4},{7,5},{8,14},{9,15},{10,... | collective-permute-start | bytes 786440 | tf_op jit(solution)/shard_map/ppermute | solution.py:26
  26.5 38.8 %collective-permute-start.22 = (bf16[512,512]{1,0:T(8,128)(2,1)S(1)}, bf16[512,512]{1,0:T(8,128)(2,1)S(1)}, u32[]{:S(2)}, u32[]{:S(2)}) collective-permute-start(bf16[512,512]{1,0:T(8,128)(2,1)S(1)} %get-tuple-element.74), channel_id=1, source_target_pairs={{0,1},{1,0},{2,3},{3,2},{4,5},{5,4},{6,7},{7,6},{8,9},{9,8},{10,11... | collective-permute-start | bytes 1572872 | tf_op jit(solution)/shard_map/ppermute | solution.py:30
  26.6 43.4 %collective-permute-start.21 = (bf16[512,1024]{1,0:T(8,128)(2,1)S(1)}, bf16[512,1024]{1,0:T(8,128)(2,1)S(1)}, u32[]{:S(2)}, u32[]{:S(2)}) collective-permute-start(bf16[512,1024]{1,0:T(8,128)(2,1)S(1)} %get-tuple-element.73), channel_id=1, source_target_pairs={{0,1},{1,0},{2,3},{3,2},{4,5},{5,4},{6,7},{7,6},{8,9},{9,8},{10,11... | collective-permute-start | bytes 3145736 | tf_op jit(solution)/shard_map/ppermute | solution.py:30
  32.1 6.8 %collective-permute-start.10 = (bf16[80,512]{1,0:T(8,128)(2,1)S(1)}, bf16[80,512]{1,0:T(8,128)(2,1)S(1)}, u32[]{:S(2)}, u32[]{:S(2)}) collective-permute-start(bf16[80,512]{1,0:T(8,128)(2,1)S(1)} %get-tuple-element.61), channel_id=1, source_target_pairs={{0,16},{8,24},{16,0},{24,8},{32,48},{40,56},{48,32},{56,40},{64,80... | collective-permute-start | bytes 245768 | tf_op jit(solution)/shard_map/ppermute | solution.py:34
  36.1 5.7 %collective-permute-start.11 = (bf16[80,512]{1,0:T(8,128)(2,1)S(1)}, bf16[80,512]{1,0:T(8,128)(2,1)S(1)}, u32[]{:S(2)}, u32[]{:S(2)}) collective-permute-start(bf16[80,512]{1,0:T(8,128)(2,1)S(1)} %get-tuple-element.62), channel_id=1, source_target_pairs={{0,24},{8,16},{16,8},{24,0},{32,56},{40,48},{48,40},{56,32},{64,88... | collective-permute-start | bytes 245768 | tf_op jit(solution)/shard_map/ppermute | solution.py:34
  42.4 7.7 %collective-permute-start.12 = (bf16[80,512]{1,0:T(8,128)(2,1)S(1)}, bf16[80,512]{1,0:T(8,128)(2,1)S(1)}, u32[]{:S(2)}, u32[]{:S(2)}) collective-permute-start(bf16[80,512]{1,0:T(8,128)(2,1)S(1)} %line.1.refs_12_), channel_id=1, source_target_pairs={{0,32},{8,40},{16,48},{24,56},{32,0},{40,8},{48,16},{56,24},{64,96... | collective-permute-start | bytes 245768 | tf_op jit(solution)/shard_map/ppermute | solution.py:38
  44.0 6.1 %collective-permute-start.13 = (bf16[80,512]{1,0:T(8,128)(2,1)S(1)}, bf16[80,512]{1,0:T(8,128)(2,1)S(1)}, u32[]{:S(2)}, u32[]{:S(2)}) collective-permute-start(bf16[80,512]{1,0:T(8,128)(2,1)S(1)} %line.1.refs_12_), channel_id=1, source_target_pairs={{0,64},{8,72},{16,80},{24,88},{32,96},{40,104},{48,112},{56,120},{... | collective-permute-start | bytes 245768 | tf_op jit(solution)/shard_map/ppermute | solution.py:38
  46.7 5.7 %collective-permute-start.14 = (bf16[80,512]{1,0:T(8,128)(2,1)S(1)}, bf16[80,512]{1,0:T(8,128)(2,1)S(1)}, u32[]{:S(2)}, u32[]{:S(2)}) collective-permute-start(bf16[80,512]{1,0:T(8,128)(2,1)S(1)} %line.1.refs_12_), channel_id=1, source_target_pairs={{0,96},{8,104},{16,112},{24,120},{32,64},{40,72},{48,80},{56,88},{... | collective-permute-start | bytes 245768 | tf_op jit(solution)/shard_map/ppermute | solution.py:38
  53.2 5.4 %collective-permute-start.15 = (bf16[64,512]{1,0:T(8,128)(2,1)S(1)}, bf16[64,512]{1,0:T(8,128)(2,1)S(1)}, u32[]{:S(2)}, u32[]{:S(2)}) collective-permute-start(bf16[64,512]{1,0:T(8,128)(2,1)S(1)} %get-tuple-element.65), channel_id=1, source_target_pairs={{0,8},{8,0},{16,24},{24,16},{32,40},{40,32},{48,56},{56,48},{64,72... | collective-permute-start | bytes 196616 | tf_op jit(solution)/shard_map/ppermute | solution.py:34
  53.7 6.3 %collective-permute-start.16 = (bf16[64,512]{1,0:T(8,128)(2,1)S(1)}, bf16[64,512]{1,0:T(8,128)(2,1)S(1)}, u32[]{:S(2)}, u32[]{:S(2)}) collective-permute-start(bf16[64,512]{1,0:T(8,128)(2,1)S(1)} %get-tuple-element.66), channel_id=1, source_target_pairs={{0,16},{8,24},{16,0},{24,8},{32,48},{40,56},{48,32},{56,40},{64,80... | collective-permute-start | bytes 196616 | tf_op jit(solution)/shard_map/ppermute | solution.py:34
  57.0 5.5 %collective-permute-start.17 = (bf16[64,512]{1,0:T(8,128)(2,1)S(1)}, bf16[64,512]{1,0:T(8,128)(2,1)S(1)}, u32[]{:S(2)}, u32[]{:S(2)}) collective-permute-start(bf16[64,512]{1,0:T(8,128)(2,1)S(1)} %get-tuple-element.67), channel_id=1, source_target_pairs={{0,24},{8,16},{16,8},{24,0},{32,56},{40,48},{48,40},{56,32},{64,88... | collective-permute-start | bytes 196616 | tf_op jit(solution)/shard_map/ppermute | solution.py:34
  66.9 9.7 %collective-permute-start.27 = (bf16[256,512]{1,0:T(8,128)(2,1)S(1)}, bf16[256,512]{1,0:T(8,128)(2,1)S(1)}, u32[]{:S(2)}, u32[]{:S(2)}) collective-permute-start(bf16[256,512]{1,0:T(8,128)(2,1)S(1)} %far1.1.refs_7_), channel_id=1, source_target_pairs={{0,6},{1,7},{2,0},{3,1},{4,2},{5,3},{6,4},{7,5},{8,14},{9,15},{10,... | collective-permute-start | bytes 786440 | tf_op jit(solution)/shard_map/ppermute | solution.py:26
  69.9 10.6 %collective-permute-start.20 = (bf16[512,512]{1,0:T(8,128)(2,1)S(1)}, bf16[512,512]{1,0:T(8,128)(2,1)S(1)}, u32[]{:S(2)}, u32[]{:S(2)}) collective-permute-start(bf16[512,512]{1,0:T(8,128)(2,1)S(1)} %get-tuple-element.71), channel_id=1, source_target_pairs={{0,1},{1,0},{2,3},{3,2},{4,5},{5,4},{6,7},{7,6},{8,9},{9,8},{10,11... | collective-permute-start | bytes 1572872 | tf_op jit(solution)/shard_map/ppermute | solution.py:30
  70.0 10.4 %collective-permute-start.25 = (bf16[256,512]{1,0:T(8,128)(2,1)S(1)}, bf16[256,512]{1,0:T(8,128)(2,1)S(1)}, u32[]{:S(2)}, u32[]{:S(2)}) collective-permute-start(bf16[256,512]{1,0:T(8,128)(2,1)S(1)} %far0.1.refs_4_.refs_6_), channel_id=1, source_target_pairs={{0,2},{1,3},{2,4},{3,5},{4,6},{5,7},{6,0},{7,1},{8,10},{9,11},{10,... | collective-permute-start | bytes 786440 | tf_op jit(solution)/shard_map/ppermute | solution.py:26
  71.3 10.9 %collective-permute-start.23 = (bf16[256,512]{1,0:T(8,128)(2,1)S(1)}, bf16[256,512]{1,0:T(8,128)(2,1)S(1)}, u32[]{:S(2)}, u32[]{:S(2)}) collective-permute-start(bf16[256,512]{1,0:T(8,128)(2,1)S(1)} %get-tuple-element.75), channel_id=1, source_target_pairs={{0,6},{1,7},{2,0},{3,1},{4,2},{5,3},{6,4},{7,5},{8,14},{9,15},{10,... | collective-permute-start | bytes 786440 | tf_op jit(solution)/shard_map/ppermute | solution.py:26
  74.6 11.4 %collective-permute-start.24 = (bf16[256,512]{1,0:T(8,128)(2,1)S(1)}, bf16[256,512]{1,0:T(8,128)(2,1)S(1)}, u32[]{:S(2)}, u32[]{:S(2)}) collective-permute-start(bf16[256,512]{1,0:T(8,128)(2,1)S(1)} %get-tuple-element.76), channel_id=1, source_target_pairs={{0,2},{1,3},{2,4},{3,5},{4,6},{5,7},{6,0},{7,1},{8,10},{9,11},{10,... | collective-permute-start | bytes 786440 | tf_op jit(solution)/shard_map/ppermute | solution.py:26
  76.7 10.6 %collective-permute-start.28 = (bf16[256,512]{1,0:T(8,128)(2,1)S(1)}, bf16[256,512]{1,0:T(8,128)(2,1)S(1)}, u32[]{:S(2)}, u32[]{:S(2)}) collective-permute-start(bf16[256,512]{1,0:T(8,128)(2,1)S(1)} %add_convert_fusion), channel_id=1, source_target_pairs={{0,6},{1,7},{2,0},{3,1},{4,2},{5,3},{6,4},{7,5},{8,14},{9,15},{10,... | collective-permute-start | bytes 786440 | tf_op jit(solution)/shard_map/ppermute | solution.py:26
  80.5 10.6 %collective-permute-start.26 = (bf16[256,512]{1,0:T(8,128)(2,1)S(1)}, bf16[256,512]{1,0:T(8,128)(2,1)S(1)}, u32[]{:S(2)}, u32[]{:S(2)}) collective-permute-start(bf16[256,512]{1,0:T(8,128)(2,1)S(1)} %add_convert_fusion.1), channel_id=1, source_target_pairs={{0,2},{1,3},{2,4},{3,5},{4,6},{5,7},{6,0},{7,1},{8,10},{9,11},{10,... | collective-permute-start | bytes 786440 | tf_op jit(solution)/shard_map/ppermute | solution.py:26
  (13 other events, 75.7 us)

commit v3 on v2

--- a/solution.py
+++ b/solution.py
@@ -17,13 +17,12 @@
 MSG = CUT + 16
 BF, F32 = jnp.bfloat16, jnp.float32
 VM = pl.BlockSpec(memory_space=pltpu.VMEM)
-SM = pl.BlockSpec(memory_space=pltpu.SMEM)
 ANY = pl.BlockSpec(memory_space=pl.ANY)
 HBM = pl.BlockSpec(memory_space=pltpu.HBM)
 
 
-def tp_shift(value, step):
-    return lax.ppermute(value, "tp", [(i, (i + 2 * step) % 8) for i in range(8)])
+def y_flip(value, k):
+    return lax.ppermute(value, "tp", [(i, i ^ (2 * k)) for i in range(8)])
 
 
 def tp_swap(value):
@@ -36,6 +35,16 @@
 
 def x_flip(value, k):
     return lax.ppermute(value, "ctx", [(i, i ^ (4 * k)) for i in range(16)])
+
+
+def my(name):
+    ctx, tp = lax.axis_index("ctx"), lax.axis_index("tp")
+    return {"x": ctx // SIDE, "z": ctx % SIDE, "y": tp // 2, "core": tp % 2}[name]
+
+
+def rows_of(step, same):
+    core = my("core") if same else 1 - my("core")
+    return pl.ds(pl.multiple_of((2 * (my("y") ^ step) + core) * WIDE, WIDE), WIDE)
 
 
 def dot(a, b):
@@ -60,35 +69,48 @@
     )(*args, *after)
 
 
-def project_body(owners, halves, n_weights, started, place, *refs):
+def join_body(top1, low1, top3, low3, near1, near3):
+    for top, low, near in ((top1, low1, near1), (top3, low3, near3)):
+        near[:HALF, :] = top[...]
+        near[HALF:, :] = low[...]
+
+
+def project_body(owners, halves, n_weights, started, gated, *refs):
     shards = []
     for half in halves:
-        shards.append(jnp.concatenate([refs[0][...], refs[1][...]], axis=0) if half else refs[0][...])
+        if half:
+            shards.append(jnp.concatenate([refs[0][...], refs[1][...]], axis=0))
+        else:
+            shards.append(refs[0][...])
         refs = refs[2 if half else 1:]
     weights, refs = refs[:n_weights], refs[n_weights:]
     sums, outs = (refs[:n_weights], refs[n_weights:]) if started else ([None] * n_weights, refs)
     for weight, before, out in zip(weights, sums, outs):
         total = None if before is None else before[...]
         for shard, owner in zip(shards, owners):
-            rows = pl.ds(pl.multiple_of(place[owner] * WIDE, WIDE), WIDE)
-            new = dot(shard, weight[rows, :])
+            new = dot(shard, weight[rows_of(*owner), :])
             total = new if total is None else total + new
-        out[...] = total
-
-
-def project(place, owners, shards, weights, before, name, after=()):
+        out[...] = gate_of(total) if gated else total
+
+
+def gate_of(total):
+    gate = total.astype(BF).astype(F32)
+    return gate / (1.0 + jnp.exp(-gate))
+
+
+def project(owners, shards, weights, before, name, after=(), gated=False, hint=1):
     halves = [isinstance(s, tuple) for s in shards]
     flat = [p for s in shards for p in (s if isinstance(s, tuple) else (s,))]
     n = len(weights)
     widths = [w.shape[1] for w in weights]
     return call(
-        functools.partial(project_body, owners, halves, n, before is not None),
+        functools.partial(project_body, owners, halves, n, before is not None, gated),
         [((ROWS, width), F32) for width in widths],
-        [SM] + [VM] * (len(flat) + n + (n if before else 0)),
-        [place, *flat, *weights, *(before or [])],
+        [VM] * (len(flat) + n + (n if before else 0)),
+        [*flat, *weights, *(before or [])],
         name,
-        flops=2 * ROWS * WIDE * len(owners) * sum(widths),
-        moved=WIDE * len(owners) * sum(widths) * 2,
+        flops=2 * ROWS * WIDE * len(owners) * sum(widths) * hint + 1,
+        moved=WIDE * len(owners) * sum(widths) * 2 * hint + 1,
         after=after,
     )
 
@@ -110,16 +132,16 @@
     )(*values, *after)
 
 
-def state_body(place, own0, own1, key_sum, value_sum, wk, wv, remain, factor, keys, values, mine, m1, m2, m3, state):
+def state_body(own0, own1, key_sum, value_sum, wk, wv, remain, factor, keys, values, mine, m1, m2, m3, state):
     x = jnp.concatenate([own0[...], own1[...]], axis=0)
-    rows = pl.ds(pl.multiple_of(place[7] * WIDE, WIDE), WIDE)
+    rows = rows_of(2, 0)
     k = ((key_sum[...] + dot(x, wk[rows, :])) * DK ** (-0.5)).astype(BF)
     v = (value_sum[...] + dot(x, wv[rows, :])).astype(BF)
     keys[...] = k
     values[...] = v
     weighted = (k.astype(F32) * remain[...]).astype(BF)
     state[...] = lax.dot_general(weighted, v, (((0,), (0,)), ((), ())), preferred_element_type=F32)
-    z = place[8]
+    z = my("z")
     total = factor[...]
     high = total.astype(BF)
     rest = (total - high.astype(F32)).astype(BF)
@@ -153,16 +175,16 @@
     return total
 
 
-def line_of(place, mine, factor, messages):
+def line_of(mine, factor, messages):
     opened = [open_message(m) for m in messages]
-    z = place[8]
+    z = my("z")
     pieces = [mine[...]] + [piece for piece, _ in opened]
     factors = [factor[...]] + [f for _, f in opened]
     return pieces, factors, [z ^ k for k in range(SIDE)]
 
 
-def line_body(place, mine, factor, m1, m2, m3, out):
-    pieces, factors, sources = line_of(place, mine, factor, (m1, m2, m3))
+def line_body(mine, factor, m1, m2, m3, out):
+    pieces, factors, sources = line_of(mine, factor, (m1, m2, m3))
     total = between(factors, sources, -1, SIDE)
     high = total.astype(BF)
     rest = (total - high.astype(F32)).astype(BF)
@@ -172,9 +194,9 @@
     )
 
 
-def entry_body(place, mine, factor, m1, m2, m3, n1, n2, n3, e0, e1, e2, e3):
-    pieces, factors, sources = line_of(place, mine, factor, (m1, m2, m3))
-    x, z = place[9], place[8]
+def entry_body(mine, factor, m1, m2, m3, n1, n2, n3, e0, e1, e2, e3):
+    pieces, factors, sources = line_of(mine, factor, (m1, m2, m3))
+    x, z = my("x"), my("z")
     opened = [open_message(n) for n in (n1, n2, n3)]
     entry = prefix([p for p, _ in opened], [f for _, f in opened], [x ^ k for k in range(1, SIDE)], x)
     for k, ref in enumerate((e0, e1, e2, e3)):
@@ -204,31 +226,35 @@
     local[...] = dot((scores * mask[...]).astype(BF), values[...])
 
 
-def hidden_body(half, place, queries, e0, e1, e2, e3, local, decay, gate_sum, hidden, whole):
-    z = place[8]
+def hidden_body(half, queries, e0, e1, e2, e3, local, decay, gates, hidden, whole):
+    z = my("z")
     rows = pl.ds(half * HALF, HALF)
     for k, ref in enumerate((e0, e1, e2, e3)):
         whole[pl.ds(pl.multiple_of((z ^ k) * CUT, CUT), CUT), :] = ref[...]
     retained = local[rows, :] + decay[rows, :] * dot(queries[rows, :], whole[...])
     center = retained - jnp.mean(retained, axis=-1, keepdims=True)
     variance = jnp.mean(center * center, axis=-1, keepdims=True)
-    gate = gate_sum[rows, :].astype(BF).astype(F32)
-    hidden[...] = (gate / (1.0 + jnp.exp(-gate)) * (center * lax.rsqrt(variance + 1e-5))).astype(BF)
-
-
-def halve_body(before, after, top, low):
-    top[...] = before[:HALF]
-    low[...] = after[HALF:]
-
-
-STEPS = (2, 1, -1, 0)
-
-
-def pick_body(place, weight, given_far, given, given_own, kept_far, kept, kept_own, sems):
-    core, y = place[10], place[11]
+    hidden[...] = (gates[rows, :] * (center * lax.rsqrt(variance + 1e-5))).astype(BF)
+
+
+def cut_body(tokens, top, low, sems):
+    copies = [
+        pltpu.make_async_copy(tokens.at[pl.ds(i * HALF, HALF), :], out, sems.at[i]) for i, out in enumerate((top, low))
+    ]
+    for copy in copies:
+        copy.start()
+    for copy in copies:
+        copy.wait()
+
+
+STEPS = (2, 1, 3, 0)
+
+
+def pick_body(weight, given_far, given, given_own, kept_far, kept, kept_own, sems):
+    core, y = my("core"), my("y")
     copies = []
     for i, step in enumerate(STEPS):
-        block = (y + step) % SIDE
+        block = y ^ step
         for j, (outs, which) in enumerate((((given_far, given, given_own), 1 - core), ((kept_far, kept, kept_own), core))):
             columns = pl.ds(pl.multiple_of((2 * block + which) * DV, DV), DV)
             out = (outs[0], outs[1].at[:, pl.ds(0, DV)], outs[1].at[:, pl.ds(DV, DV)], outs[2])[i]
@@ -278,44 +304,44 @@
 
 
 def shards(tokens, w_query, w_key, w_value, w_gate, w_out, log_decay):
-    ctx, tp = lax.axis_index("ctx"), lax.axis_index("tp")
     w_out = pltpu.with_memory_space_constraint(w_out, pltpu.HBM)
-    x, z, y, core = ctx // SIDE, ctx % SIDE, tp // 2, tp % 2
-    owners = [2 * ((y + step) % SIDE) + c for step in (0, -1, 1, 2) for c in (core, 1 - core)]
-    place = jnp.stack([jnp.asarray(v, jnp.int32) for v in (*owners, z, x, core, y)])
-
+
+    top, low = call(
+        cut_body, [((HALF, WIDE), BF)] * 2, [ANY], [tokens], "cut", scratch=[pltpu.SemaphoreType.DMA((2,))],
+        moved=ROWS * WIDE * 4,
+    )
+    a1, a3 = y_flip(top, 1), y_flip(low, 3)
+    b1, b3 = y_flip(low, 1), y_flip(top, 3)
     own_s = tp_swap(tokens)
-    before, after = tp_shift(tokens, 1), tp_shift(tokens, -1)
     remain, decay, factor, mask = call(
         decay_body,
         [((ROWS, 1), F32)] * 2 + [((1, DV), F32), ((ROWS, ROWS), F32)],
         [VM],
         [log_decay],
         "decay",
-        flops=ROWS * ROWS * 64,
     )
     given_far, given, given_own, kept_far, kept, kept_own = call(
-        pick_body, [((DV, DV), BF), ((DV, 2 * DV), BF), ((DV, DV), BF)] * 2, [SM, HBM], [place, w_out], "pick",
-        scratch=[pltpu.SemaphoreType.DMA((SIDE, 2))], moved=8 * DV * DV * 4,
-    )
+        pick_body, [((DV, DV), BF), ((DV, 2 * DV), BF), ((DV, DV), BF)] * 2, [HBM], [w_out], "pick",
+        scratch=[pltpu.SemaphoreType.DMA((SIDE, 2))], moved=1,
+    )
+    kv = (w_key, w_value)
+    sums = project(((0, 1), (0, 0)), (tokens, own_s), kv, None, "kv_own", hint=0)
+    a1, a3 = tie((a1, a3), [kept_far, mask, sums[0]], "tie_a")
+    c3, c1 = y_flip(a1, 3), y_flip(a3, 1)
     theirs_far, theirs, theirs_own = tp_swap(given_far), tp_swap(given), tp_swap(given_own)
 
-    kv = (w_key, w_value)
-    sums = project(place, (0, 1), (tokens, own_s), kv, None, "kv_own", after=[kept_far])
-    before, after = tie((before, after), [sums[0], mask], "tie")
-    halves = call(
-        halve_body, [((HALF, WIDE), BF)] * 2, [VM] * 2, [before, after], "halve", moved=ROWS * WIDE * 2,
-    )
-    before_s, after_s = tp_swap(before), tp_swap(after)
-    across = (tp_shift(halves[0], 1), tp_shift(halves[1], -1))
+    near1, near3 = call(join_body, [((ROWS, WIDE), BF)] * 2, [VM] * 4, [a1, b1, b3, a3], "join", moved=1)
+    near1_s, near3_s = tp_swap(near1), tp_swap(near3)
+    sums = project(((1, 1), (3, 1)), (near1, near3), kv, sums, "kv_near", hint=0)
+    across = tie((c3, c1), sums[:1], "tie_c")
     across_s = tuple(tp_swap(p) for p in across)
-    sums = project(place, (2, 4, 3, 5), (before, after, before_s, after_s), kv, sums, "kv_near")
-    sums = project(place, (6,), (across,), kv, sums, "kv_far")
+    sums = project(((2, 1),), (tuple(across),), kv, sums, "kv_far", hint=10)
+    sums = project(((1, 0), (3, 0)), (near1_s, near3_s), kv, sums, "kv_near_s", hint=0)
     keys, values, mine, m1, m2, m3 = call(
         state_body,
         [((ROWS, DK), BF), ((ROWS, DV), BF), ((CUT, DV), F32)] + [((MSG, DV), BF)] * 3,
-        [SM] + [VM] * 8,
-        [place, *across_s, *sums, w_key, w_value, remain, factor],
+        [VM] * 8,
+        [*across_s, *sums, w_key, w_value, remain, factor],
         "state",
         scratch=[pltpu.VMEM((DK, DV), F32)],
         flops=2 * ROWS * (WIDE * (DK + DV) + DK * DV),
@@ -323,18 +349,18 @@
     )
     messages = [z_flip(m, k + 1) for k, m in enumerate((m1, m2, m3))]
 
-    everything = (tokens, own_s, before, after, before_s, after_s, across, across_s)
-    order = (0, 1, 2, 4, 3, 5, 6, 7)
-    (query_sum,) = project(place, order, everything, (w_query,), None, "queries", after=[keys])
+    everything = (tokens, own_s, near1, near3, near1_s, near3_s, tuple(across), across_s)
+    order = ((0, 1), (0, 0), (1, 1), (3, 1), (1, 0), (3, 0), (2, 1), (2, 0))
+    (query_sum,) = project(order, everything, (w_query,), None, "queries", after=[keys])
     (line,) = call(
-        line_body, [((MSG, DV), BF)], [SM] + [VM] * 5, [place, mine, factor, *messages], "line", moved=MSG * DV * 8,
+        line_body, [((MSG, DV), BF)], [VM] * 5, [mine, factor, *messages], "line", moved=MSG * DV * 8,
         after=[query_sum],
     )
     lines = [x_flip(line, k) for k in range(1, SIDE)]
-    (gate_sum,) = project(place, order, everything, (w_gate,), None, "gates", after=[line])
+    (gates,) = project(order, everything, (w_gate,), None, "gates", after=[line], gated=True)
     e0, e1, e2, e3 = call(
-        entry_body, [((CUT, DV), BF)] * 4, [SM] + [VM] * 8, [place, mine, factor, *messages, *lines], "entry",
-        moved=MSG * DV * 16, after=[gate_sum],
+        entry_body, [((CUT, DV), BF)] * 4, [VM] * 8, [mine, factor, *messages, *lines], "entry",
+        moved=MSG * DV * 16, after=[gates],
     )
     queries, local = call(
         local_body,
@@ -350,24 +376,24 @@
     hidden, other, far = [], [], []
     for half in range(2):
         (part,) = call(
-            functools.partial(hidden_body, half), [((HALF, DV), BF)], [SM] + [VM] * 8,
-            [place, queries, e0, e1, e2, e3, local, decay, gate_sum], f"hidden{half}",
+            functools.partial(hidden_body, half), [((HALF, DV), BF)], [VM] * 8,
+            [queries, e0, e1, e2, e3, local, decay, gates], f"hidden{half}",
             scratch=[pltpu.VMEM((DK, DV), BF)], flops=ROWS * DK * DV, moved=ROWS * DV * 4, after=hidden,
         )
         hidden.append(part)
         other.append(tp_swap(part))
     for half in range(2):
         far += partial(hidden[half: half + 1], other[half: half + 1], kept_far, theirs_far, (BF,), f"far{half}", after=far)
-    via_right, via_left = tp_shift(far[0], 1), tp_shift(far[1], -1)
-    r_top, r_low, l_top, l_low = partial(hidden, other, kept, theirs, (F32, BF, BF, F32), "beside", after=far)
-    low_right, top_left = tp_shift(r_low, 1), tp_shift(l_top, -1)
-    top_right, low_left = tp_shift(added(r_top, via_right), 1), tp_shift(added(l_low, via_left), -1)
+    via3, via1 = y_flip(far[0], 3), y_flip(far[1], 1)
+    top1, low1, top3, low3 = partial(hidden, other, kept, theirs, (F32, BF, BF, F32), "beside", after=far)
+    from1_low, from3_top = y_flip(low1, 1), y_flip(top3, 3)
+    from1_top, from3_low = y_flip(added(top1, via3), 1), y_flip(added(low3, via1), 3)
     own = call(
-        own_body, [((HALF, DV), F32)] * 2, [VM] * 8, [*hidden, *other, kept_own, theirs_own, top_left, low_right], "own",
+        own_body, [((HALF, DV), F32)] * 2, [VM] * 8, [*hidden, *other, kept_own, theirs_own, from3_top, from1_low], "own",
         flops=4 * ROWS * DV * DV, moved=8 * DV * DV,
     )
     (out,) = call(
-        final_body, [((ROWS, DV), BF)], [VM] * 4, [*own, top_right, low_left], "final", moved=ROWS * DV * 2,
+        final_body, [((ROWS, DV), BF)], [VM] * 4, [*own, from1_top, from3_low], "final", moved=ROWS * DV * 2,
     )
     return out
 

time: 92.8 us -> 83.2 us (0.90)
  Pallas kernels: 22.6 us -> 16.5 us
  starting transfers between devices: 33.5 us -> 31.3 us
  waiting for transfers between devices: 32.7 us -> 31.7 us
    pallas_call x19 -> x21, Pallas kernels: 22.6 us -> 16.5 us  [call(): pl.pallas_call(whole, out_shape=shapes, in_specs=list(in_specs) + [ANY] *...]
    ppermute x10 -> x12, starting transfers between devices: 16.7 us -> 13.6 us  [y_flip(): return lax.ppermute(value, 'tp', [(i, i ^ 2 * k) for i in range(8)])]
    ppermute x10 -> x12, waiting for transfers between devices: 23 us -> 21 us  [y_flip(): return lax.ppermute(value, 'tp', [(i, i ^ 2 * k) for i in range(8)])]
  transfers between devices with their start and end apart: 29 -> 31, of which waited for: 12 -> 15; matrix products, arithmetic and copies ran while one was open for 0% -> 0% of each run, Pallas kernels for 24% -> 19%
where the time goes in v3:
time: 83.2 us; the launch traced here: 82.8 us
  waiting for transfers between devices  31.7 us (38%)
  starting transfers between devices  31.3 us (38%)
  Pallas kernels  16.5 us (20%)
  local copies, waits for them, and re-layouts  2.81 us (3%)
    ppermute x12, waiting for transfers between devices, y_flip(): return lax.ppermute(value, 'tp', [(i, i ^ 2 * k) for i in range(8)])  21 us
    pallas_call x21, Pallas kernels, call(): pl.pallas_call(whole, out_shape=shapes, in_specs=list(in_specs) + [ANY] *...  16.5 us
    ppermute x12, starting transfers between devices, y_flip(): return lax.ppermute(value, 'tp', [(i, i ^ 2 * k) for i in range(8)])  13.6 us
    ppermute x6, starting transfers between devices, z_flip(): return lax.ppermute(value, 'ctx', [(i, i ^ k) for i in range(16)])  10.5 us
    ppermute x6, waiting for transfers between devices, z_flip(): return lax.ppermute(value, 'ctx', [(i, i ^ k) for i in range(16)])  7.24 us
    ppermute x3, starting transfers between devices, x_flip(): return lax.ppermute(value, 'ctx', [(i, i ^ 4 * k) for i in range(16)])  4.78 us
    unnamed x16, local copies, waits for them, and re-layouts  2.81 us
    ppermute x3, waiting for transfers between devices, x_flip(): return lax.ppermute(value, 'ctx', [(i, i ^ 4 * k) for i in range(16)])  2.71 us
  transfers between devices with their start and end apart: 31, of which 15 were waited for; matrix products, arithmetic and copies ran while one was open for 0% of the time, Pallas kernels for 19%

profile of v3, /device:TPU:0, one launch (start us, length us, event | category | flops | bytes accessed | tf_op | source)
XLA Modules:
  0.0 82.8 jit_solution(373553547221344425)
XLA Ops:
  1.3 1.7 %collective-permute-start.1 = (bf16[256,512]{1,0:T(8,128)(2,1)S(1)}, bf16[256,512]{1,0:T(8,128)(2,1)S(1)}, u32[]{:S(2)}, u32[]{:S(2)}) collective-permute-start(bf16[256,512]{1,0:T(8,128)(2,1)S(1)} %get-tuple-element.49), channel_id=1, source_target_pairs={{0,2},{1,3},{2,0},{3,1},{4,6},{5,7},{6,4},{7,5},{8,10},{9,11},{10,... | collective-permute-start | bytes 786440 | tf_op jit(solution)/shard_map/ppermute | solution.py:25
  3.0 2.2 %collective-permute-start.2 = (bf16[256,512]{1,0:T(8,128)(2,1)S(1)}, bf16[256,512]{1,0:T(8,128)(2,1)S(1)}, u32[]{:S(2)}, u32[]{:S(2)}) collective-permute-start(bf16[256,512]{1,0:T(8,128)(2,1)S(1)} %get-tuple-element.50), channel_id=1, source_target_pairs={{0,6},{1,7},{2,4},{3,5},{4,2},{5,3},{6,0},{7,1},{8,14},{9,15},{10,... | collective-permute-start | bytes 786440 | tf_op jit(solution)/shard_map/ppermute | solution.py:25
  6.5 2.2 %pick.1 = (bf16[512,512]{1,0:T(8,128)(2,1)S(1)}, bf16[512,1024]{1,0:T(8,128)(2,1)S(1)}, bf16[512,512]{1,0:T(8,128)(2,1)S(1)}, bf16[512,512]{1,0:T(8,128)(2,1)S(1...) custom-call(bf16[512,4096]{1,0:T(8,128)(2,1)} %refs_0_.7), custom_call_target="tpu_custom_call" | custom-call | bytes 1 | tf_op jit(solution)/shard_map/pick/pallas_call | solution.py:60
  9.1 1.6 %copy-done.1 = bf16[4096,256]{1,0:T(8,128)(2,1)S(1)} copy-done((bf16[4096,256]{1,0:T(8,128)(2,1)S(1)}, bf16[4096,256]{1,0:T(8,128)(2,1)}, u32[]{:S(2)}) %copy-start.1) | copy-done | bytes 2097176
  11.7 1.6 %collective-permute-done.2.refs_1_ = bf16[256,512]{1,0:T(8,128)(2,1)S(1)} collective-permute-done((bf16[256,512]{1,0:T(8,128)(2,1)S(1)}, bf16[256,512]{1,0:T(8,128)(2,1)S(1)}, u32[]{:S(2)}, u32[]{:S(2)}) %collective-permute-start.2) | collective-permute-done | bytes 262176 | tf_op jit(solution)/shard_map/ppermute | solution.py:25
  13.3 2.2 %collective-permute-start.7 = (bf16[256,512]{1,0:T(8,128)(2,1)S(1)}, bf16[256,512]{1,0:T(8,128)(2,1)S(1)}, u32[]{:S(2)}, u32[]{:S(2)}) collective-permute-start(bf16[256,512]{1,0:T(8,128)(2,1)S(1)} %get-tuple-element.54.refs_0_), channel_id=1, source_target_pairs={{0,6},{1,7},{2,4},{3,5},{4,2},{5,3},{6,0},{7,1},{8,14},{9,15},{10,... | collective-permute-start | bytes 786440 | tf_op jit(solution)/shard_map/ppermute | solution.py:25
  15.8 3.2 %collective-permute-done.4.refs_2_ = bf16[256,512]{1,0:T(8,128)(2,1)S(1)} collective-permute-done((bf16[256,512]{1,0:T(8,128)(2,1)S(1)}, bf16[256,512]{1,0:T(8,128)(2,1)S(1)}, u32[]{:S(2)}, u32[]{:S(2)}) %collective-permute-start.4) | collective-permute-done | bytes 262176 | tf_op jit(solution)/shard_map/ppermute | solution.py:25
  20.7 3.4 %collective-permute-done.7.refs_0_ = bf16[256,512]{1,0:T(8,128)(2,1)S(1)} collective-permute-done((bf16[256,512]{1,0:T(8,128)(2,1)S(1)}, bf16[256,512]{1,0:T(8,128)(2,1)S(1)}, u32[]{:S(2)}, u32[]{:S(2)}) %collective-permute-start.7) | collective-permute-done | bytes 262176 | tf_op jit(solution)/shard_map/ppermute | solution.py:25
  27.4 2.0 %collective-permute-start.11 = (bf16[80,512]{1,0:T(8,128)(2,1)S(1)}, bf16[80,512]{1,0:T(8,128)(2,1)S(1)}, u32[]{:S(2)}, u32[]{:S(2)}) collective-permute-start(bf16[80,512]{1,0:T(8,128)(2,1)S(1)} %get-tuple-element.72), channel_id=1, source_target_pairs={{0,8},{8,0},{16,24},{24,16},{32,40},{40,32},{48,56},{56,48},{64,72... | collective-permute-start | bytes 245768 | tf_op jit(solution)/shard_map/ppermute | solution.py:33
  29.4 3.6 %collective-permute-start.12 = (bf16[80,512]{1,0:T(8,128)(2,1)S(1)}, bf16[80,512]{1,0:T(8,128)(2,1)S(1)}, u32[]{:S(2)}, u32[]{:S(2)}) collective-permute-start(bf16[80,512]{1,0:T(8,128)(2,1)S(1)} %get-tuple-element.73), channel_id=1, source_target_pairs={{0,16},{8,24},{16,0},{24,8},{32,48},{40,56},{48,32},{56,40},{64,80... | collective-permute-start | bytes 245768 | tf_op jit(solution)/shard_map/ppermute | solution.py:33
  34.2 3.3 %collective-permute-done.12.refs_3_ = bf16[80,512]{1,0:T(8,128)(2,1)S(1)} collective-permute-done((bf16[80,512]{1,0:T(8,128)(2,1)S(1)}, bf16[80,512]{1,0:T(8,128)(2,1)S(1)}, u32[]{:S(2)}, u32[]{:S(2)}) %collective-permute-start.12) | collective-permute-done | bytes 81952 | tf_op jit(solution)/shard_map/ppermute | solution.py:33
  37.6 1.7 %collective-permute-done.13.refs_4_ = bf16[80,512]{1,0:T(8,128)(2,1)S(1)} collective-permute-done((bf16[80,512]{1,0:T(8,128)(2,1)S(1)}, bf16[80,512]{1,0:T(8,128)(2,1)S(1)}, u32[]{:S(2)}, u32[]{:S(2)}) %collective-permute-start.13) | collective-permute-done | bytes 81952 | tf_op jit(solution)/shard_map/ppermute | solution.py:33
  39.3 1.6 %collective-permute-start.14 = (bf16[80,512]{1,0:T(8,128)(2,1)S(1)}, bf16[80,512]{1,0:T(8,128)(2,1)S(1)}, u32[]{:S(2)}, u32[]{:S(2)}) collective-permute-start(bf16[80,512]{1,0:T(8,128)(2,1)S(1)} %line.1.refs_11_), channel_id=1, source_target_pairs={{0,32},{8,40},{16,48},{24,56},{32,0},{40,8},{48,16},{56,24},{64,96... | collective-permute-start | bytes 245768 | tf_op jit(solution)/shard_map/ppermute | solution.py:37
  40.9 2.7 %collective-permute-start.15 = (bf16[80,512]{1,0:T(8,128)(2,1)S(1)}, bf16[80,512]{1,0:T(8,128)(2,1)S(1)}, u32[]{:S(2)}, u32[]{:S(2)}) collective-permute-start(bf16[80,512]{1,0:T(8,128)(2,1)S(1)} %line.1.refs_11_), channel_id=1, source_target_pairs={{0,64},{8,72},{16,80},{24,88},{32,96},{40,104},{48,112},{56,120},{... | collective-permute-start | bytes 245768 | tf_op jit(solution)/shard_map/ppermute | solution.py:37
  44.1 2.5 %gates.1.refs_8_.refs_7_ = f32[512,512]{1,0:T(8,128)S(1)} custom-call(bf16[512,512]{1,0:T(8,128)(2,1)S(1)} %copy-done.4, bf16[512,512]{1,0:T(8,128)(2,1)S(1)} %collective-permute-done.refs_1_, bf16[512,512]{1,0:T(8,128)(2,1)S(1)} %get-tuple-element.56.refs_0_.refs_2_, bf16[512,512]{1,0:T(8,128)(2,1)S(1)} %get-tuple-element.57.refs_1_.refs_3_, ...), custom_call_target="tpu_custom_call" | custom-call | flops 2147483648 | bytes 4194305 | tf_op jit(solution)/shard_map/gates/pallas_call | solution.py:60
  47.7 1.7 %collective-permute-done.16.refs_7_ = bf16[80,512]{1,0:T(8,128)(2,1)S(1)} collective-permute-done((bf16[80,512]{1,0:T(8,128)(2,1)S(1)}, bf16[80,512]{1,0:T(8,128)(2,1)S(1)}, u32[]{:S(2)}, u32[]{:S(2)}) %collective-permute-start.16) | collective-permute-done | bytes 81952 | tf_op jit(solution)/shard_map/ppermute | solution.py:37
  49.9 2.1 %collective-permute-start.18 = (bf16[64,512]{1,0:T(8,128)(2,1)S(1)}, bf16[64,512]{1,0:T(8,128)(2,1)S(1)}, u32[]{:S(2)}, u32[]{:S(2)}) collective-permute-start(bf16[64,512]{1,0:T(8,128)(2,1)S(1)} %get-tuple-element.78), channel_id=1, source_target_pairs={{0,16},{8,24},{16,0},{24,8},{32,48},{40,56},{48,32},{56,40},{64,80... | collective-permute-start | bytes 196616 | tf_op jit(solution)/shard_map/ppermute | solution.py:33
  52.0 2.6 %collective-permute-start.19 = (bf16[64,512]{1,0:T(8,128)(2,1)S(1)}, bf16[64,512]{1,0:T(8,128)(2,1)S(1)}, u32[]{:S(2)}, u32[]{:S(2)}) collective-permute-start(bf16[64,512]{1,0:T(8,128)(2,1)S(1)} %get-tuple-element.79), channel_id=1, source_target_pairs={{0,24},{8,16},{16,8},{24,0},{32,56},{40,48},{48,40},{56,32},{64,88... | collective-permute-start | bytes 196616 | tf_op jit(solution)/shard_map/ppermute | solution.py:33
  55.9 1.6 %collective-permute-done.19.refs_4_ = bf16[64,512]{1,0:T(8,128)(2,1)S(1)} collective-permute-done((bf16[64,512]{1,0:T(8,128)(2,1)S(1)}, bf16[64,512]{1,0:T(8,128)(2,1)S(1)}, u32[]{:S(2)}, u32[]{:S(2)}) %collective-permute-start.19) | collective-permute-done | bytes 65568 | tf_op jit(solution)/shard_map/ppermute | solution.py:33
  61.1 2.2 %collective-permute-start.27 = (bf16[256,512]{1,0:T(8,128)(2,1)S(1)}, bf16[256,512]{1,0:T(8,128)(2,1)S(1)}, u32[]{:S(2)}, u32[]{:S(2)}) collective-permute-start(bf16[256,512]{1,0:T(8,128)(2,1)S(1)} %far0.1.refs_4_.refs_6_), channel_id=1, source_target_pairs={{0,6},{1,7},{2,4},{3,5},{4,2},{5,3},{6,0},{7,1},{8,14},{9,15},{10,... | collective-permute-start | bytes 786440 | tf_op jit(solution)/shard_map/ppermute | solution.py:25
  66.1 3.7 %collective-permute-done.29 = bf16[256,512]{1,0:T(8,128)(2,1)S(1)} collective-permute-done((bf16[256,512]{1,0:T(8,128)(2,1)S(1)}, bf16[256,512]{1,0:T(8,128)(2,1)S(1)}, u32[]{:S(2)}, u32[]{:S(2)}) %collective-permute-start.29) | collective-permute-done | bytes 262176 | tf_op jit(solution)/shard_map/ppermute | solution.py:25
  69.9 2.2 %collective-permute-start.30 = (bf16[256,512]{1,0:T(8,128)(2,1)S(1)}, bf16[256,512]{1,0:T(8,128)(2,1)S(1)}, u32[]{:S(2)}, u32[]{:S(2)}) collective-permute-start(bf16[256,512]{1,0:T(8,128)(2,1)S(1)} %add_convert_fusion), channel_id=1, source_target_pairs={{0,6},{1,7},{2,4},{3,5},{4,2},{5,3},{6,0},{7,1},{8,14},{9,15},{10,... | collective-permute-start | bytes 786440 | tf_op jit(solution)/shard_map/ppermute | solution.py:25
  72.3 4.8 %collective-permute-done.25.refs_6_ = bf16[256,512]{1,0:T(8,128)(2,1)S(1)} collective-permute-done((bf16[256,512]{1,0:T(8,128)(2,1)S(1)}, bf16[256,512]{1,0:T(8,128)(2,1)S(1)}, u32[]{:S(2)}, u32[]{:S(2)}) %collective-permute-start.25) | collective-permute-done | bytes 262176 | tf_op jit(solution)/shard_map/ppermute | solution.py:25
  77.8 4.1 %collective-permute-done.30.refs_3_ = bf16[256,512]{1,0:T(8,128)(2,1)S(1)} collective-permute-done((bf16[256,512]{1,0:T(8,128)(2,1)S(1)}, bf16[256,512]{1,0:T(8,128)(2,1)S(1)}, u32[]{:S(2)}, u32[]{:S(2)}) %collective-permute-start.30) | collective-permute-done | bytes 262176 | tf_op jit(solution)/shard_map/ppermute | solution.py:25
  (79 shorter events, 22.1 us)
Async XLA Ops:
  0.0 9.1 %collective-permute-start = (bf16[512,512]{1,0:T(8,128)(2,1)}, bf16[512,512]{1,0:T(8,128)(2,1)S(1)}, u32[]{:S(2)}, u32[]{:S(2)}) collective-permute-start(bf16[512,512]{1,0:T(8,128)(2,1)} %refs_0_.11), channel_id=1, source_target_pairs={{0,1},{1,0},{2,3},{3,2},{4,5},{5,4},{6,7},{7,6},{8,9},{9,8},{10,11... | collective-permute-start | bytes 1572872 | tf_op jit(solution)/shard_map/ppermute | solution.py:29
  1.3 10.4 %collective-permute-start.1 = (bf16[256,512]{1,0:T(8,128)(2,1)S(1)}, bf16[256,512]{1,0:T(8,128)(2,1)S(1)}, u32[]{:S(2)}, u32[]{:S(2)}) collective-permute-start(bf16[256,512]{1,0:T(8,128)(2,1)S(1)} %get-tuple-element.49), channel_id=1, source_target_pairs={{0,2},{1,3},{2,0},{3,1},{4,6},{5,7},{6,4},{7,5},{8,10},{9,11},{10,... | collective-permute-start | bytes 786440 | tf_op jit(solution)/shard_map/ppermute | solution.py:25
  3.0 10.3 %collective-permute-start.2 = (bf16[256,512]{1,0:T(8,128)(2,1)S(1)}, bf16[256,512]{1,0:T(8,128)(2,1)S(1)}, u32[]{:S(2)}, u32[]{:S(2)}) collective-permute-start(bf16[256,512]{1,0:T(8,128)(2,1)S(1)} %get-tuple-element.50), channel_id=1, source_target_pairs={{0,6},{1,7},{2,4},{3,5},{4,2},{5,3},{6,0},{7,1},{8,14},{9,15},{10,... | collective-permute-start | bytes 786440 | tf_op jit(solution)/shard_map/ppermute | solution.py:25
  5.2 10.6 %collective-permute-start.3 = (bf16[256,512]{1,0:T(8,128)(2,1)S(1)}, bf16[256,512]{1,0:T(8,128)(2,1)S(1)}, u32[]{:S(2)}, u32[]{:S(2)}) collective-permute-start(bf16[256,512]{1,0:T(8,128)(2,1)S(1)} %get-tuple-element.50), channel_id=1, source_target_pairs={{0,2},{1,3},{2,0},{3,1},{4,6},{5,7},{6,4},{7,5},{8,10},{9,11},{10,... | collective-permute-start | bytes 786440 | tf_op jit(solution)/shard_map/ppermute | solution.py:25
  5.9 13.1 %collective-permute-start.4 = (bf16[256,512]{1,0:T(8,128)(2,1)S(1)}, bf16[256,512]{1,0:T(8,128)(2,1)S(1)}, u32[]{:S(2)}, u32[]{:S(2)}) collective-permute-start(bf16[256,512]{1,0:T(8,128)(2,1)S(1)} %get-tuple-element.49), channel_id=1, source_target_pairs={{0,6},{1,7},{2,4},{3,5},{4,2},{5,3},{6,0},{7,1},{8,14},{9,15},{10,... | collective-permute-start | bytes 786440 | tf_op jit(solution)/shard_map/ppermute | solution.py:25
  13.3 10.8 %collective-permute-start.7 = (bf16[256,512]{1,0:T(8,128)(2,1)S(1)}, bf16[256,512]{1,0:T(8,128)(2,1)S(1)}, u32[]{:S(2)}, u32[]{:S(2)}) collective-permute-start(bf16[256,512]{1,0:T(8,128)(2,1)S(1)} %get-tuple-element.54.refs_0_), channel_id=1, source_target_pairs={{0,6},{1,7},{2,4},{3,5},{4,2},{5,3},{6,0},{7,1},{8,14},{9,15},{10,... | collective-permute-start | bytes 786440 | tf_op jit(solution)/shard_map/ppermute | solution.py:25
  15.5 8.6 %collective-permute-start.8 = (bf16[256,512]{1,0:T(8,128)(2,1)S(1)}, bf16[256,512]{1,0:T(8,128)(2,1)S(1)}, u32[]{:S(2)}, u32[]{:S(2)}) collective-permute-start(bf16[256,512]{1,0:T(8,128)(2,1)S(1)} %get-tuple-element.55.refs_3_), channel_id=1, source_target_pairs={{0,2},{1,3},{2,0},{3,1},{4,6},{5,7},{6,4},{7,5},{8,10},{9,11},{10,... | collective-permute-start | bytes 786440 | tf_op jit(solution)/shard_map/ppermute | solution.py:25
  19.0 6.2 %collective-permute-start.5 = (bf16[512,512]{1,0:T(8,128)(2,1)S(1)}, bf16[512,512]{1,0:T(8,128)(2,1)S(1)}, u32[]{:S(2)}, u32[]{:S(2)}) collective-permute-start(bf16[512,512]{1,0:T(8,128)(2,1)S(1)} %get-tuple-element.56.refs_0_.refs_2_), channel_id=1, source_target_pairs={{0,1},{1,0},{2,3},{3,2},{4,5},{5,4},{6,7},{7,6},{8,9},{9,8},{10,11... | collective-permute-start | bytes 1572872 | tf_op jit(solution)/shard_map/ppermute | solution.py:29
  19.1 6.2 %collective-permute-start.6 = (bf16[512,512]{1,0:T(8,128)(2,1)S(1)}, bf16[512,512]{1,0:T(8,128)(2,1)S(1)}, u32[]{:S(2)}, u32[]{:S(2)}) collective-permute-start(bf16[512,512]{1,0:T(8,128)(2,1)S(1)} %get-tuple-element.57.refs_1_.refs_3_), channel_id=1, source_target_pairs={{0,1},{1,0},{2,3},{3,2},{4,5},{5,4},{6,7},{7,6},{8,9},{9,8},{10,11... | collective-permute-start | bytes 1572872 | tf_op jit(solution)/shard_map/ppermute | solution.py:29
  19.6 43.7 %collective-permute-start.23 = (bf16[512,1024]{1,0:T(8,128)(2,1)S(1)}, bf16[512,1024]{1,0:T(8,128)(2,1)S(1)}, u32[]{:S(2)}, u32[]{:S(2)}) collective-permute-start(bf16[512,1024]{1,0:T(8,128)(2,1)S(1)} %get-tuple-element.85), channel_id=1, source_target_pairs={{0,1},{1,0},{2,3},{3,2},{4,5},{5,4},{6,7},{7,6},{8,9},{9,8},{10,11... | collective-permute-start | bytes 3145736 | tf_op jit(solution)/shard_map/ppermute | solution.py:29
  25.2 33.8 %collective-permute-start.24 = (bf16[512,512]{1,0:T(8,128)(2,1)S(1)}, bf16[512,512]{1,0:T(8,128)(2,1)S(1)}, u32[]{:S(2)}, u32[]{:S(2)}) collective-permute-start(bf16[512,512]{1,0:T(8,128)(2,1)S(1)} %get-tuple-element.86), channel_id=1, source_target_pairs={{0,1},{1,0},{2,3},{3,2},{4,5},{5,4},{6,7},{7,6},{8,9},{9,8},{10,11... | collective-permute-start | bytes 1572872 | tf_op jit(solution)/shard_map/ppermute | solution.py:29
  27.4 6.8 %collective-permute-start.11 = (bf16[80,512]{1,0:T(8,128)(2,1)S(1)}, bf16[80,512]{1,0:T(8,128)(2,1)S(1)}, u32[]{:S(2)}, u32[]{:S(2)}) collective-permute-start(bf16[80,512]{1,0:T(8,128)(2,1)S(1)} %get-tuple-element.72), channel_id=1, source_target_pairs={{0,8},{8,0},{16,24},{24,16},{32,40},{40,32},{48,56},{56,48},{64,72... | collective-permute-start | bytes 245768 | tf_op jit(solution)/shard_map/ppermute | solution.py:33
  29.4 8.2 %collective-permute-start.12 = (bf16[80,512]{1,0:T(8,128)(2,1)S(1)}, bf16[80,512]{1,0:T(8,128)(2,1)S(1)}, u32[]{:S(2)}, u32[]{:S(2)}) collective-permute-start(bf16[80,512]{1,0:T(8,128)(2,1)S(1)} %get-tuple-element.73), channel_id=1, source_target_pairs={{0,16},{8,24},{16,0},{24,8},{32,48},{40,56},{48,32},{56,40},{64,80... | collective-permute-start | bytes 245768 | tf_op jit(solution)/shard_map/ppermute | solution.py:33
  32.9 6.3 %collective-permute-start.13 = (bf16[80,512]{1,0:T(8,128)(2,1)S(1)}, bf16[80,512]{1,0:T(8,128)(2,1)S(1)}, u32[]{:S(2)}, u32[]{:S(2)}) collective-permute-start(bf16[80,512]{1,0:T(8,128)(2,1)S(1)} %get-tuple-element.74), channel_id=1, source_target_pairs={{0,24},{8,16},{16,8},{24,0},{32,56},{40,48},{48,40},{56,32},{64,88... | collective-permute-start | bytes 245768 | tf_op jit(solution)/shard_map/ppermute | solution.py:33
  39.3 7.3 %collective-permute-start.14 = (bf16[80,512]{1,0:T(8,128)(2,1)S(1)}, bf16[80,512]{1,0:T(8,128)(2,1)S(1)}, u32[]{:S(2)}, u32[]{:S(2)}) collective-permute-start(bf16[80,512]{1,0:T(8,128)(2,1)S(1)} %line.1.refs_11_), channel_id=1, source_target_pairs={{0,32},{8,40},{16,48},{24,56},{32,0},{40,8},{48,16},{56,24},{64,96... | collective-permute-start | bytes 245768 | tf_op jit(solution)/shard_map/ppermute | solution.py:37
  40.9 6.8 %collective-permute-start.15 = (bf16[80,512]{1,0:T(8,128)(2,1)S(1)}, bf16[80,512]{1,0:T(8,128)(2,1)S(1)}, u32[]{:S(2)}, u32[]{:S(2)}) collective-permute-start(bf16[80,512]{1,0:T(8,128)(2,1)S(1)} %line.1.refs_11_), channel_id=1, source_target_pairs={{0,64},{8,72},{16,80},{24,88},{32,96},{40,104},{48,112},{56,120},{... | collective-permute-start | bytes 245768 | tf_op jit(solution)/shard_map/ppermute | solution.py:37
  49.9 6.0 %collective-permute-start.18 = (bf16[64,512]{1,0:T(8,128)(2,1)S(1)}, bf16[64,512]{1,0:T(8,128)(2,1)S(1)}, u32[]{:S(2)}, u32[]{:S(2)}) collective-permute-start(bf16[64,512]{1,0:T(8,128)(2,1)S(1)} %get-tuple-element.78), channel_id=1, source_target_pairs={{0,16},{8,24},{16,0},{24,8},{32,48},{40,56},{48,32},{56,40},{64,80... | collective-permute-start | bytes 196616 | tf_op jit(solution)/shard_map/ppermute | solution.py:33
  60.6 9.2 %collective-permute-start.29 = (bf16[256,512]{1,0:T(8,128)(2,1)S(1)}, bf16[256,512]{1,0:T(8,128)(2,1)S(1)}, u32[]{:S(2)}, u32[]{:S(2)}) collective-permute-start(bf16[256,512]{1,0:T(8,128)(2,1)S(1)} %far1.1.refs_7_), channel_id=1, source_target_pairs={{0,2},{1,3},{2,0},{3,1},{4,6},{5,7},{6,4},{7,5},{8,10},{9,11},{10,... | collective-permute-start | bytes 786440 | tf_op jit(solution)/shard_map/ppermute | solution.py:25
  60.7 11.6 %collective-permute-start.22 = (bf16[512,512]{1,0:T(8,128)(2,1)S(1)}, bf16[512,512]{1,0:T(8,128)(2,1)S(1)}, u32[]{:S(2)}, u32[]{:S(2)}) collective-permute-start(bf16[512,512]{1,0:T(8,128)(2,1)S(1)} %get-tuple-element.83), channel_id=1, source_target_pairs={{0,1},{1,0},{2,3},{3,2},{4,5},{5,4},{6,7},{7,6},{8,9},{9,8},{10,11... | collective-permute-start | bytes 1572872 | tf_op jit(solution)/shard_map/ppermute | solution.py:29
  61.1 11.0 %collective-permute-start.27 = (bf16[256,512]{1,0:T(8,128)(2,1)S(1)}, bf16[256,512]{1,0:T(8,128)(2,1)S(1)}, u32[]{:S(2)}, u32[]{:S(2)}) collective-permute-start(bf16[256,512]{1,0:T(8,128)(2,1)S(1)} %far0.1.refs_4_.refs_6_), channel_id=1, source_target_pairs={{0,6},{1,7},{2,4},{3,5},{4,2},{5,3},{6,0},{7,1},{8,14},{9,15},{10,... | collective-permute-start | bytes 786440 | tf_op jit(solution)/shard_map/ppermute | solution.py:25
  64.6 12.6 %collective-permute-start.25 = (bf16[256,512]{1,0:T(8,128)(2,1)S(1)}, bf16[256,512]{1,0:T(8,128)(2,1)S(1)}, u32[]{:S(2)}, u32[]{:S(2)}) collective-permute-start(bf16[256,512]{1,0:T(8,128)(2,1)S(1)} %get-tuple-element.87), channel_id=1, source_target_pairs={{0,6},{1,7},{2,4},{3,5},{4,2},{5,3},{6,0},{7,1},{8,14},{9,15},{10,... | collective-permute-start | bytes 786440 | tf_op jit(solution)/shard_map/ppermute | solution.py:25
  65.7 11.4 %collective-permute-start.26 = (bf16[256,512]{1,0:T(8,128)(2,1)S(1)}, bf16[256,512]{1,0:T(8,128)(2,1)S(1)}, u32[]{:S(2)}, u32[]{:S(2)}) collective-permute-start(bf16[256,512]{1,0:T(8,128)(2,1)S(1)} %get-tuple-element.88), channel_id=1, source_target_pairs={{0,2},{1,3},{2,0},{3,1},{4,6},{5,7},{6,4},{7,5},{8,10},{9,11},{10,... | collective-permute-start | bytes 786440 | tf_op jit(solution)/shard_map/ppermute | solution.py:25
  69.9 12.0 %collective-permute-start.30 = (bf16[256,512]{1,0:T(8,128)(2,1)S(1)}, bf16[256,512]{1,0:T(8,128)(2,1)S(1)}, u32[]{:S(2)}, u32[]{:S(2)}) collective-permute-start(bf16[256,512]{1,0:T(8,128)(2,1)S(1)} %add_convert_fusion), channel_id=1, source_target_pairs={{0,6},{1,7},{2,4},{3,5},{4,2},{5,3},{6,0},{7,1},{8,14},{9,15},{10,... | collective-permute-start | bytes 786440 | tf_op jit(solution)/shard_map/ppermute | solution.py:25
  72.2 9.7 %collective-permute-start.28 = (bf16[256,512]{1,0:T(8,128)(2,1)S(1)}, bf16[256,512]{1,0:T(8,128)(2,1)S(1)}, u32[]{:S(2)}, u32[]{:S(2)}) collective-permute-start(bf16[256,512]{1,0:T(8,128)(2,1)S(1)} %add_convert_fusion.1), channel_id=1, source_target_pairs={{0,2},{1,3},{2,0},{3,1},{4,6},{5,7},{6,4},{7,5},{8,10},{9,11},{10,... | collective-permute-start | bytes 786440 | tf_op jit(solution)/shard_map/ppermute | solution.py:25
  (15 other events, 84.3 us)

commit v4 on v3

--- a/solution.py
+++ b/solution.py
@@ -21,8 +21,16 @@
 HBM = pl.BlockSpec(memory_space=pltpu.HBM)
 
 
+def turn(k, core):
+    return k ^ (2 * core) if k % 2 else k
+
+
+def meet(k, core):
+    return turn((0, 2, 3, 1)[k], core)
+
+
 def y_flip(value, k):
-    return lax.ppermute(value, "tp", [(i, i ^ (2 * k)) for i in range(8)])
+    return lax.ppermute(value, "tp", [(i, i ^ (2 * turn(k, i % 2))) for i in range(8)])
 
 
 def tp_swap(value):
@@ -30,11 +38,16 @@
 
 
 def z_flip(value, k):
-    return lax.ppermute(value, "ctx", [(i, i ^ k) for i in range(16)])
+    return ctx_flip(value, k, 1)
 
 
 def x_flip(value, k):
-    return lax.ppermute(value, "ctx", [(i, i ^ (4 * k)) for i in range(16)])
+    return ctx_flip(value, k, 4)
+
+
+def ctx_flip(value, k, unit):
+    pairs = [(8 * i + j, 8 * (i ^ (unit * meet(k, j % 2))) + j) for i in range(16) for j in range(8)]
+    return lax.ppermute(value, ("ctx", "tp"), pairs)
 
 
 def my(name):
@@ -44,7 +57,7 @@
 
 def rows_of(step, same):
     core = my("core") if same else 1 - my("core")
-    return pl.ds(pl.multiple_of((2 * (my("y") ^ step) + core) * WIDE, WIDE), WIDE)
+    return pl.ds(pl.multiple_of((2 * (my("y") ^ turn(step, core)) + core) * WIDE, WIDE), WIDE)
 
 
 def dot(a, b):
@@ -146,7 +159,7 @@
     high = total.astype(BF)
     rest = (total - high.astype(F32)).astype(BF)
     for i, ref in enumerate((mine, m1, m2, m3)):
-        piece = state[pl.ds(pl.multiple_of((z ^ i) * CUT, CUT), CUT), :]
+        piece = state[pl.ds(pl.multiple_of((z ^ meet(i, my("core"))) * CUT, CUT), CUT), :]
         if i == 0:
             ref[...] = piece
         else:
@@ -180,7 +193,7 @@
     z = my("z")
     pieces = [mine[...]] + [piece for piece, _ in opened]
     factors = [factor[...]] + [f for _, f in opened]
-    return pieces, factors, [z ^ k for k in range(SIDE)]
+    return pieces, factors, [z ^ meet(k, my("core")) for k in range(SIDE)]
 
 
 def line_body(mine, factor, m1, m2, m3, out):
@@ -198,9 +211,9 @@
     pieces, factors, sources = line_of(mine, factor, (m1, m2, m3))
     x, z = my("x"), my("z")
     opened = [open_message(n) for n in (n1, n2, n3)]
-    entry = prefix([p for p, _ in opened], [f for _, f in opened], [x ^ k for k in range(1, SIDE)], x)
+    entry = prefix([p for p, _ in opened], [f for _, f in opened], [x ^ meet(k, my("core")) for k in range(1, SIDE)], x)
     for k, ref in enumerate((e0, e1, e2, e3)):
-        target = z ^ k
+        target = z ^ meet(k, my("core"))
         whole = prefix(pieces, factors, sources, target) + between(factors, sources, -1, target) * entry
         ref[...] = whole.astype(BF)
 
@@ -230,7 +243,7 @@
     z = my("z")
     rows = pl.ds(half * HALF, HALF)
     for k, ref in enumerate((e0, e1, e2, e3)):
-        whole[pl.ds(pl.multiple_of((z ^ k) * CUT, CUT), CUT), :] = ref[...]
+        whole[pl.ds(pl.multiple_of((z ^ meet(k, my("core"))) * CUT, CUT), CUT), :] = ref[...]
     retained = local[rows, :] + decay[rows, :] * dot(queries[rows, :], whole[...])
     center = retained - jnp.mean(retained, axis=-1, keepdims=True)
     variance = jnp.mean(center * center, axis=-1, keepdims=True)
@@ -250,14 +263,14 @@
 STEPS = (2, 1, 3, 0)
 
 
-def pick_body(weight, given_far, given, given_own, kept_far, kept, kept_own, sems):
+def pick_body(weight, given_far, given, kept_far, kept, sems):
     core, y = my("core"), my("y")
     copies = []
     for i, step in enumerate(STEPS):
-        block = y ^ step
-        for j, (outs, which) in enumerate((((given_far, given, given_own), 1 - core), ((kept_far, kept, kept_own), core))):
+        for j, (outs, which) in enumerate((((given_far, given), 1 - core), ((kept_far, kept), core))):
+            block = y ^ turn(step, which)
             columns = pl.ds(pl.multiple_of((2 * block + which) * DV, DV), DV)
-            out = (outs[0], outs[1].at[:, pl.ds(0, DV)], outs[1].at[:, pl.ds(DV, DV)], outs[2])[i]
+            out = outs[0] if i == 0 else outs[1].at[:, pl.ds((i - 1) * DV, DV)]
             copy = pltpu.make_async_copy(weight.at[:, columns], out, sems.at[i, j])
             copy.start()
             copies.append(copy)
@@ -269,14 +282,16 @@
     hidden = jnp.concatenate([r[...] for r in refs[:n]], axis=0)
     other = jnp.concatenate([r[...] for r in refs[n: 2 * n]], axis=0)
     mine, theirs, outs = refs[2 * n], refs[2 * n + 1], refs[2 * n + 2:]
-    total = dot(hidden, mine[...]) + dot(other, theirs[...])
+    columns = pl.ds(0, len(outs) // n * DV)
+    total = dot(hidden, mine[:, columns]) + dot(other, theirs[:, columns])
     for i, out in enumerate(outs):
         rows, columns = (i % n) * HALF, (i // n) * DV
         out[...] = total[rows: rows + HALF, columns: columns + DV].astype(out.dtype)
 
 
 def partial(hidden, other, mine, theirs, kinds, name, after=()):
-    width, n = mine.shape[1], len(hidden)
+    n = len(hidden)
+    width = len(kinds) // n * DV
     return call(
         functools.partial(partial_body, n),
         [((HALF, DV), kind) for kind in kinds],
@@ -290,8 +305,9 @@
 
 
 def own_body(h0, h1, o0, o1, mine, theirs, top, low, out_top, out_low):
+    columns = pl.ds(2 * DV, DV)
     for h, o, come, out in ((h0, o0, top, out_top), (h1, o1, low, out_low)):
-        out[...] = dot(h[...], mine[...]) + dot(o[...], theirs[...]) + come[...].astype(F32)
+        out[...] = dot(h[...], mine[:, columns]) + dot(o[...], theirs[:, columns]) + come[...].astype(F32)
 
 
 def final_body(own_top, own_low, top, low, out):
@@ -320,15 +336,15 @@
         [log_decay],
         "decay",
     )
-    given_far, given, given_own, kept_far, kept, kept_own = call(
-        pick_body, [((DV, DV), BF), ((DV, 2 * DV), BF), ((DV, DV), BF)] * 2, [HBM], [w_out], "pick",
+    given_far, given, kept_far, kept = call(
+        pick_body, [((DV, DV), BF), ((DV, 3 * DV), BF)] * 2, [HBM], [w_out], "pick",
         scratch=[pltpu.SemaphoreType.DMA((SIDE, 2))], moved=1,
     )
     kv = (w_key, w_value)
     sums = project(((0, 1), (0, 0)), (tokens, own_s), kv, None, "kv_own", hint=0)
     a1, a3 = tie((a1, a3), [kept_far, mask, sums[0]], "tie_a")
     c3, c1 = y_flip(a1, 3), y_flip(a3, 1)
-    theirs_far, theirs, theirs_own = tp_swap(given_far), tp_swap(given), tp_swap(given_own)
+    theirs_far, theirs = tp_swap(given_far), tp_swap(given)
 
     near1, near3 = call(join_body, [((ROWS, WIDE), BF)] * 2, [VM] * 4, [a1, b1, b3, a3], "join", moved=1)
     near1_s, near3_s = tp_swap(near1), tp_swap(near3)
@@ -389,7 +405,7 @@
     from1_low, from3_top = y_flip(low1, 1), y_flip(top3, 3)
     from1_top, from3_low = y_flip(added(top1, via3), 1), y_flip(added(low3, via1), 3)
     own = call(
-        own_body, [((HALF, DV), F32)] * 2, [VM] * 8, [*hidden, *other, kept_own, theirs_own, from3_top, from1_low], "own",
+        own_body, [((HALF, DV), F32)] * 2, [VM] * 8, [*hidden, *other, kept, theirs, from3_top, from1_low], "own",
         flops=4 * ROWS * DV * DV, moved=8 * DV * DV,
     )
     (out,) = call(

time: 83.2 us -> 79.1 us (0.951)
  waiting for transfers between devices: 31.7 us -> 26.5 us
    ppermute x21, waiting for transfers between devices: 31 us -> 25.8 us  [the longest x12 16.5 us: y_flip(): lax.ppermute(value, 'tp', [(i, i ^ 2 * turn(k, i % 2)) for i in range(8)])]
    ppermute x21, starting transfers between devices: 28.9 us -> 29.9 us  [the longest x12 16.9 us: y_flip(): lax.ppermute(value, 'tp', [(i, i ^ 2 * turn(k, i % 2)) for i in range(8)])]
    ppermute x10 -> x9, starting transfers between devices: 2.46 us -> 1.98 us  [tp_swap(): return lax.ppermute(value, 'tp', [(i, i ^ 1) for i in range(8)])]
  transfers between devices with their start and end apart: 31 -> 30, of which waited for: 15 -> 13; matrix products, arithmetic and copies ran while one was open for 0% -> 0% of each run, Pallas kernels for 19% -> 20%
where the time goes in v4:
time: 79.1 us; the launch traced here: 78.1 us
  starting transfers between devices  31.8 us (40%)
  waiting for transfers between devices  26.5 us (34%)
  Pallas kernels  16.6 us (21%)
  local copies, waits for them, and re-layouts  2.66 us (3%)
    ppermute x12, starting transfers between devices, y_flip(): lax.ppermute(value, 'tp', [(i, i ^ 2 * turn(k, i % 2)) for i in range(8)])  16.9 us
    pallas_call x21, Pallas kernels, call(): pl.pallas_call(whole, out_shape=shapes, in_specs=list(in_specs) + [ANY] *...  16.6 us
    ppermute x12, waiting for transfers between devices, y_flip(): lax.ppermute(value, 'tp', [(i, i ^ 2 * turn(k, i % 2)) for i in range(8)])  16.5 us
    ppermute x9, starting transfers between devices, ctx_flip(): return lax.ppermute(value, ('ctx', 'tp'), pairs)  13 us
    ppermute x9, waiting for transfers between devices, ctx_flip(): return lax.ppermute(value, ('ctx', 'tp'), pairs)  9.26 us
    unnamed x16, local copies, waits for them, and re-layouts  2.66 us
    ppermute x9, starting transfers between devices, tp_swap(): return lax.ppermute(value, 'tp', [(i, i ^ 1) for i in range(8)])  1.98 us
  transfers between devices with their start and end apart: 30, of which 13 were waited for; matrix products, arithmetic and copies ran while one was open for 0% of the time, Pallas kernels for 20%

profile of v4, /device:TPU:0, one launch (start us, length us, event | category | flops | bytes accessed | tf_op | source)
XLA Modules:
  0.0 78.1 jit_solution(11286984581360368148)
XLA Ops:
  1.1 1.7 %collective-permute-start.1 = (bf16[256,512]{1,0:T(8,128)(2,1)S(1)}, bf16[256,512]{1,0:T(8,128)(2,1)S(1)}, u32[]{:S(2)}, u32[]{:S(2)}) collective-permute-start(bf16[256,512]{1,0:T(8,128)(2,1)S(1)} %get-tuple-element.47), channel_id=1, source_target_pairs={{0,2},{1,7},{2,0},{3,5},{4,6},{5,3},{6,4},{7,1},{8,10},{9,15},{10,... | collective-permute-start | bytes 786440 | tf_op jit(solution)/shard_map/ppermute | solution.py:33
  2.9 2.2 %collective-permute-start.2 = (bf16[256,512]{1,0:T(8,128)(2,1)S(1)}, bf16[256,512]{1,0:T(8,128)(2,1)S(1)}, u32[]{:S(2)}, u32[]{:S(2)}) collective-permute-start(bf16[256,512]{1,0:T(8,128)(2,1)S(1)} %get-tuple-element.48), channel_id=1, source_target_pairs={{0,6},{1,3},{2,4},{3,1},{4,2},{5,7},{6,0},{7,5},{8,14},{9,11},{10,... | collective-permute-start | bytes 786440 | tf_op jit(solution)/shard_map/ppermute | solution.py:33
  6.3 2.2 %pick.1 = (bf16[512,512]{1,0:T(8,128)(2,1)S(1)}, bf16[512,1536]{1,0:T(8,128)(2,1)S(1)}, bf16[512,512]{1,0:T(8,128)(2,1)S(1)}, bf16[512,1536]{1,0:T(8,128)(2,1)S(1)}) custom-call(bf16[512,4096]{1,0:T(8,128)(2,1)} %refs_0_.7), custom_call_target="tpu_custom_call" | custom-call | bytes 1 | tf_op jit(solution)/shard_map/pick/pallas_call | solution.py:73
  9.1 1.6 %copy-done.1 = bf16[4096,256]{1,0:T(8,128)(2,1)S(1)} copy-done((bf16[4096,256]{1,0:T(8,128)(2,1)S(1)}, bf16[4096,256]{1,0:T(8,128)(2,1)}, u32[]{:S(2)}) %copy-start.1) | copy-done | bytes 2097176
  11.7 1.7 %collective-permute-done.2.refs_1_ = bf16[256,512]{1,0:T(8,128)(2,1)S(1)} collective-permute-done((bf16[256,512]{1,0:T(8,128)(2,1)S(1)}, bf16[256,512]{1,0:T(8,128)(2,1)S(1)}, u32[]{:S(2)}, u32[]{:S(2)}) %collective-permute-start.2) | collective-permute-done | bytes 262176 | tf_op jit(solution)/shard_map/ppermute | solution.py:33
  13.3 2.1 %collective-permute-start.7 = (bf16[256,512]{1,0:T(8,128)(2,1)S(1)}, bf16[256,512]{1,0:T(8,128)(2,1)S(1)}, u32[]{:S(2)}, u32[]{:S(2)}) collective-permute-start(bf16[256,512]{1,0:T(8,128)(2,1)S(1)} %get-tuple-element.52.refs_0_), channel_id=1, source_target_pairs={{0,6},{1,3},{2,4},{3,1},{4,2},{5,7},{6,0},{7,5},{8,14},{9,11},{10,... | collective-permute-start | bytes 786440 | tf_op jit(solution)/shard_map/ppermute | solution.py:33
  15.5 1.4 %collective-permute-done.4.refs_2_ = bf16[256,512]{1,0:T(8,128)(2,1)S(1)} collective-permute-done((bf16[256,512]{1,0:T(8,128)(2,1)S(1)}, bf16[256,512]{1,0:T(8,128)(2,1)S(1)}, u32[]{:S(2)}, u32[]{:S(2)}) %collective-permute-start.4) | collective-permute-done | bytes 262176 | tf_op jit(solution)/shard_map/ppermute | solution.py:33
  18.6 4.0 %collective-permute-done.7.refs_0_ = bf16[256,512]{1,0:T(8,128)(2,1)S(1)} collective-permute-done((bf16[256,512]{1,0:T(8,128)(2,1)S(1)}, bf16[256,512]{1,0:T(8,128)(2,1)S(1)}, u32[]{:S(2)}, u32[]{:S(2)}) %collective-permute-start.7) | collective-permute-done | bytes 262176 | tf_op jit(solution)/shard_map/ppermute | solution.py:33
  25.9 4.0 %collective-permute-start.11 = (bf16[80,512]{1,0:T(8,128)(2,1)S(1)}, bf16[80,512]{1,0:T(8,128)(2,1)S(1)}, u32[]{:S(2)}, u32[]{:S(2)}) collective-permute-start(bf16[80,512]{1,0:T(8,128)(2,1)S(1)} %get-tuple-element.70), channel_id=1, source_target_pairs={{0,16},{1,17},{2,18},{3,19},{4,20},{5,21},{6,22},{7,23},{8,24},{9,... | collective-permute-start | bytes 245768 | tf_op jit(solution)/shard_map/ppermute | solution.py:50
  30.9 1.2 %queries.1.refs_5_.refs_0_ = f32[512,256]{1,0:T(8,128)S(1)} custom-call(bf16[512,512]{1,0:T(8,128)(2,1)S(1)} %copy-done.4, bf16[512,512]{1,0:T(8,128)(2,1)S(1)} %collective-permute-done.refs_1_, bf16[512,512]{1,0:T(8,128)(2,1)S(1)} %get-tuple-element.54.refs_0_.refs_2_, bf16[512,512]{1,0:T(8,128)(2,1)S(1)} %get-tuple-element.55.refs_1_.refs_3_, ...), custom_call_target="tpu_custom_call" | custom-call | flops 1073741824 | bytes 2097153 | tf_op jit(solution)/shard_map/queries/pallas_call | solution.py:73
  33.0 3.3 %collective-permute-done.12.refs_3_ = bf16[80,512]{1,0:T(8,128)(2,1)S(1)} collective-permute-done((bf16[80,512]{1,0:T(8,128)(2,1)S(1)}, bf16[80,512]{1,0:T(8,128)(2,1)S(1)}, u32[]{:S(2)}, u32[]{:S(2)}) %collective-permute-start.12) | collective-permute-done | bytes 81952 | tf_op jit(solution)/shard_map/ppermute | solution.py:50
  36.4 3.1 %collective-permute-start.14 = (bf16[80,512]{1,0:T(8,128)(2,1)S(1)}, bf16[80,512]{1,0:T(8,128)(2,1)S(1)}, u32[]{:S(2)}, u32[]{:S(2)}) collective-permute-start(bf16[80,512]{1,0:T(8,128)(2,1)S(1)} %line.1.refs_11_), channel_id=1, source_target_pairs={{0,64},{1,65},{2,66},{3,67},{4,68},{5,69},{6,70},{7,71},{8,72},{9,... | collective-permute-start | bytes 245768 | tf_op jit(solution)/shard_map/ppermute | solution.py:50
  40.7 2.5 %gates.1.refs_8_.refs_7_ = f32[512,512]{1,0:T(8,128)S(1)} custom-call(bf16[512,512]{1,0:T(8,128)(2,1)S(1)} %copy-done.4, bf16[512,512]{1,0:T(8,128)(2,1)S(1)} %collective-permute-done.refs_1_, bf16[512,512]{1,0:T(8,128)(2,1)S(1)} %get-tuple-element.54.refs_0_.refs_2_, bf16[512,512]{1,0:T(8,128)(2,1)S(1)} %get-tuple-element.55.refs_1_.refs_3_, ...), custom_call_target="tpu_custom_call" | custom-call | flops 2147483648 | bytes 4194305 | tf_op jit(solution)/shard_map/gates/pallas_call | solution.py:73
  43.2 2.0 %collective-permute-done.15.refs_6_ = bf16[80,512]{1,0:T(8,128)(2,1)S(1)} collective-permute-done((bf16[80,512]{1,0:T(8,128)(2,1)S(1)}, bf16[80,512]{1,0:T(8,128)(2,1)S(1)}, u32[]{:S(2)}, u32[]{:S(2)}) %collective-permute-start.15) | collective-permute-done | bytes 81952 | tf_op jit(solution)/shard_map/ppermute | solution.py:50
  45.5 1.9 %collective-permute-start.17 = (bf16[64,512]{1,0:T(8,128)(2,1)S(1)}, bf16[64,512]{1,0:T(8,128)(2,1)S(1)}, u32[]{:S(2)}, u32[]{:S(2)}) collective-permute-start(bf16[64,512]{1,0:T(8,128)(2,1)S(1)} %get-tuple-element.75), channel_id=1, source_target_pairs={{0,16},{1,17},{2,18},{3,19},{4,20},{5,21},{6,22},{7,23},{8,24},{9,... | collective-permute-start | bytes 196616 | tf_op jit(solution)/shard_map/ppermute | solution.py:50
  47.4 1.1 %collective-permute-start.18 = (bf16[64,512]{1,0:T(8,128)(2,1)S(1)}, bf16[64,512]{1,0:T(8,128)(2,1)S(1)}, u32[]{:S(2)}, u32[]{:S(2)}) collective-permute-start(bf16[64,512]{1,0:T(8,128)(2,1)S(1)} %get-tuple-element.76), channel_id=1, source_target_pairs={{0,24},{1,9},{2,26},{3,11},{4,28},{5,13},{6,30},{7,15},{8,16},{9,1... | collective-permute-start | bytes 196616 | tf_op jit(solution)/shard_map/ppermute | solution.py:50
  49.9 1.7 %collective-permute-done.17.refs_2_ = bf16[64,512]{1,0:T(8,128)(2,1)S(1)} collective-permute-done((bf16[64,512]{1,0:T(8,128)(2,1)S(1)}, bf16[64,512]{1,0:T(8,128)(2,1)S(1)}, u32[]{:S(2)}, u32[]{:S(2)}) %collective-permute-start.17) | collective-permute-done | bytes 65568 | tf_op jit(solution)/shard_map/ppermute | solution.py:50
  51.6 1.3 %collective-permute-done.18.refs_3_ = bf16[64,512]{1,0:T(8,128)(2,1)S(1)} collective-permute-done((bf16[64,512]{1,0:T(8,128)(2,1)S(1)}, bf16[64,512]{1,0:T(8,128)(2,1)S(1)}, u32[]{:S(2)}, u32[]{:S(2)}) %collective-permute-start.18) | collective-permute-done | bytes 65568 | tf_op jit(solution)/shard_map/ppermute | solution.py:50
  56.7 2.4 %collective-permute-start.26 = (bf16[256,512]{1,0:T(8,128)(2,1)S(1)}, bf16[256,512]{1,0:T(8,128)(2,1)S(1)}, u32[]{:S(2)}, u32[]{:S(2)}) collective-permute-start(bf16[256,512]{1,0:T(8,128)(2,1)S(1)} %far0.1.refs_4_.refs_6_), channel_id=1, source_target_pairs={{0,6},{1,3},{2,4},{3,1},{4,2},{5,7},{6,0},{7,5},{8,14},{9,11},{10,... | collective-permute-start | bytes 786440 | tf_op jit(solution)/shard_map/ppermute | solution.py:33
  59.1 1.2 %beside.1 = (f32[256,512]{1,0:T(8,128)S(1)}, bf16[256,512]{1,0:T(8,128)(2,1)S(1)}, bf16[256,512]{1,0:T(8,128)(2,1)S(1)}, f32[256,512]{1,0:T(8,128)S(1)}) custom-call(bf16[256,512]{1,0:T(8,128)(2,1)S(1)} %hidden0.1.refs_8_.refs_0_, bf16[256,512]{1,0:T(8,128)(2,1)S(1)} %hidden1.1.refs_0_.refs_1_, bf16[256,512]{1,0:T(8,128)(2,1)S(1)} %collective-permute-done.20.refs_1_.refs_2_, ...), custom_call_target="tpu_custom_call" | custom-call | flops 1073741824 | bytes 2097152 | tf_op jit(solution)/shard_map/beside/pallas_call | solution.py:73
  61.8 1.4 %collective-permute-done.28 = bf16[256,512]{1,0:T(8,128)(2,1)S(1)} collective-permute-done((bf16[256,512]{1,0:T(8,128)(2,1)S(1)}, bf16[256,512]{1,0:T(8,128)(2,1)S(1)}, u32[]{:S(2)}, u32[]{:S(2)}) %collective-permute-start.28) | collective-permute-done | bytes 262176 | tf_op jit(solution)/shard_map/ppermute | solution.py:33
  63.3 4.9 %collective-permute-start.29 = (bf16[256,512]{1,0:T(8,128)(2,1)S(1)}, bf16[256,512]{1,0:T(8,128)(2,1)S(1)}, u32[]{:S(2)}, u32[]{:S(2)}) collective-permute-start(bf16[256,512]{1,0:T(8,128)(2,1)S(1)} %add_convert_fusion), channel_id=1, source_target_pairs={{0,6},{1,3},{2,4},{3,1},{4,2},{5,7},{6,0},{7,5},{8,14},{9,11},{10,... | collective-permute-start | bytes 786440 | tf_op jit(solution)/shard_map/ppermute | solution.py:33
  68.4 3.3 %collective-permute-done.24.refs_6_ = bf16[256,512]{1,0:T(8,128)(2,1)S(1)} collective-permute-done((bf16[256,512]{1,0:T(8,128)(2,1)S(1)}, bf16[256,512]{1,0:T(8,128)(2,1)S(1)}, u32[]{:S(2)}, u32[]{:S(2)}) %collective-permute-start.24) | collective-permute-done | bytes 262176 | tf_op jit(solution)/shard_map/ppermute | solution.py:33
  72.4 4.7 %collective-permute-done.29.refs_3_ = bf16[256,512]{1,0:T(8,128)(2,1)S(1)} collective-permute-done((bf16[256,512]{1,0:T(8,128)(2,1)S(1)}, bf16[256,512]{1,0:T(8,128)(2,1)S(1)}, u32[]{:S(2)}, u32[]{:S(2)}) %collective-permute-start.29) | collective-permute-done | bytes 262176 | tf_op jit(solution)/shard_map/ppermute | solution.py:33
  (77 shorter events, 20.6 us)
Async XLA Ops:
  0.0 8.6 %collective-permute-start = (bf16[512,512]{1,0:T(8,128)(2,1)}, bf16[512,512]{1,0:T(8,128)(2,1)S(1)}, u32[]{:S(2)}, u32[]{:S(2)}) collective-permute-start(bf16[512,512]{1,0:T(8,128)(2,1)} %refs_0_.11), channel_id=1, source_target_pairs={{0,1},{1,0},{2,3},{3,2},{4,5},{5,4},{6,7},{7,6},{8,9},{9,8},{10,11... | collective-permute-start | bytes 1572872 | tf_op jit(solution)/shard_map/ppermute | solution.py:37
  1.1 10.5 %collective-permute-start.1 = (bf16[256,512]{1,0:T(8,128)(2,1)S(1)}, bf16[256,512]{1,0:T(8,128)(2,1)S(1)}, u32[]{:S(2)}, u32[]{:S(2)}) collective-permute-start(bf16[256,512]{1,0:T(8,128)(2,1)S(1)} %get-tuple-element.47), channel_id=1, source_target_pairs={{0,2},{1,7},{2,0},{3,5},{4,6},{5,3},{6,4},{7,1},{8,10},{9,15},{10,... | collective-permute-start | bytes 786440 | tf_op jit(solution)/shard_map/ppermute | solution.py:33
  2.9 10.5 %collective-permute-start.2 = (bf16[256,512]{1,0:T(8,128)(2,1)S(1)}, bf16[256,512]{1,0:T(8,128)(2,1)S(1)}, u32[]{:S(2)}, u32[]{:S(2)}) collective-permute-start(bf16[256,512]{1,0:T(8,128)(2,1)S(1)} %get-tuple-element.48), channel_id=1, source_target_pairs={{0,6},{1,3},{2,4},{3,1},{4,2},{5,7},{6,0},{7,5},{8,14},{9,11},{10,... | collective-permute-start | bytes 786440 | tf_op jit(solution)/shard_map/ppermute | solution.py:33
  5.0 10.4 %collective-permute-start.3 = (bf16[256,512]{1,0:T(8,128)(2,1)S(1)}, bf16[256,512]{1,0:T(8,128)(2,1)S(1)}, u32[]{:S(2)}, u32[]{:S(2)}) collective-permute-start(bf16[256,512]{1,0:T(8,128)(2,1)S(1)} %get-tuple-element.48), channel_id=1, source_target_pairs={{0,2},{1,7},{2,0},{3,5},{4,6},{5,3},{6,4},{7,1},{8,10},{9,15},{10,... | collective-permute-start | bytes 786440 | tf_op jit(solution)/shard_map/ppermute | solution.py:33
  5.7 11.2 %collective-permute-start.4 = (bf16[256,512]{1,0:T(8,128)(2,1)S(1)}, bf16[256,512]{1,0:T(8,128)(2,1)S(1)}, u32[]{:S(2)}, u32[]{:S(2)}) collective-permute-start(bf16[256,512]{1,0:T(8,128)(2,1)S(1)} %get-tuple-element.47), channel_id=1, source_target_pairs={{0,6},{1,3},{2,4},{3,1},{4,2},{5,7},{6,0},{7,5},{8,14},{9,11},{10,... | collective-permute-start | bytes 786440 | tf_op jit(solution)/shard_map/ppermute | solution.py:33
  8.6 50.5 %collective-permute-start.22 = (bf16[512,1536]{1,0:T(8,128)(2,1)S(1)}, bf16[512,1536]{1,0:T(8,128)(2,1)S(1)}, u32[]{:S(2)}, u32[]{:S(2)}) collective-permute-start(bf16[512,1536]{1,0:T(8,128)(2,1)S(1)} %get-tuple-element.81), channel_id=1, source_target_pairs={{0,1},{1,0},{2,3},{3,2},{4,5},{5,4},{6,7},{7,6},{8,9},{9,8},{10,11... | collective-permute-start | bytes 4718600 | tf_op jit(solution)/shard_map/ppermute | solution.py:37
  13.3 9.3 %collective-permute-start.7 = (bf16[256,512]{1,0:T(8,128)(2,1)S(1)}, bf16[256,512]{1,0:T(8,128)(2,1)S(1)}, u32[]{:S(2)}, u32[]{:S(2)}) collective-permute-start(bf16[256,512]{1,0:T(8,128)(2,1)S(1)} %get-tuple-element.52.refs_0_), channel_id=1, source_target_pairs={{0,6},{1,3},{2,4},{3,1},{4,2},{5,7},{6,0},{7,5},{8,14},{9,11},{10,... | collective-permute-start | bytes 786440 | tf_op jit(solution)/shard_map/ppermute | solution.py:33
  15.5 7.1 %collective-permute-start.8 = (bf16[256,512]{1,0:T(8,128)(2,1)S(1)}, bf16[256,512]{1,0:T(8,128)(2,1)S(1)}, u32[]{:S(2)}, u32[]{:S(2)}) collective-permute-start(bf16[256,512]{1,0:T(8,128)(2,1)S(1)} %get-tuple-element.53.refs_3_), channel_id=1, source_target_pairs={{0,2},{1,7},{2,0},{3,5},{4,6},{5,3},{6,4},{7,1},{8,10},{9,15},{10,... | collective-permute-start | bytes 786440 | tf_op jit(solution)/shard_map/ppermute | solution.py:33
  17.0 6.7 %collective-permute-start.5 = (bf16[512,512]{1,0:T(8,128)(2,1)S(1)}, bf16[512,512]{1,0:T(8,128)(2,1)S(1)}, u32[]{:S(2)}, u32[]{:S(2)}) collective-permute-start(bf16[512,512]{1,0:T(8,128)(2,1)S(1)} %get-tuple-element.54.refs_0_.refs_2_), channel_id=1, source_target_pairs={{0,1},{1,0},{2,3},{3,2},{4,5},{5,4},{6,7},{7,6},{8,9},{9,8},{10,11... | collective-permute-start | bytes 1572872 | tf_op jit(solution)/shard_map/ppermute | solution.py:37
  17.1 6.8 %collective-permute-start.6 = (bf16[512,512]{1,0:T(8,128)(2,1)S(1)}, bf16[512,512]{1,0:T(8,128)(2,1)S(1)}, u32[]{:S(2)}, u32[]{:S(2)}) collective-permute-start(bf16[512,512]{1,0:T(8,128)(2,1)S(1)} %get-tuple-element.55.refs_1_.refs_3_), channel_id=1, source_target_pairs={{0,1},{1,0},{2,3},{3,2},{4,5},{5,4},{6,7},{7,6},{8,9},{9,8},{10,11... | collective-permute-start | bytes 1572872 | tf_op jit(solution)/shard_map/ppermute | solution.py:37
  23.7 30.8 %collective-permute-start.23 = (bf16[512,512]{1,0:T(8,128)(2,1)S(1)}, bf16[512,512]{1,0:T(8,128)(2,1)S(1)}, u32[]{:S(2)}, u32[]{:S(2)}) collective-permute-start(bf16[512,512]{1,0:T(8,128)(2,1)S(1)} %get-tuple-element.82), channel_id=1, source_target_pairs={{0,1},{1,0},{2,3},{3,2},{4,5},{5,4},{6,7},{7,6},{8,9},{9,8},{10,11... | collective-permute-start | bytes 1572872 | tf_op jit(solution)/shard_map/ppermute | solution.py:37
  25.9 7.1 %collective-permute-start.11 = (bf16[80,512]{1,0:T(8,128)(2,1)S(1)}, bf16[80,512]{1,0:T(8,128)(2,1)S(1)}, u32[]{:S(2)}, u32[]{:S(2)}) collective-permute-start(bf16[80,512]{1,0:T(8,128)(2,1)S(1)} %get-tuple-element.70), channel_id=1, source_target_pairs={{0,16},{1,17},{2,18},{3,19},{4,20},{5,21},{6,22},{7,23},{8,24},{9,... | collective-permute-start | bytes 245768 | tf_op jit(solution)/shard_map/ppermute | solution.py:50
  29.8 6.5 %collective-permute-start.12 = (bf16[80,512]{1,0:T(8,128)(2,1)S(1)}, bf16[80,512]{1,0:T(8,128)(2,1)S(1)}, u32[]{:S(2)}, u32[]{:S(2)}) collective-permute-start(bf16[80,512]{1,0:T(8,128)(2,1)S(1)} %get-tuple-element.71), channel_id=1, source_target_pairs={{0,24},{1,9},{2,26},{3,11},{4,28},{5,13},{6,30},{7,15},{8,16},{9,1... | collective-permute-start | bytes 245768 | tf_op jit(solution)/shard_map/ppermute | solution.py:50
  30.5 5.7 %collective-permute-start.13 = (bf16[80,512]{1,0:T(8,128)(2,1)S(1)}, bf16[80,512]{1,0:T(8,128)(2,1)S(1)}, u32[]{:S(2)}, u32[]{:S(2)}) collective-permute-start(bf16[80,512]{1,0:T(8,128)(2,1)S(1)} %get-tuple-element.72), channel_id=1, source_target_pairs={{0,8},{1,25},{2,10},{3,27},{4,12},{5,29},{6,14},{7,31},{8,0},{9,17... | collective-permute-start | bytes 245768 | tf_op jit(solution)/shard_map/ppermute | solution.py:50
  36.4 6.8 %collective-permute-start.14 = (bf16[80,512]{1,0:T(8,128)(2,1)S(1)}, bf16[80,512]{1,0:T(8,128)(2,1)S(1)}, u32[]{:S(2)}, u32[]{:S(2)}) collective-permute-start(bf16[80,512]{1,0:T(8,128)(2,1)S(1)} %line.1.refs_11_), channel_id=1, source_target_pairs={{0,64},{1,65},{2,66},{3,67},{4,68},{5,69},{6,70},{7,71},{8,72},{9,... | collective-permute-start | bytes 245768 | tf_op jit(solution)/shard_map/ppermute | solution.py:50
  39.5 5.7 %collective-permute-start.15 = (bf16[80,512]{1,0:T(8,128)(2,1)S(1)}, bf16[80,512]{1,0:T(8,128)(2,1)S(1)}, u32[]{:S(2)}, u32[]{:S(2)}) collective-permute-start(bf16[80,512]{1,0:T(8,128)(2,1)S(1)} %line.1.refs_11_), channel_id=1, source_target_pairs={{0,96},{1,33},{2,98},{3,35},{4,100},{5,37},{6,102},{7,39},{8,104},... | collective-permute-start | bytes 245768 | tf_op jit(solution)/shard_map/ppermute | solution.py:50
  45.5 6.1 %collective-permute-start.17 = (bf16[64,512]{1,0:T(8,128)(2,1)S(1)}, bf16[64,512]{1,0:T(8,128)(2,1)S(1)}, u32[]{:S(2)}, u32[]{:S(2)}) collective-permute-start(bf16[64,512]{1,0:T(8,128)(2,1)S(1)} %get-tuple-element.75), channel_id=1, source_target_pairs={{0,16},{1,17},{2,18},{3,19},{4,20},{5,21},{6,22},{7,23},{8,24},{9,... | collective-permute-start | bytes 196616 | tf_op jit(solution)/shard_map/ppermute | solution.py:50
  47.4 5.6 %collective-permute-start.18 = (bf16[64,512]{1,0:T(8,128)(2,1)S(1)}, bf16[64,512]{1,0:T(8,128)(2,1)S(1)}, u32[]{:S(2)}, u32[]{:S(2)}) collective-permute-start(bf16[64,512]{1,0:T(8,128)(2,1)S(1)} %get-tuple-element.76), channel_id=1, source_target_pairs={{0,24},{1,9},{2,26},{3,11},{4,28},{5,13},{6,30},{7,15},{8,16},{9,1... | collective-permute-start | bytes 196616 | tf_op jit(solution)/shard_map/ppermute | solution.py:50
  56.1 7.2 %collective-permute-start.28 = (bf16[256,512]{1,0:T(8,128)(2,1)S(1)}, bf16[256,512]{1,0:T(8,128)(2,1)S(1)}, u32[]{:S(2)}, u32[]{:S(2)}) collective-permute-start(bf16[256,512]{1,0:T(8,128)(2,1)S(1)} %far1.1.refs_7_), channel_id=1, source_target_pairs={{0,2},{1,7},{2,0},{3,5},{4,6},{5,3},{6,4},{7,1},{8,10},{9,15},{10,... | collective-permute-start | bytes 786440 | tf_op jit(solution)/shard_map/ppermute | solution.py:33
  56.7 11.5 %collective-permute-start.26 = (bf16[256,512]{1,0:T(8,128)(2,1)S(1)}, bf16[256,512]{1,0:T(8,128)(2,1)S(1)}, u32[]{:S(2)}, u32[]{:S(2)}) collective-permute-start(bf16[256,512]{1,0:T(8,128)(2,1)S(1)} %far0.1.refs_4_.refs_6_), channel_id=1, source_target_pairs={{0,6},{1,3},{2,4},{3,1},{4,2},{5,7},{6,0},{7,5},{8,14},{9,11},{10,... | collective-permute-start | bytes 786440 | tf_op jit(solution)/shard_map/ppermute | solution.py:33
  60.3 11.4 %collective-permute-start.24 = (bf16[256,512]{1,0:T(8,128)(2,1)S(1)}, bf16[256,512]{1,0:T(8,128)(2,1)S(1)}, u32[]{:S(2)}, u32[]{:S(2)}) collective-permute-start(bf16[256,512]{1,0:T(8,128)(2,1)S(1)} %get-tuple-element.83), channel_id=1, source_target_pairs={{0,6},{1,3},{2,4},{3,1},{4,2},{5,7},{6,0},{7,5},{8,14},{9,11},{10,... | collective-permute-start | bytes 786440 | tf_op jit(solution)/shard_map/ppermute | solution.py:33
  61.3 10.4 %collective-permute-start.25 = (bf16[256,512]{1,0:T(8,128)(2,1)S(1)}, bf16[256,512]{1,0:T(8,128)(2,1)S(1)}, u32[]{:S(2)}, u32[]{:S(2)}) collective-permute-start(bf16[256,512]{1,0:T(8,128)(2,1)S(1)} %get-tuple-element.84), channel_id=1, source_target_pairs={{0,2},{1,7},{2,0},{3,5},{4,6},{5,3},{6,4},{7,1},{8,10},{9,15},{10,... | collective-permute-start | bytes 786440 | tf_op jit(solution)/shard_map/ppermute | solution.py:33
  63.3 13.8 %collective-permute-start.29 = (bf16[256,512]{1,0:T(8,128)(2,1)S(1)}, bf16[256,512]{1,0:T(8,128)(2,1)S(1)}, u32[]{:S(2)}, u32[]{:S(2)}) collective-permute-start(bf16[256,512]{1,0:T(8,128)(2,1)S(1)} %add_convert_fusion), channel_id=1, source_target_pairs={{0,6},{1,3},{2,4},{3,1},{4,2},{5,7},{6,0},{7,5},{8,14},{9,11},{10,... | collective-permute-start | bytes 786440 | tf_op jit(solution)/shard_map/ppermute | solution.py:33
  68.3 8.8 %collective-permute-start.27 = (bf16[256,512]{1,0:T(8,128)(2,1)S(1)}, bf16[256,512]{1,0:T(8,128)(2,1)S(1)}, u32[]{:S(2)}, u32[]{:S(2)}) collective-permute-start(bf16[256,512]{1,0:T(8,128)(2,1)S(1)} %add_convert_fusion.1), channel_id=1, source_target_pairs={{0,2},{1,7},{2,0},{3,5},{4,6},{5,3},{6,4},{7,1},{8,10},{9,15},{10,... | collective-permute-start | bytes 786440 | tf_op jit(solution)/shard_map/ppermute | solution.py:33
  (14 other events, 61.2 us)

commit v5 on v4

--- a/solution.py
+++ b/solution.py
@@ -22,11 +22,14 @@
 
 
 def turn(k, core):
-    return k ^ (2 * core) if k % 2 else k
-
-
-def meet(k, core):
-    return turn((0, 2, 3, 1)[k], core)
+    return k ^ (2 * (1 - core)) if k % 2 else k
+
+
+def meet(k, core, order):
+    return turn(order[k], core)
+
+
+Z_ORDER, X_ORDER = (0, 2, 1, 3), (0, 2, 1, 3)
 
 
 def y_flip(value, k):
@@ -46,7 +49,7 @@
 
 
 def ctx_flip(value, k, unit):
-    pairs = [(8 * i + j, 8 * (i ^ (unit * meet(k, j % 2))) + j) for i in range(16) for j in range(8)]
+    pairs = [(8 * i + j, 8 * (i ^ (unit * meet(k, j % 2, Z_ORDER if unit == 1 else X_ORDER))) + j) for i in range(16) for j in range(8)]
     return lax.ppermute(value, ("ctx", "tp"), pairs)
 
 
@@ -159,7 +162,7 @@
     high = total.astype(BF)
     rest = (total - high.astype(F32)).astype(BF)
     for i, ref in enumerate((mine, m1, m2, m3)):
-        piece = state[pl.ds(pl.multiple_of((z ^ meet(i, my("core"))) * CUT, CUT), CUT), :]
+        piece = state[pl.ds(pl.multiple_of((z ^ meet(i, my("core"), Z_ORDER)) * CUT, CUT), CUT), :]
         if i == 0:
             ref[...] = piece
         else:
@@ -193,7 +196,7 @@
     z = my("z")
     pieces = [mine[...]] + [piece for piece, _ in opened]
     factors = [factor[...]] + [f for _, f in opened]
-    return pieces, factors, [z ^ meet(k, my("core")) for k in range(SIDE)]
+    return pieces, factors, [z ^ meet(k, my("core"), Z_ORDER) for k in range(SIDE)]
 
 
 def line_body(mine, factor, m1, m2, m3, out):
@@ -211,9 +214,9 @@
     pieces, factors, sources = line_of(mine, factor, (m1, m2, m3))
     x, z = my("x"), my("z")
     opened = [open_message(n) for n in (n1, n2, n3)]
-    entry = prefix([p for p, _ in opened], [f for _, f in opened], [x ^ meet(k, my("core")) for k in range(1, SIDE)], x)
+    entry = prefix([p for p, _ in opened], [f for _, f in opened], [x ^ meet(k, my("core"), X_ORDER) for k in range(1, SIDE)], x)
     for k, ref in enumerate((e0, e1, e2, e3)):
-        target = z ^ meet(k, my("core"))
+        target = z ^ meet(k, my("core"), Z_ORDER)
         whole = prefix(pieces, factors, sources, target) + between(factors, sources, -1, target) * entry
         ref[...] = whole.astype(BF)
 
@@ -243,7 +246,7 @@
     z = my("z")
     rows = pl.ds(half * HALF, HALF)
     for k, ref in enumerate((e0, e1, e2, e3)):
-        whole[pl.ds(pl.multiple_of((z ^ meet(k, my("core"))) * CUT, CUT), CUT), :] = ref[...]
+        whole[pl.ds(pl.multiple_of((z ^ meet(k, my("core"), Z_ORDER)) * CUT, CUT), CUT), :] = ref[...]
     retained = local[rows, :] + decay[rows, :] * dot(queries[rows, :], whole[...])
     center = retained - jnp.mean(retained, axis=-1, keepdims=True)
     variance = jnp.mean(center * center, axis=-1, keepdims=True)
@@ -302,6 +305,15 @@
         moved=4 * DV * width,
         after=after,
     )
+
+
+def mine_body(h0, h1, weight, out):
+    for i, h in enumerate((h0, h1)):
+        out[i * HALF: (i + 1) * HALF, :] = dot(h[...], weight[...])
+
+
+def far_body(half, mine, other, weight, out):
+    out[...] = (mine[pl.ds(half * HALF, HALF), :] + dot(other[...], weight[...])).astype(BF)
 
 
 def own_body(h0, h1, o0, o1, mine, theirs, top, low, out_top, out_low):
@@ -398,8 +410,14 @@
         )
         hidden.append(part)
         other.append(tp_swap(part))
+    (mine,) = call(
+        mine_body, [((ROWS, DV), F32)], [VM] * 3, [*hidden, kept_far], "far_mine", flops=2 * ROWS * DV * DV, moved=2 * DV * DV
+    )
     for half in range(2):
-        far += partial(hidden[half: half + 1], other[half: half + 1], kept_far, theirs_far, (BF,), f"far{half}", after=far)
+        far += call(
+            functools.partial(far_body, half), [((HALF, DV), BF)], [VM] * 3, [mine, other[half], theirs_far], f"far{half}",
+            flops=2 * HALF * DV * DV, moved=2 * DV * DV, after=far,
+        )
     via3, via1 = y_flip(far[0], 3), y_flip(far[1], 1)
     top1, low1, top3, low3 = partial(hidden, other, kept, theirs, (F32, BF, BF, F32), "beside", after=far)
     from1_low, from3_top = y_flip(low1, 1), y_flip(top3, 3)

time: 79.1 us -> 78.5 us (level); the launches traced: 78.1 us -> 78.3 us
  waiting for transfers between devices: 26.5 us -> 28.8 us
  starting transfers between devices: 31.8 us -> 29.6 us
    ppermute x12, waiting for transfers between devices: 16.5 us -> 19.1 us  [y_flip(): lax.ppermute(value, 'tp', [(i, i ^ 2 * turn(k, i % 2)) for i in range(8)])]
    ppermute x12, starting transfers between devices: 16.9 us -> 14.6 us  [y_flip(): lax.ppermute(value, 'tp', [(i, i ^ 2 * turn(k, i % 2)) for i in range(8)])]
    pallas_call x21 -> x22, Pallas kernels: 16.6 us -> 16.7 us  [call(): pl.pallas_call(whole, out_shape=shapes, in_specs=list(in_specs) + [ANY] *...]
  transfers between devices with their start and end apart: 30 -> 30, of which waited for: 13 -> 17; matrix products, arithmetic and copies ran while one was open for 0% -> 0% of each run, Pallas kernels for 20% -> 20%
where the time goes in v5:
time: 78.5 us; the launch traced here: 78.3 us
  starting transfers between devices  29.6 us (38%)
  waiting for transfers between devices  28.8 us (37%)
  Pallas kernels  16.7 us (21%)
  local copies, waits for them, and re-layouts  2.66 us (3%)
    ppermute x12, waiting for transfers between devices, y_flip(): lax.ppermute(value, 'tp', [(i, i ^ 2 * turn(k, i % 2)) for i in range(8)])  19.1 us
    pallas_call x22, Pallas kernels, call(): pl.pallas_call(whole, out_shape=shapes, in_specs=list(in_specs) + [ANY] *...  16.7 us
    ppermute x12, starting transfers between devices, y_flip(): lax.ppermute(value, 'tp', [(i, i ^ 2 * turn(k, i % 2)) for i in range(8)])  14.6 us
    ppermute x9, starting transfers between devices, ctx_flip(): return lax.ppermute(value, ('ctx', 'tp'), pairs)  13.1 us
    ppermute x9, waiting for transfers between devices, ctx_flip(): return lax.ppermute(value, ('ctx', 'tp'), pairs)  9.3 us
    unnamed x16, local copies, waits for them, and re-layouts  2.66 us
    ppermute x9, starting transfers between devices, tp_swap(): return lax.ppermute(value, 'tp', [(i, i ^ 1) for i in range(8)])  1.94 us
  transfers between devices with their start and end apart: 30, of which 17 were waited for; matrix products, arithmetic and copies ran while one was open for 0% of the time, Pallas kernels for 20%

profile of v5, /device:TPU:0, one launch (start us, length us, event | category | flops | bytes accessed | tf_op | source)
XLA Modules:
  0.0 78.3 jit_solution(7462620484266778761)
XLA Ops:
  1.1 3.2 %collective-permute-start.1 = (bf16[256,512]{1,0:T(8,128)(2,1)S(1)}, bf16[256,512]{1,0:T(8,128)(2,1)S(1)}, u32[]{:S(2)}, u32[]{:S(2)}) collective-permute-start(bf16[256,512]{1,0:T(8,128)(2,1)S(1)} %get-tuple-element.47), channel_id=1, source_target_pairs={{0,6},{1,3},{2,4},{3,1},{4,2},{5,7},{6,0},{7,5},{8,14},{9,11},{10,... | collective-permute-start | bytes 786440 | tf_op jit(solution)/shard_map/ppermute | solution.py:36
  6.3 2.2 %pick.1 = (bf16[512,512]{1,0:T(8,128)(2,1)S(1)}, bf16[512,1536]{1,0:T(8,128)(2,1)S(1)}, bf16[512,512]{1,0:T(8,128)(2,1)S(1)}, bf16[512,1536]{1,0:T(8,128)(2,1)S(1)}) custom-call(bf16[512,4096]{1,0:T(8,128)(2,1)} %refs_0_.7), custom_call_target="tpu_custom_call" | custom-call | bytes 1 | tf_op jit(solution)/shard_map/pick/pallas_call | solution.py:76
  9.1 1.6 %copy-done.1 = bf16[4096,256]{1,0:T(8,128)(2,1)S(1)} copy-done((bf16[4096,256]{1,0:T(8,128)(2,1)S(1)}, bf16[4096,256]{1,0:T(8,128)(2,1)}, u32[]{:S(2)}) %copy-start.1) | copy-done | bytes 2097176
  11.7 1.5 %collective-permute-done.2.refs_1_ = bf16[256,512]{1,0:T(8,128)(2,1)S(1)} collective-permute-done((bf16[256,512]{1,0:T(8,128)(2,1)S(1)}, bf16[256,512]{1,0:T(8,128)(2,1)S(1)}, u32[]{:S(2)}, u32[]{:S(2)}) %collective-permute-start.2) | collective-permute-done | bytes 262176 | tf_op jit(solution)/shard_map/ppermute | solution.py:36
  13.7 1.5 %collective-permute-start.8 = (bf16[256,512]{1,0:T(8,128)(2,1)S(1)}, bf16[256,512]{1,0:T(8,128)(2,1)S(1)}, u32[]{:S(2)}, u32[]{:S(2)}) collective-permute-start(bf16[256,512]{1,0:T(8,128)(2,1)S(1)} %get-tuple-element.53.refs_3_), channel_id=1, source_target_pairs={{0,6},{1,3},{2,4},{3,1},{4,2},{5,7},{6,0},{7,5},{8,14},{9,11},{10,... | collective-permute-start | bytes 786440 | tf_op jit(solution)/shard_map/ppermute | solution.py:36
  15.1 1.5 %collective-permute-done.3.refs_1_ = bf16[256,512]{1,0:T(8,128)(2,1)S(1)} collective-permute-done((bf16[256,512]{1,0:T(8,128)(2,1)S(1)}, bf16[256,512]{1,0:T(8,128)(2,1)S(1)}, u32[]{:S(2)}, u32[]{:S(2)}) %collective-permute-start.3) | collective-permute-done | bytes 262176 | tf_op jit(solution)/shard_map/ppermute | solution.py:36
  18.3 3.7 %collective-permute-done.7.refs_0_ = bf16[256,512]{1,0:T(8,128)(2,1)S(1)} collective-permute-done((bf16[256,512]{1,0:T(8,128)(2,1)S(1)}, bf16[256,512]{1,0:T(8,128)(2,1)S(1)}, u32[]{:S(2)}, u32[]{:S(2)}) %collective-permute-start.7) | collective-permute-done | bytes 262176 | tf_op jit(solution)/shard_map/ppermute | solution.py:36
  26.1 4.0 %collective-permute-start.11 = (bf16[80,512]{1,0:T(8,128)(2,1)S(1)}, bf16[80,512]{1,0:T(8,128)(2,1)S(1)}, u32[]{:S(2)}, u32[]{:S(2)}) collective-permute-start(bf16[80,512]{1,0:T(8,128)(2,1)S(1)} %get-tuple-element.70), channel_id=1, source_target_pairs={{0,16},{1,17},{2,18},{3,19},{4,20},{5,21},{6,22},{7,23},{8,24},{9,... | collective-permute-start | bytes 245768 | tf_op jit(solution)/shard_map/ppermute | solution.py:53
  31.1 1.2 %queries.1.refs_5_.refs_0_ = f32[512,256]{1,0:T(8,128)S(1)} custom-call(bf16[512,512]{1,0:T(8,128)(2,1)S(1)} %copy-done.4, bf16[512,512]{1,0:T(8,128)(2,1)S(1)} %collective-permute-done.refs_1_, bf16[512,512]{1,0:T(8,128)(2,1)S(1)} %get-tuple-element.54.refs_0_.refs_2_, bf16[512,512]{1,0:T(8,128)(2,1)S(1)} %get-tuple-element.55.refs_1_.refs_3_, ...), custom_call_target="tpu_custom_call" | custom-call | flops 1073741824 | bytes 2097153 | tf_op jit(solution)/shard_map/queries/pallas_call | solution.py:76
  33.3 3.3 %collective-permute-done.12.refs_3_ = bf16[80,512]{1,0:T(8,128)(2,1)S(1)} collective-permute-done((bf16[80,512]{1,0:T(8,128)(2,1)S(1)}, bf16[80,512]{1,0:T(8,128)(2,1)S(1)}, u32[]{:S(2)}, u32[]{:S(2)}) %collective-permute-start.12) | collective-permute-done | bytes 81952 | tf_op jit(solution)/shard_map/ppermute | solution.py:53
  36.7 3.1 %collective-permute-start.14 = (bf16[80,512]{1,0:T(8,128)(2,1)S(1)}, bf16[80,512]{1,0:T(8,128)(2,1)S(1)}, u32[]{:S(2)}, u32[]{:S(2)}) collective-permute-start(bf16[80,512]{1,0:T(8,128)(2,1)S(1)} %line.1.refs_11_), channel_id=1, source_target_pairs={{0,64},{1,65},{2,66},{3,67},{4,68},{5,69},{6,70},{7,71},{8,72},{9,... | collective-permute-start | bytes 245768 | tf_op jit(solution)/shard_map/ppermute | solution.py:53
  39.8 1.1 %collective-permute-start.15 = (bf16[80,512]{1,0:T(8,128)(2,1)S(1)}, bf16[80,512]{1,0:T(8,128)(2,1)S(1)}, u32[]{:S(2)}, u32[]{:S(2)}) collective-permute-start(bf16[80,512]{1,0:T(8,128)(2,1)S(1)} %line.1.refs_11_), channel_id=1, source_target_pairs={{0,96},{1,33},{2,98},{3,35},{4,100},{5,37},{6,102},{7,39},{8,104},... | collective-permute-start | bytes 245768 | tf_op jit(solution)/shard_map/ppermute | solution.py:53
  41.0 2.5 %gates.1.refs_8_.refs_7_ = f32[512,512]{1,0:T(8,128)S(1)} custom-call(bf16[512,512]{1,0:T(8,128)(2,1)S(1)} %copy-done.4, bf16[512,512]{1,0:T(8,128)(2,1)S(1)} %collective-permute-done.refs_1_, bf16[512,512]{1,0:T(8,128)(2,1)S(1)} %get-tuple-element.54.refs_0_.refs_2_, bf16[512,512]{1,0:T(8,128)(2,1)S(1)} %get-tuple-element.55.refs_1_.refs_3_, ...), custom_call_target="tpu_custom_call" | custom-call | flops 2147483648 | bytes 4194305 | tf_op jit(solution)/shard_map/gates/pallas_call | solution.py:76
  43.5 2.0 %collective-permute-done.15.refs_6_ = bf16[80,512]{1,0:T(8,128)(2,1)S(1)} collective-permute-done((bf16[80,512]{1,0:T(8,128)(2,1)S(1)}, bf16[80,512]{1,0:T(8,128)(2,1)S(1)}, u32[]{:S(2)}, u32[]{:S(2)}) %collective-permute-start.15) | collective-permute-done | bytes 81952 | tf_op jit(solution)/shard_map/ppermute | solution.py:53
  45.8 1.9 %collective-permute-start.17 = (bf16[64,512]{1,0:T(8,128)(2,1)S(1)}, bf16[64,512]{1,0:T(8,128)(2,1)S(1)}, u32[]{:S(2)}, u32[]{:S(2)}) collective-permute-start(bf16[64,512]{1,0:T(8,128)(2,1)S(1)} %get-tuple-element.75), channel_id=1, source_target_pairs={{0,16},{1,17},{2,18},{3,19},{4,20},{5,21},{6,22},{7,23},{8,24},{9,... | collective-permute-start | bytes 196616 | tf_op jit(solution)/shard_map/ppermute | solution.py:53
  50.2 1.7 %collective-permute-done.17.refs_2_ = bf16[64,512]{1,0:T(8,128)(2,1)S(1)} collective-permute-done((bf16[64,512]{1,0:T(8,128)(2,1)S(1)}, bf16[64,512]{1,0:T(8,128)(2,1)S(1)}, u32[]{:S(2)}, u32[]{:S(2)}) %collective-permute-start.17) | collective-permute-done | bytes 65568 | tf_op jit(solution)/shard_map/ppermute | solution.py:53
  51.9 1.3 %collective-permute-done.18.refs_3_ = bf16[64,512]{1,0:T(8,128)(2,1)S(1)} collective-permute-done((bf16[64,512]{1,0:T(8,128)(2,1)S(1)}, bf16[64,512]{1,0:T(8,128)(2,1)S(1)}, u32[]{:S(2)}, u32[]{:S(2)}) %collective-permute-start.18) | collective-permute-done | bytes 65568 | tf_op jit(solution)/shard_map/ppermute | solution.py:53
  56.2 3.0 %collective-permute-start.28 = (bf16[256,512]{1,0:T(8,128)(2,1)S(1)}, bf16[256,512]{1,0:T(8,128)(2,1)S(1)}, u32[]{:S(2)}, u32[]{:S(2)}) collective-permute-start(bf16[256,512]{1,0:T(8,128)(2,1)S(1)} %far1.1.refs_7_), channel_id=1, source_target_pairs={{0,6},{1,3},{2,4},{3,1},{4,2},{5,7},{6,0},{7,5},{8,14},{9,11},{10,... | collective-permute-start | bytes 786440 | tf_op jit(solution)/shard_map/ppermute | solution.py:36
  59.3 1.2 %beside.1 = (f32[256,512]{1,0:T(8,128)S(1)}, bf16[256,512]{1,0:T(8,128)(2,1)S(1)}, bf16[256,512]{1,0:T(8,128)(2,1)S(1)}, f32[256,512]{1,0:T(8,128)S(1)}) custom-call(bf16[256,512]{1,0:T(8,128)(2,1)S(1)} %hidden0.1.refs_8_.refs_0_, bf16[256,512]{1,0:T(8,128)(2,1)S(1)} %hidden1.1.refs_1_, bf16[256,512]{1,0:T(8,128)(2,1)S(1)} %collective-permute-done.20.refs_1_.refs_2_, ...), custom_call_target="tpu_custom_call" | custom-call | flops 1073741824 | bytes 2097152 | tf_op jit(solution)/shard_map/beside/pallas_call | solution.py:76
  60.5 2.1 %collective-permute-start.24 = (bf16[256,512]{1,0:T(8,128)(2,1)S(1)}, bf16[256,512]{1,0:T(8,128)(2,1)S(1)}, u32[]{:S(2)}, u32[]{:S(2)}) collective-permute-start(bf16[256,512]{1,0:T(8,128)(2,1)S(1)} %get-tuple-element.83), channel_id=1, source_target_pairs={{0,2},{1,7},{2,0},{3,5},{4,6},{5,3},{6,4},{7,1},{8,10},{9,15},{10,... | collective-permute-start | bytes 786440 | tf_op jit(solution)/shard_map/ppermute | solution.py:36
  62.9 3.7 %collective-permute-done.28 = bf16[256,512]{1,0:T(8,128)(2,1)S(1)} collective-permute-done((bf16[256,512]{1,0:T(8,128)(2,1)S(1)}, bf16[256,512]{1,0:T(8,128)(2,1)S(1)}, u32[]{:S(2)}, u32[]{:S(2)}) %collective-permute-start.28) | collective-permute-done | bytes 262176 | tf_op jit(solution)/shard_map/ppermute | solution.py:36
  67.9 2.0 %collective-permute-start.27 = (bf16[256,512]{1,0:T(8,128)(2,1)S(1)}, bf16[256,512]{1,0:T(8,128)(2,1)S(1)}, u32[]{:S(2)}, u32[]{:S(2)}) collective-permute-start(bf16[256,512]{1,0:T(8,128)(2,1)S(1)} %add_convert_fusion.1), channel_id=1, source_target_pairs={{0,6},{1,3},{2,4},{3,1},{4,2},{5,7},{6,0},{7,5},{8,14},{9,11},{10,... | collective-permute-start | bytes 786440 | tf_op jit(solution)/shard_map/ppermute | solution.py:36
  69.9 2.8 %collective-permute-done.24.refs_6_ = bf16[256,512]{1,0:T(8,128)(2,1)S(1)} collective-permute-done((bf16[256,512]{1,0:T(8,128)(2,1)S(1)}, bf16[256,512]{1,0:T(8,128)(2,1)S(1)}, u32[]{:S(2)}, u32[]{:S(2)}) %collective-permute-start.24) | collective-permute-done | bytes 262176 | tf_op jit(solution)/shard_map/ppermute | solution.py:36
  73.8 3.1 %collective-permute-done.29.refs_3_ = bf16[256,512]{1,0:T(8,128)(2,1)S(1)} collective-permute-done((bf16[256,512]{1,0:T(8,128)(2,1)S(1)}, bf16[256,512]{1,0:T(8,128)(2,1)S(1)}, u32[]{:S(2)}, u32[]{:S(2)}) %collective-permute-start.29) | collective-permute-done | bytes 262176 | tf_op jit(solution)/shard_map/ppermute | solution.py:36
  (78 shorter events, 22.5 us)
Async XLA Ops:
  0.0 8.6 %collective-permute-start = (bf16[512,512]{1,0:T(8,128)(2,1)}, bf16[512,512]{1,0:T(8,128)(2,1)S(1)}, u32[]{:S(2)}, u32[]{:S(2)}) collective-permute-start(bf16[512,512]{1,0:T(8,128)(2,1)} %refs_0_.11), channel_id=1, source_target_pairs={{0,1},{1,0},{2,3},{3,2},{4,5},{5,4},{6,7},{7,6},{8,9},{9,8},{10,11... | collective-permute-start | bytes 1572872 | tf_op jit(solution)/shard_map/ppermute | solution.py:40
  1.1 10.5 %collective-permute-start.1 = (bf16[256,512]{1,0:T(8,128)(2,1)S(1)}, bf16[256,512]{1,0:T(8,128)(2,1)S(1)}, u32[]{:S(2)}, u32[]{:S(2)}) collective-permute-start(bf16[256,512]{1,0:T(8,128)(2,1)S(1)} %get-tuple-element.47), channel_id=1, source_target_pairs={{0,6},{1,3},{2,4},{3,1},{4,2},{5,7},{6,0},{7,5},{8,14},{9,11},{10,... | collective-permute-start | bytes 786440 | tf_op jit(solution)/shard_map/ppermute | solution.py:36
  4.3 8.9 %collective-permute-start.2 = (bf16[256,512]{1,0:T(8,128)(2,1)S(1)}, bf16[256,512]{1,0:T(8,128)(2,1)S(1)}, u32[]{:S(2)}, u32[]{:S(2)}) collective-permute-start(bf16[256,512]{1,0:T(8,128)(2,1)S(1)} %get-tuple-element.48), channel_id=1, source_target_pairs={{0,2},{1,7},{2,0},{3,5},{4,6},{5,3},{6,4},{7,1},{8,10},{9,15},{10,... | collective-permute-start | bytes 786440 | tf_op jit(solution)/shard_map/ppermute | solution.py:36
  4.4 12.2 %collective-permute-start.3 = (bf16[256,512]{1,0:T(8,128)(2,1)S(1)}, bf16[256,512]{1,0:T(8,128)(2,1)S(1)}, u32[]{:S(2)}, u32[]{:S(2)}) collective-permute-start(bf16[256,512]{1,0:T(8,128)(2,1)S(1)} %get-tuple-element.48), channel_id=1, source_target_pairs={{0,6},{1,3},{2,4},{3,1},{4,2},{5,7},{6,0},{7,5},{8,14},{9,11},{10,... | collective-permute-start | bytes 786440 | tf_op jit(solution)/shard_map/ppermute | solution.py:36
  5.5 11.1 %collective-permute-start.4 = (bf16[256,512]{1,0:T(8,128)(2,1)S(1)}, bf16[256,512]{1,0:T(8,128)(2,1)S(1)}, u32[]{:S(2)}, u32[]{:S(2)}) collective-permute-start(bf16[256,512]{1,0:T(8,128)(2,1)S(1)} %get-tuple-element.47), channel_id=1, source_target_pairs={{0,2},{1,7},{2,0},{3,5},{4,6},{5,3},{6,4},{7,1},{8,10},{9,15},{10,... | collective-permute-start | bytes 786440 | tf_op jit(solution)/shard_map/ppermute | solution.py:36
  8.6 50.7 %collective-permute-start.22 = (bf16[512,1536]{1,0:T(8,128)(2,1)S(1)}, bf16[512,1536]{1,0:T(8,128)(2,1)S(1)}, u32[]{:S(2)}, u32[]{:S(2)}) collective-permute-start(bf16[512,1536]{1,0:T(8,128)(2,1)S(1)} %get-tuple-element.81), channel_id=1, source_target_pairs={{0,1},{1,0},{2,3},{3,2},{4,5},{5,4},{6,7},{7,6},{8,9},{9,8},{10,11... | collective-permute-start | bytes 4718600 | tf_op jit(solution)/shard_map/ppermute | solution.py:40
  13.2 8.8 %collective-permute-start.7 = (bf16[256,512]{1,0:T(8,128)(2,1)S(1)}, bf16[256,512]{1,0:T(8,128)(2,1)S(1)}, u32[]{:S(2)}, u32[]{:S(2)}) collective-permute-start(bf16[256,512]{1,0:T(8,128)(2,1)S(1)} %get-tuple-element.52.refs_0_), channel_id=1, source_target_pairs={{0,2},{1,7},{2,0},{3,5},{4,6},{5,3},{6,4},{7,1},{8,10},{9,15},{10,... | collective-permute-start | bytes 786440 | tf_op jit(solution)/shard_map/ppermute | solution.py:36
  13.7 9.1 %collective-permute-start.8 = (bf16[256,512]{1,0:T(8,128)(2,1)S(1)}, bf16[256,512]{1,0:T(8,128)(2,1)S(1)}, u32[]{:S(2)}, u32[]{:S(2)}) collective-permute-start(bf16[256,512]{1,0:T(8,128)(2,1)S(1)} %get-tuple-element.53.refs_3_), channel_id=1, source_target_pairs={{0,6},{1,3},{2,4},{3,1},{4,2},{5,7},{6,0},{7,5},{8,14},{9,11},{10,... | collective-permute-start | bytes 786440 | tf_op jit(solution)/shard_map/ppermute | solution.py:36
  16.7 7.2 %collective-permute-start.5 = (bf16[512,512]{1,0:T(8,128)(2,1)S(1)}, bf16[512,512]{1,0:T(8,128)(2,1)S(1)}, u32[]{:S(2)}, u32[]{:S(2)}) collective-permute-start(bf16[512,512]{1,0:T(8,128)(2,1)S(1)} %get-tuple-element.54.refs_0_.refs_2_), channel_id=1, source_target_pairs={{0,1},{1,0},{2,3},{3,2},{4,5},{5,4},{6,7},{7,6},{8,9},{9,8},{10,11... | collective-permute-start | bytes 1572872 | tf_op jit(solution)/shard_map/ppermute | solution.py:40
  17.2 6.8 %collective-permute-start.6 = (bf16[512,512]{1,0:T(8,128)(2,1)S(1)}, bf16[512,512]{1,0:T(8,128)(2,1)S(1)}, u32[]{:S(2)}, u32[]{:S(2)}) collective-permute-start(bf16[512,512]{1,0:T(8,128)(2,1)S(1)} %get-tuple-element.55.refs_1_.refs_3_), channel_id=1, source_target_pairs={{0,1},{1,0},{2,3},{3,2},{4,5},{5,4},{6,7},{7,6},{8,9},{9,8},{10,11... | collective-permute-start | bytes 1572872 | tf_op jit(solution)/shard_map/ppermute | solution.py:40
  23.9 31.3 %collective-permute-start.23 = (bf16[512,512]{1,0:T(8,128)(2,1)S(1)}, bf16[512,512]{1,0:T(8,128)(2,1)S(1)}, u32[]{:S(2)}, u32[]{:S(2)}) collective-permute-start(bf16[512,512]{1,0:T(8,128)(2,1)S(1)} %get-tuple-element.82), channel_id=1, source_target_pairs={{0,1},{1,0},{2,3},{3,2},{4,5},{5,4},{6,7},{7,6},{8,9},{9,8},{10,11... | collective-permute-start | bytes 1572872 | tf_op jit(solution)/shard_map/ppermute | solution.py:40
  26.1 7.2 %collective-permute-start.11 = (bf16[80,512]{1,0:T(8,128)(2,1)S(1)}, bf16[80,512]{1,0:T(8,128)(2,1)S(1)}, u32[]{:S(2)}, u32[]{:S(2)}) collective-permute-start(bf16[80,512]{1,0:T(8,128)(2,1)S(1)} %get-tuple-element.70), channel_id=1, source_target_pairs={{0,16},{1,17},{2,18},{3,19},{4,20},{5,21},{6,22},{7,23},{8,24},{9,... | collective-permute-start | bytes 245768 | tf_op jit(solution)/shard_map/ppermute | solution.py:53
  30.1 6.5 %collective-permute-start.12 = (bf16[80,512]{1,0:T(8,128)(2,1)S(1)}, bf16[80,512]{1,0:T(8,128)(2,1)S(1)}, u32[]{:S(2)}, u32[]{:S(2)}) collective-permute-start(bf16[80,512]{1,0:T(8,128)(2,1)S(1)} %get-tuple-element.71), channel_id=1, source_target_pairs={{0,24},{1,9},{2,26},{3,11},{4,28},{5,13},{6,30},{7,15},{8,16},{9,1... | collective-permute-start | bytes 245768 | tf_op jit(solution)/shard_map/ppermute | solution.py:53
  30.8 5.8 %collective-permute-start.13 = (bf16[80,512]{1,0:T(8,128)(2,1)S(1)}, bf16[80,512]{1,0:T(8,128)(2,1)S(1)}, u32[]{:S(2)}, u32[]{:S(2)}) collective-permute-start(bf16[80,512]{1,0:T(8,128)(2,1)S(1)} %get-tuple-element.72), channel_id=1, source_target_pairs={{0,8},{1,25},{2,10},{3,27},{4,12},{5,29},{6,14},{7,31},{8,0},{9,17... | collective-permute-start | bytes 245768 | tf_op jit(solution)/shard_map/ppermute | solution.py:53
  36.7 6.7 %collective-permute-start.14 = (bf16[80,512]{1,0:T(8,128)(2,1)S(1)}, bf16[80,512]{1,0:T(8,128)(2,1)S(1)}, u32[]{:S(2)}, u32[]{:S(2)}) collective-permute-start(bf16[80,512]{1,0:T(8,128)(2,1)S(1)} %line.1.refs_11_), channel_id=1, source_target_pairs={{0,64},{1,65},{2,66},{3,67},{4,68},{5,69},{6,70},{7,71},{8,72},{9,... | collective-permute-start | bytes 245768 | tf_op jit(solution)/shard_map/ppermute | solution.py:53
  39.8 5.7 %collective-permute-start.15 = (bf16[80,512]{1,0:T(8,128)(2,1)S(1)}, bf16[80,512]{1,0:T(8,128)(2,1)S(1)}, u32[]{:S(2)}, u32[]{:S(2)}) collective-permute-start(bf16[80,512]{1,0:T(8,128)(2,1)S(1)} %line.1.refs_11_), channel_id=1, source_target_pairs={{0,96},{1,33},{2,98},{3,35},{4,100},{5,37},{6,102},{7,39},{8,104},... | collective-permute-start | bytes 245768 | tf_op jit(solution)/shard_map/ppermute | solution.py:53
  45.8 6.1 %collective-permute-start.17 = (bf16[64,512]{1,0:T(8,128)(2,1)S(1)}, bf16[64,512]{1,0:T(8,128)(2,1)S(1)}, u32[]{:S(2)}, u32[]{:S(2)}) collective-permute-start(bf16[64,512]{1,0:T(8,128)(2,1)S(1)} %get-tuple-element.75), channel_id=1, source_target_pairs={{0,16},{1,17},{2,18},{3,19},{4,20},{5,21},{6,22},{7,23},{8,24},{9,... | collective-permute-start | bytes 196616 | tf_op jit(solution)/shard_map/ppermute | solution.py:53
  47.7 5.6 %collective-permute-start.18 = (bf16[64,512]{1,0:T(8,128)(2,1)S(1)}, bf16[64,512]{1,0:T(8,128)(2,1)S(1)}, u32[]{:S(2)}, u32[]{:S(2)}) collective-permute-start(bf16[64,512]{1,0:T(8,128)(2,1)S(1)} %get-tuple-element.76), channel_id=1, source_target_pairs={{0,24},{1,9},{2,26},{3,11},{4,28},{5,13},{6,30},{7,15},{8,16},{9,1... | collective-permute-start | bytes 196616 | tf_op jit(solution)/shard_map/ppermute | solution.py:53
  56.2 10.4 %collective-permute-start.28 = (bf16[256,512]{1,0:T(8,128)(2,1)S(1)}, bf16[256,512]{1,0:T(8,128)(2,1)S(1)}, u32[]{:S(2)}, u32[]{:S(2)}) collective-permute-start(bf16[256,512]{1,0:T(8,128)(2,1)S(1)} %far1.1.refs_7_), channel_id=1, source_target_pairs={{0,6},{1,3},{2,4},{3,1},{4,2},{5,7},{6,0},{7,5},{8,14},{9,11},{10,... | collective-permute-start | bytes 786440 | tf_op jit(solution)/shard_map/ppermute | solution.py:36
  59.2 8.6 %collective-permute-start.26 = (bf16[256,512]{1,0:T(8,128)(2,1)S(1)}, bf16[256,512]{1,0:T(8,128)(2,1)S(1)}, u32[]{:S(2)}, u32[]{:S(2)}) collective-permute-start(bf16[256,512]{1,0:T(8,128)(2,1)S(1)} %far0.1.refs_3_.refs_6_), channel_id=1, source_target_pairs={{0,2},{1,7},{2,0},{3,5},{4,6},{5,3},{6,4},{7,1},{8,10},{9,15},{10,... | collective-permute-start | bytes 786440 | tf_op jit(solution)/shard_map/ppermute | solution.py:36
  60.5 12.2 %collective-permute-start.24 = (bf16[256,512]{1,0:T(8,128)(2,1)S(1)}, bf16[256,512]{1,0:T(8,128)(2,1)S(1)}, u32[]{:S(2)}, u32[]{:S(2)}) collective-permute-start(bf16[256,512]{1,0:T(8,128)(2,1)S(1)} %get-tuple-element.83), channel_id=1, source_target_pairs={{0,2},{1,7},{2,0},{3,5},{4,6},{5,3},{6,4},{7,1},{8,10},{9,15},{10,... | collective-permute-start | bytes 786440 | tf_op jit(solution)/shard_map/ppermute | solution.py:36
  62.6 10.5 %collective-permute-start.25 = (bf16[256,512]{1,0:T(8,128)(2,1)S(1)}, bf16[256,512]{1,0:T(8,128)(2,1)S(1)}, u32[]{:S(2)}, u32[]{:S(2)}) collective-permute-start(bf16[256,512]{1,0:T(8,128)(2,1)S(1)} %get-tuple-element.84), channel_id=1, source_target_pairs={{0,6},{1,3},{2,4},{3,1},{4,2},{5,7},{6,0},{7,5},{8,14},{9,11},{10,... | collective-permute-start | bytes 786440 | tf_op jit(solution)/shard_map/ppermute | solution.py:36
  66.7 10.1 %collective-permute-start.29 = (bf16[256,512]{1,0:T(8,128)(2,1)S(1)}, bf16[256,512]{1,0:T(8,128)(2,1)S(1)}, u32[]{:S(2)}, u32[]{:S(2)}) collective-permute-start(bf16[256,512]{1,0:T(8,128)(2,1)S(1)} %add_convert_fusion), channel_id=1, source_target_pairs={{0,2},{1,7},{2,0},{3,5},{4,6},{5,3},{6,4},{7,1},{8,10},{9,15},{10,... | collective-permute-start | bytes 786440 | tf_op jit(solution)/shard_map/ppermute | solution.py:36
  67.9 9.5 %collective-permute-start.27 = (bf16[256,512]{1,0:T(8,128)(2,1)S(1)}, bf16[256,512]{1,0:T(8,128)(2,1)S(1)}, u32[]{:S(2)}, u32[]{:S(2)}) collective-permute-start(bf16[256,512]{1,0:T(8,128)(2,1)S(1)} %add_convert_fusion.1), channel_id=1, source_target_pairs={{0,6},{1,3},{2,4},{3,1},{4,2},{5,7},{6,0},{7,5},{8,14},{9,11},{10,... | collective-permute-start | bytes 786440 | tf_op jit(solution)/shard_map/ppermute | solution.py:36
  (14 other events, 58.1 us)

commit v6 on v5

--- a/solution.py
+++ b/solution.py
@@ -307,13 +307,9 @@
     )
 
 
-def mine_body(h0, h1, weight, out):
-    for i, h in enumerate((h0, h1)):
-        out[i * HALF: (i + 1) * HALF, :] = dot(h[...], weight[...])
-
-
-def far_body(half, mine, other, weight, out):
-    out[...] = (mine[pl.ds(half * HALF, HALF), :] + dot(other[...], weight[...])).astype(BF)
+def far_body(h0, h1, o0, o1, mine, theirs, top, low):
+    for h, o, out in ((h0, o0, top), (h1, o1, low)):
+        out[...] = (dot(h[...], mine[...]) + dot(o[...], theirs[...])).astype(BF)
 
 
 def own_body(h0, h1, o0, o1, mine, theirs, top, low, out_top, out_low):
@@ -379,16 +375,16 @@
 
     everything = (tokens, own_s, near1, near3, near1_s, near3_s, tuple(across), across_s)
     order = ((0, 1), (0, 0), (1, 1), (3, 1), (1, 0), (3, 0), (2, 1), (2, 0))
-    (query_sum,) = project(order, everything, (w_query,), None, "queries", after=[keys])
+    (gates,) = project(order, everything, (w_gate,), None, "gates", after=[keys], gated=True)
     (line,) = call(
         line_body, [((MSG, DV), BF)], [VM] * 5, [mine, factor, *messages], "line", moved=MSG * DV * 8,
-        after=[query_sum],
+        after=[gates],
     )
     lines = [x_flip(line, k) for k in range(1, SIDE)]
-    (gates,) = project(order, everything, (w_gate,), None, "gates", after=[line], gated=True)
+    (query_sum,) = project(order, everything, (w_query,), None, "queries", after=[line])
     e0, e1, e2, e3 = call(
         entry_body, [((CUT, DV), BF)] * 4, [VM] * 8, [mine, factor, *messages, *lines], "entry",
-        moved=MSG * DV * 16, after=[gates],
+        moved=MSG * DV * 16, after=[query_sum],
     )
     queries, local = call(
         local_body,
@@ -410,14 +406,10 @@
         )
         hidden.append(part)
         other.append(tp_swap(part))
-    (mine,) = call(
-        mine_body, [((ROWS, DV), F32)], [VM] * 3, [*hidden, kept_far], "far_mine", flops=2 * ROWS * DV * DV, moved=2 * DV * DV
-    )
-    for half in range(2):
-        far += call(
-            functools.partial(far_body, half), [((HALF, DV), BF)], [VM] * 3, [mine, other[half], theirs_far], f"far{half}",
-            flops=2 * HALF * DV * DV, moved=2 * DV * DV, after=far,
-        )
+    far = call(
+        far_body, [((HALF, DV), BF)] * 2, [VM] * 6, [*hidden, *other, kept_far, theirs_far], "far",
+        flops=4 * ROWS * DV * DV, moved=4 * DV * DV,
+    )
     via3, via1 = y_flip(far[0], 3), y_flip(far[1], 1)
     top1, low1, top3, low3 = partial(hidden, other, kept, theirs, (F32, BF, BF, F32), "beside", after=far)
     from1_low, from3_top = y_flip(low1, 1), y_flip(top3, 3)

time: 78.5 us -> 78.8 us (level)
  waiting for transfers between devices: 28.8 us -> 29.8 us
    ppermute x9, waiting for transfers between devices: 0.43 us -> 1.41 us  [tp_swap(): return lax.ppermute(value, 'tp', [(i, i ^ 1) for i in range(8)])]
    pallas_call x22 -> x20, Pallas kernels: 16.7 us -> 16.4 us  [call(): pl.pallas_call(whole, out_shape=shapes, in_specs=list(in_specs) + [ANY] *...]
  transfers between devices with their start and end apart: 30 -> 30, of which waited for: 17 -> 16; matrix products, arithmetic and copies ran while one was open for 0% -> 0% of each run, Pallas kernels for 20% -> 20%
where the time goes in v6:
time: 78.8 us; the launch traced here: 78.6 us
  waiting for transfers between devices  29.8 us (38%)
  starting transfers between devices  29.3 us (37%)
  Pallas kernels  16.4 us (21%)
  local copies, waits for them, and re-layouts  2.66 us (3%)
    ppermute x12, waiting for transfers between devices, y_flip(): lax.ppermute(value, 'tp', [(i, i ^ 2 * turn(k, i % 2)) for i in range(8)])  19.2 us
    pallas_call x20, Pallas kernels, call(): pl.pallas_call(whole, out_shape=shapes, in_specs=list(in_specs) + [ANY] *...  16.4 us
    ppermute x12, starting transfers between devices, y_flip(): lax.ppermute(value, 'tp', [(i, i ^ 2 * turn(k, i % 2)) for i in range(8)])  14.4 us
    ppermute x9, starting transfers between devices, ctx_flip(): return lax.ppermute(value, ('ctx', 'tp'), pairs)  13.1 us
    ppermute x9, waiting for transfers between devices, ctx_flip(): return lax.ppermute(value, ('ctx', 'tp'), pairs)  9.19 us
    unnamed x16, local copies, waits for them, and re-layouts  2.66 us
    ppermute x9, starting transfers between devices, tp_swap(): return lax.ppermute(value, 'tp', [(i, i ^ 1) for i in range(8)])  1.85 us
  transfers between devices with their start and end apart: 30, of which 16 were waited for; matrix products, arithmetic and copies ran while one was open for 0% of the time, Pallas kernels for 20%

profile of v6, /device:TPU:0, one launch (start us, length us, event | category | flops | bytes accessed | tf_op | source)
XLA Modules:
  0.0 78.6 jit_solution(18267371597878309314)
XLA Ops:
  1.1 3.2 %collective-permute-start.1 = (bf16[256,512]{1,0:T(8,128)(2,1)S(1)}, bf16[256,512]{1,0:T(8,128)(2,1)S(1)}, u32[]{:S(2)}, u32[]{:S(2)}) collective-permute-start(bf16[256,512]{1,0:T(8,128)(2,1)S(1)} %get-tuple-element.49), channel_id=1, source_target_pairs={{0,6},{1,3},{2,4},{3,1},{4,2},{5,7},{6,0},{7,5},{8,14},{9,11},{10,... | collective-permute-start | bytes 786440 | tf_op jit(solution)/shard_map/ppermute | solution.py:36
  6.3 2.2 %pick.1 = (bf16[512,512]{1,0:T(8,128)(2,1)S(1)}, bf16[512,1536]{1,0:T(8,128)(2,1)S(1)}, bf16[512,512]{1,0:T(8,128)(2,1)S(1)}, bf16[512,1536]{1,0:T(8,128)(2,1)S(1)}) custom-call(bf16[512,4096]{1,0:T(8,128)(2,1)} %refs_0_.7), custom_call_target="tpu_custom_call" | custom-call | bytes 1 | tf_op jit(solution)/shard_map/pick/pallas_call | solution.py:76
  9.1 1.6 %copy-done.1 = bf16[4096,256]{1,0:T(8,128)(2,1)S(1)} copy-done((bf16[4096,256]{1,0:T(8,128)(2,1)S(1)}, bf16[4096,256]{1,0:T(8,128)(2,1)}, u32[]{:S(2)}) %copy-start.1) | copy-done | bytes 2097176
  11.7 1.5 %collective-permute-done.2.refs_1_ = bf16[256,512]{1,0:T(8,128)(2,1)S(1)} collective-permute-done((bf16[256,512]{1,0:T(8,128)(2,1)S(1)}, bf16[256,512]{1,0:T(8,128)(2,1)S(1)}, u32[]{:S(2)}, u32[]{:S(2)}) %collective-permute-start.2) | collective-permute-done | bytes 262176 | tf_op jit(solution)/shard_map/ppermute | solution.py:36
  13.7 1.5 %collective-permute-start.8 = (bf16[256,512]{1,0:T(8,128)(2,1)S(1)}, bf16[256,512]{1,0:T(8,128)(2,1)S(1)}, u32[]{:S(2)}, u32[]{:S(2)}) collective-permute-start(bf16[256,512]{1,0:T(8,128)(2,1)S(1)} %get-tuple-element.55.refs_3_), channel_id=1, source_target_pairs={{0,6},{1,3},{2,4},{3,1},{4,2},{5,7},{6,0},{7,5},{8,14},{9,11},{10,... | collective-permute-start | bytes 786440 | tf_op jit(solution)/shard_map/ppermute | solution.py:36
  15.1 1.5 %collective-permute-done.3.refs_1_ = bf16[256,512]{1,0:T(8,128)(2,1)S(1)} collective-permute-done((bf16[256,512]{1,0:T(8,128)(2,1)S(1)}, bf16[256,512]{1,0:T(8,128)(2,1)S(1)}, u32[]{:S(2)}, u32[]{:S(2)}) %collective-permute-start.3) | collective-permute-done | bytes 262176 | tf_op jit(solution)/shard_map/ppermute | solution.py:36
  18.3 3.7 %collective-permute-done.7.refs_0_ = bf16[256,512]{1,0:T(8,128)(2,1)S(1)} collective-permute-done((bf16[256,512]{1,0:T(8,128)(2,1)S(1)}, bf16[256,512]{1,0:T(8,128)(2,1)S(1)}, u32[]{:S(2)}, u32[]{:S(2)}) %collective-permute-start.7) | collective-permute-done | bytes 262176 | tf_op jit(solution)/shard_map/ppermute | solution.py:36
  26.1 4.0 %collective-permute-start.11 = (bf16[80,512]{1,0:T(8,128)(2,1)S(1)}, bf16[80,512]{1,0:T(8,128)(2,1)S(1)}, u32[]{:S(2)}, u32[]{:S(2)}) collective-permute-start(bf16[80,512]{1,0:T(8,128)(2,1)S(1)} %get-tuple-element.70), channel_id=1, source_target_pairs={{0,16},{1,17},{2,18},{3,19},{4,20},{5,21},{6,22},{7,23},{8,24},{9,... | collective-permute-start | bytes 245768 | tf_op jit(solution)/shard_map/ppermute | solution.py:53
  31.1 2.5 %gates.1.refs_5_.refs_7_ = f32[512,512]{1,0:T(8,128)S(1)} custom-call(bf16[512,512]{1,0:T(8,128)(2,1)S(1)} %copy-done.4, bf16[512,512]{1,0:T(8,128)(2,1)S(1)} %collective-permute-done.refs_1_, bf16[512,512]{1,0:T(8,128)(2,1)S(1)} %get-tuple-element.56.refs_0_.refs_2_, bf16[512,512]{1,0:T(8,128)(2,1)S(1)} %get-tuple-element.57.refs_1_.refs_3_, ...), custom_call_target="tpu_custom_call" | custom-call | flops 2147483648 | bytes 4194305 | tf_op jit(solution)/shard_map/gates/pallas_call | solution.py:76
  33.6 3.0 %collective-permute-done.12.refs_3_ = bf16[80,512]{1,0:T(8,128)(2,1)S(1)} collective-permute-done((bf16[80,512]{1,0:T(8,128)(2,1)S(1)}, bf16[80,512]{1,0:T(8,128)(2,1)S(1)}, u32[]{:S(2)}, u32[]{:S(2)}) %collective-permute-start.12) | collective-permute-done | bytes 81952 | tf_op jit(solution)/shard_map/ppermute | solution.py:53
  36.7 3.1 %collective-permute-start.14 = (bf16[80,512]{1,0:T(8,128)(2,1)S(1)}, bf16[80,512]{1,0:T(8,128)(2,1)S(1)}, u32[]{:S(2)}, u32[]{:S(2)}) collective-permute-start(bf16[80,512]{1,0:T(8,128)(2,1)S(1)} %line.1.refs_11_), channel_id=1, source_target_pairs={{0,64},{1,65},{2,66},{3,67},{4,68},{5,69},{6,70},{7,71},{8,72},{9,... | collective-permute-start | bytes 245768 | tf_op jit(solution)/shard_map/ppermute | solution.py:53
  40.9 1.3 %queries.1.refs_8_.refs_0_ = f32[512,256]{1,0:T(8,128)S(1)} custom-call(bf16[512,512]{1,0:T(8,128)(2,1)S(1)} %copy-done.4, bf16[512,512]{1,0:T(8,128)(2,1)S(1)} %collective-permute-done.refs_1_, bf16[512,512]{1,0:T(8,128)(2,1)S(1)} %get-tuple-element.56.refs_0_.refs_2_, bf16[512,512]{1,0:T(8,128)(2,1)S(1)} %get-tuple-element.57.refs_1_.refs_3_, ...), custom_call_target="tpu_custom_call" | custom-call | flops 1073741824 | bytes 2097153 | tf_op jit(solution)/shard_map/queries/pallas_call | solution.py:76
  42.7 2.7 %collective-permute-done.15.refs_6_ = bf16[80,512]{1,0:T(8,128)(2,1)S(1)} collective-permute-done((bf16[80,512]{1,0:T(8,128)(2,1)S(1)}, bf16[80,512]{1,0:T(8,128)(2,1)S(1)}, u32[]{:S(2)}, u32[]{:S(2)}) %collective-permute-start.15) | collective-permute-done | bytes 81952 | tf_op jit(solution)/shard_map/ppermute | solution.py:53
  45.8 1.9 %collective-permute-start.17 = (bf16[64,512]{1,0:T(8,128)(2,1)S(1)}, bf16[64,512]{1,0:T(8,128)(2,1)S(1)}, u32[]{:S(2)}, u32[]{:S(2)}) collective-permute-start(bf16[64,512]{1,0:T(8,128)(2,1)S(1)} %get-tuple-element.77), channel_id=1, source_target_pairs={{0,16},{1,17},{2,18},{3,19},{4,20},{5,21},{6,22},{7,23},{8,24},{9,... | collective-permute-start | bytes 196616 | tf_op jit(solution)/shard_map/ppermute | solution.py:53
  50.1 1.8 %collective-permute-done.17.refs_2_ = bf16[64,512]{1,0:T(8,128)(2,1)S(1)} collective-permute-done((bf16[64,512]{1,0:T(8,128)(2,1)S(1)}, bf16[64,512]{1,0:T(8,128)(2,1)S(1)}, u32[]{:S(2)}, u32[]{:S(2)}) %collective-permute-start.17) | collective-permute-done | bytes 65568 | tf_op jit(solution)/shard_map/ppermute | solution.py:53
  51.9 1.2 %collective-permute-done.18.refs_3_ = bf16[64,512]{1,0:T(8,128)(2,1)S(1)} collective-permute-done((bf16[64,512]{1,0:T(8,128)(2,1)S(1)}, bf16[64,512]{1,0:T(8,128)(2,1)S(1)}, u32[]{:S(2)}, u32[]{:S(2)}) %collective-permute-start.18) | collective-permute-done | bytes 65568 | tf_op jit(solution)/shard_map/ppermute | solution.py:53
  56.7 3.1 %collective-permute-start.28 = (bf16[256,512]{1,0:T(8,128)(2,1)S(1)}, bf16[256,512]{1,0:T(8,128)(2,1)S(1)}, u32[]{:S(2)}, u32[]{:S(2)}) collective-permute-start(bf16[256,512]{1,0:T(8,128)(2,1)S(1)} %get-tuple-element.86.refs_7_), channel_id=1, source_target_pairs={{0,6},{1,3},{2,4},{3,1},{4,2},{5,7},{6,0},{7,5},{8,14},{9,11},{10,... | collective-permute-start | bytes 786440 | tf_op jit(solution)/shard_map/ppermute | solution.py:36
  59.8 1.2 %beside.1 = (f32[256,512]{1,0:T(8,128)S(1)}, bf16[256,512]{1,0:T(8,128)(2,1)S(1)}, bf16[256,512]{1,0:T(8,128)(2,1)S(1)}, f32[256,512]{1,0:T(8,128)S(1)}) custom-call(bf16[256,512]{1,0:T(8,128)(2,1)S(1)} %hidden0.1.refs_8_.refs_0_, bf16[256,512]{1,0:T(8,128)(2,1)S(1)} %hidden1.1.refs_1_, bf16[256,512]{1,0:T(8,128)(2,1)S(1)} %collective-permute-done.20.refs_2_, ...), custom_call_target="tpu_custom_call" | custom-call | flops 1073741824 | bytes 2097152 | tf_op jit(solution)/shard_map/beside/pallas_call | solution.py:76
  61.0 2.1 %collective-permute-start.24 = (bf16[256,512]{1,0:T(8,128)(2,1)S(1)}, bf16[256,512]{1,0:T(8,128)(2,1)S(1)}, u32[]{:S(2)}, u32[]{:S(2)}) collective-permute-start(bf16[256,512]{1,0:T(8,128)(2,1)S(1)} %get-tuple-element.87), channel_id=1, source_target_pairs={{0,2},{1,7},{2,0},{3,5},{4,6},{5,3},{6,4},{7,1},{8,10},{9,15},{10,... | collective-permute-start | bytes 786440 | tf_op jit(solution)/shard_map/ppermute | solution.py:36
  63.4 3.7 %collective-permute-done.28 = bf16[256,512]{1,0:T(8,128)(2,1)S(1)} collective-permute-done((bf16[256,512]{1,0:T(8,128)(2,1)S(1)}, bf16[256,512]{1,0:T(8,128)(2,1)S(1)}, u32[]{:S(2)}, u32[]{:S(2)}) %collective-permute-start.28) | collective-permute-done | bytes 262176 | tf_op jit(solution)/shard_map/ppermute | solution.py:36
  67.3 1.4 %collective-permute-done.26 = bf16[256,512]{1,0:T(8,128)(2,1)S(1)} collective-permute-done((bf16[256,512]{1,0:T(8,128)(2,1)S(1)}, bf16[256,512]{1,0:T(8,128)(2,1)S(1)}, u32[]{:S(2)}, u32[]{:S(2)}) %collective-permute-start.26) | collective-permute-done | bytes 262176 | tf_op jit(solution)/shard_map/ppermute | solution.py:36
  68.7 1.7 %collective-permute-start.27 = (bf16[256,512]{1,0:T(8,128)(2,1)S(1)}, bf16[256,512]{1,0:T(8,128)(2,1)S(1)}, u32[]{:S(2)}, u32[]{:S(2)}) collective-permute-start(bf16[256,512]{1,0:T(8,128)(2,1)S(1)} %add_convert_fusion.1), channel_id=1, source_target_pairs={{0,6},{1,3},{2,4},{3,1},{4,2},{5,7},{6,0},{7,5},{8,14},{9,11},{10,... | collective-permute-start | bytes 786440 | tf_op jit(solution)/shard_map/ppermute | solution.py:36
  70.5 3.2 %collective-permute-done.24.refs_6_ = bf16[256,512]{1,0:T(8,128)(2,1)S(1)} collective-permute-done((bf16[256,512]{1,0:T(8,128)(2,1)S(1)}, bf16[256,512]{1,0:T(8,128)(2,1)S(1)}, u32[]{:S(2)}, u32[]{:S(2)}) %collective-permute-start.24) | collective-permute-done | bytes 262176 | tf_op jit(solution)/shard_map/ppermute | solution.py:36
  74.4 3.0 %collective-permute-done.29.refs_3_ = bf16[256,512]{1,0:T(8,128)(2,1)S(1)} collective-permute-done((bf16[256,512]{1,0:T(8,128)(2,1)S(1)}, bf16[256,512]{1,0:T(8,128)(2,1)S(1)}, u32[]{:S(2)}, u32[]{:S(2)}) %collective-permute-start.29) | collective-permute-done | bytes 262176 | tf_op jit(solution)/shard_map/ppermute | solution.py:36
  (76 shorter events, 22.2 us)
Async XLA Ops:
  0.0 8.6 %collective-permute-start = (bf16[512,512]{1,0:T(8,128)(2,1)}, bf16[512,512]{1,0:T(8,128)(2,1)S(1)}, u32[]{:S(2)}, u32[]{:S(2)}) collective-permute-start(bf16[512,512]{1,0:T(8,128)(2,1)} %refs_0_.11), channel_id=1, source_target_pairs={{0,1},{1,0},{2,3},{3,2},{4,5},{5,4},{6,7},{7,6},{8,9},{9,8},{10,11... | collective-permute-start | bytes 1572872 | tf_op jit(solution)/shard_map/ppermute | solution.py:40
  1.1 10.5 %collective-permute-start.1 = (bf16[256,512]{1,0:T(8,128)(2,1)S(1)}, bf16[256,512]{1,0:T(8,128)(2,1)S(1)}, u32[]{:S(2)}, u32[]{:S(2)}) collective-permute-start(bf16[256,512]{1,0:T(8,128)(2,1)S(1)} %get-tuple-element.49), channel_id=1, source_target_pairs={{0,6},{1,3},{2,4},{3,1},{4,2},{5,7},{6,0},{7,5},{8,14},{9,11},{10,... | collective-permute-start | bytes 786440 | tf_op jit(solution)/shard_map/ppermute | solution.py:36
  4.3 8.9 %collective-permute-start.2 = (bf16[256,512]{1,0:T(8,128)(2,1)S(1)}, bf16[256,512]{1,0:T(8,128)(2,1)S(1)}, u32[]{:S(2)}, u32[]{:S(2)}) collective-permute-start(bf16[256,512]{1,0:T(8,128)(2,1)S(1)} %get-tuple-element.50), channel_id=1, source_target_pairs={{0,2},{1,7},{2,0},{3,5},{4,6},{5,3},{6,4},{7,1},{8,10},{9,15},{10,... | collective-permute-start | bytes 786440 | tf_op jit(solution)/shard_map/ppermute | solution.py:36
  4.4 12.2 %collective-permute-start.3 = (bf16[256,512]{1,0:T(8,128)(2,1)S(1)}, bf16[256,512]{1,0:T(8,128)(2,1)S(1)}, u32[]{:S(2)}, u32[]{:S(2)}) collective-permute-start(bf16[256,512]{1,0:T(8,128)(2,1)S(1)} %get-tuple-element.50), channel_id=1, source_target_pairs={{0,6},{1,3},{2,4},{3,1},{4,2},{5,7},{6,0},{7,5},{8,14},{9,11},{10,... | collective-permute-start | bytes 786440 | tf_op jit(solution)/shard_map/ppermute | solution.py:36
  5.5 11.1 %collective-permute-start.4 = (bf16[256,512]{1,0:T(8,128)(2,1)S(1)}, bf16[256,512]{1,0:T(8,128)(2,1)S(1)}, u32[]{:S(2)}, u32[]{:S(2)}) collective-permute-start(bf16[256,512]{1,0:T(8,128)(2,1)S(1)} %get-tuple-element.49), channel_id=1, source_target_pairs={{0,2},{1,7},{2,0},{3,5},{4,6},{5,3},{6,4},{7,1},{8,10},{9,15},{10,... | collective-permute-start | bytes 786440 | tf_op jit(solution)/shard_map/ppermute | solution.py:36
  8.6 51.2 %collective-permute-start.22 = (bf16[512,1536]{1,0:T(8,128)(2,1)S(1)}, bf16[512,1536]{1,0:T(8,128)(2,1)S(1)}, u32[]{:S(2)}, u32[]{:S(2)}) collective-permute-start(bf16[512,1536]{1,0:T(8,128)(2,1)S(1)} %get-tuple-element.83), channel_id=1, source_target_pairs={{0,1},{1,0},{2,3},{3,2},{4,5},{5,4},{6,7},{7,6},{8,9},{9,8},{10,11... | collective-permute-start | bytes 4718600 | tf_op jit(solution)/shard_map/ppermute | solution.py:40
  13.2 8.8 %collective-permute-start.7 = (bf16[256,512]{1,0:T(8,128)(2,1)S(1)}, bf16[256,512]{1,0:T(8,128)(2,1)S(1)}, u32[]{:S(2)}, u32[]{:S(2)}) collective-permute-start(bf16[256,512]{1,0:T(8,128)(2,1)S(1)} %get-tuple-element.54.refs_0_), channel_id=1, source_target_pairs={{0,2},{1,7},{2,0},{3,5},{4,6},{5,3},{6,4},{7,1},{8,10},{9,15},{10,... | collective-permute-start | bytes 786440 | tf_op jit(solution)/shard_map/ppermute | solution.py:36
  13.7 9.1 %collective-permute-start.8 = (bf16[256,512]{1,0:T(8,128)(2,1)S(1)}, bf16[256,512]{1,0:T(8,128)(2,1)S(1)}, u32[]{:S(2)}, u32[]{:S(2)}) collective-permute-start(bf16[256,512]{1,0:T(8,128)(2,1)S(1)} %get-tuple-element.55.refs_3_), channel_id=1, source_target_pairs={{0,6},{1,3},{2,4},{3,1},{4,2},{5,7},{6,0},{7,5},{8,14},{9,11},{10,... | collective-permute-start | bytes 786440 | tf_op jit(solution)/shard_map/ppermute | solution.py:36
  16.7 7.2 %collective-permute-start.5 = (bf16[512,512]{1,0:T(8,128)(2,1)S(1)}, bf16[512,512]{1,0:T(8,128)(2,1)S(1)}, u32[]{:S(2)}, u32[]{:S(2)}) collective-permute-start(bf16[512,512]{1,0:T(8,128)(2,1)S(1)} %get-tuple-element.56.refs_0_.refs_2_), channel_id=1, source_target_pairs={{0,1},{1,0},{2,3},{3,2},{4,5},{5,4},{6,7},{7,6},{8,9},{9,8},{10,11... | collective-permute-start | bytes 1572872 | tf_op jit(solution)/shard_map/ppermute | solution.py:40
  17.2 6.9 %collective-permute-start.6 = (bf16[512,512]{1,0:T(8,128)(2,1)S(1)}, bf16[512,512]{1,0:T(8,128)(2,1)S(1)}, u32[]{:S(2)}, u32[]{:S(2)}) collective-permute-start(bf16[512,512]{1,0:T(8,128)(2,1)S(1)} %get-tuple-element.57.refs_1_.refs_3_), channel_id=1, source_target_pairs={{0,1},{1,0},{2,3},{3,2},{4,5},{5,4},{6,7},{7,6},{8,9},{9,8},{10,11... | collective-permute-start | bytes 1572872 | tf_op jit(solution)/shard_map/ppermute | solution.py:40
  23.9 30.7 %collective-permute-start.23 = (bf16[512,512]{1,0:T(8,128)(2,1)S(1)}, bf16[512,512]{1,0:T(8,128)(2,1)S(1)}, u32[]{:S(2)}, u32[]{:S(2)}) collective-permute-start(bf16[512,512]{1,0:T(8,128)(2,1)S(1)} %get-tuple-element.84), channel_id=1, source_target_pairs={{0,1},{1,0},{2,3},{3,2},{4,5},{5,4},{6,7},{7,6},{8,9},{9,8},{10,11... | collective-permute-start | bytes 1572872 | tf_op jit(solution)/shard_map/ppermute | solution.py:40
  26.1 7.6 %collective-permute-start.11 = (bf16[80,512]{1,0:T(8,128)(2,1)S(1)}, bf16[80,512]{1,0:T(8,128)(2,1)S(1)}, u32[]{:S(2)}, u32[]{:S(2)}) collective-permute-start(bf16[80,512]{1,0:T(8,128)(2,1)S(1)} %get-tuple-element.70), channel_id=1, source_target_pairs={{0,16},{1,17},{2,18},{3,19},{4,20},{5,21},{6,22},{7,23},{8,24},{9,... | collective-permute-start | bytes 245768 | tf_op jit(solution)/shard_map/ppermute | solution.py:53
  30.1 6.5 %collective-permute-start.12 = (bf16[80,512]{1,0:T(8,128)(2,1)S(1)}, bf16[80,512]{1,0:T(8,128)(2,1)S(1)}, u32[]{:S(2)}, u32[]{:S(2)}) collective-permute-start(bf16[80,512]{1,0:T(8,128)(2,1)S(1)} %get-tuple-element.71), channel_id=1, source_target_pairs={{0,24},{1,9},{2,26},{3,11},{4,28},{5,13},{6,30},{7,15},{8,16},{9,1... | collective-permute-start | bytes 245768 | tf_op jit(solution)/shard_map/ppermute | solution.py:53
  30.8 5.8 %collective-permute-start.13 = (bf16[80,512]{1,0:T(8,128)(2,1)S(1)}, bf16[80,512]{1,0:T(8,128)(2,1)S(1)}, u32[]{:S(2)}, u32[]{:S(2)}) collective-permute-start(bf16[80,512]{1,0:T(8,128)(2,1)S(1)} %get-tuple-element.72), channel_id=1, source_target_pairs={{0,8},{1,25},{2,10},{3,27},{4,12},{5,29},{6,14},{7,31},{8,0},{9,17... | collective-permute-start | bytes 245768 | tf_op jit(solution)/shard_map/ppermute | solution.py:53
  36.7 6.0 %collective-permute-start.14 = (bf16[80,512]{1,0:T(8,128)(2,1)S(1)}, bf16[80,512]{1,0:T(8,128)(2,1)S(1)}, u32[]{:S(2)}, u32[]{:S(2)}) collective-permute-start(bf16[80,512]{1,0:T(8,128)(2,1)S(1)} %line.1.refs_11_), channel_id=1, source_target_pairs={{0,64},{1,65},{2,66},{3,67},{4,68},{5,69},{6,70},{7,71},{8,72},{9,... | collective-permute-start | bytes 245768 | tf_op jit(solution)/shard_map/ppermute | solution.py:53
  39.8 5.7 %collective-permute-start.15 = (bf16[80,512]{1,0:T(8,128)(2,1)S(1)}, bf16[80,512]{1,0:T(8,128)(2,1)S(1)}, u32[]{:S(2)}, u32[]{:S(2)}) collective-permute-start(bf16[80,512]{1,0:T(8,128)(2,1)S(1)} %line.1.refs_11_), channel_id=1, source_target_pairs={{0,96},{1,33},{2,98},{3,35},{4,100},{5,37},{6,102},{7,39},{8,104},... | collective-permute-start | bytes 245768 | tf_op jit(solution)/shard_map/ppermute | solution.py:53
  45.8 6.1 %collective-permute-start.17 = (bf16[64,512]{1,0:T(8,128)(2,1)S(1)}, bf16[64,512]{1,0:T(8,128)(2,1)S(1)}, u32[]{:S(2)}, u32[]{:S(2)}) collective-permute-start(bf16[64,512]{1,0:T(8,128)(2,1)S(1)} %get-tuple-element.77), channel_id=1, source_target_pairs={{0,16},{1,17},{2,18},{3,19},{4,20},{5,21},{6,22},{7,23},{8,24},{9,... | collective-permute-start | bytes 196616 | tf_op jit(solution)/shard_map/ppermute | solution.py:53
  47.6 5.5 %collective-permute-start.18 = (bf16[64,512]{1,0:T(8,128)(2,1)S(1)}, bf16[64,512]{1,0:T(8,128)(2,1)S(1)}, u32[]{:S(2)}, u32[]{:S(2)}) collective-permute-start(bf16[64,512]{1,0:T(8,128)(2,1)S(1)} %get-tuple-element.78), channel_id=1, source_target_pairs={{0,24},{1,9},{2,26},{3,11},{4,28},{5,13},{6,30},{7,15},{8,16},{9,1... | collective-permute-start | bytes 196616 | tf_op jit(solution)/shard_map/ppermute | solution.py:53
  56.7 10.4 %collective-permute-start.28 = (bf16[256,512]{1,0:T(8,128)(2,1)S(1)}, bf16[256,512]{1,0:T(8,128)(2,1)S(1)}, u32[]{:S(2)}, u32[]{:S(2)}) collective-permute-start(bf16[256,512]{1,0:T(8,128)(2,1)S(1)} %get-tuple-element.86.refs_7_), channel_id=1, source_target_pairs={{0,6},{1,3},{2,4},{3,1},{4,2},{5,7},{6,0},{7,5},{8,14},{9,11},{10,... | collective-permute-start | bytes 786440 | tf_op jit(solution)/shard_map/ppermute | solution.py:36
  59.8 8.9 %collective-permute-start.26 = (bf16[256,512]{1,0:T(8,128)(2,1)S(1)}, bf16[256,512]{1,0:T(8,128)(2,1)S(1)}, u32[]{:S(2)}, u32[]{:S(2)}) collective-permute-start(bf16[256,512]{1,0:T(8,128)(2,1)S(1)} %get-tuple-element.85.refs_6_), channel_id=1, source_target_pairs={{0,2},{1,7},{2,0},{3,5},{4,6},{5,3},{6,4},{7,1},{8,10},{9,15},{10,... | collective-permute-start | bytes 786440 | tf_op jit(solution)/shard_map/ppermute | solution.py:36
  61.0 12.6 %collective-permute-start.24 = (bf16[256,512]{1,0:T(8,128)(2,1)S(1)}, bf16[256,512]{1,0:T(8,128)(2,1)S(1)}, u32[]{:S(2)}, u32[]{:S(2)}) collective-permute-start(bf16[256,512]{1,0:T(8,128)(2,1)S(1)} %get-tuple-element.87), channel_id=1, source_target_pairs={{0,2},{1,7},{2,0},{3,5},{4,6},{5,3},{6,4},{7,1},{8,10},{9,15},{10,... | collective-permute-start | bytes 786440 | tf_op jit(solution)/shard_map/ppermute | solution.py:36
  63.2 10.5 %collective-permute-start.25 = (bf16[256,512]{1,0:T(8,128)(2,1)S(1)}, bf16[256,512]{1,0:T(8,128)(2,1)S(1)}, u32[]{:S(2)}, u32[]{:S(2)}) collective-permute-start(bf16[256,512]{1,0:T(8,128)(2,1)S(1)} %get-tuple-element.88), channel_id=1, source_target_pairs={{0,6},{1,3},{2,4},{3,1},{4,2},{5,7},{6,0},{7,5},{8,14},{9,11},{10,... | collective-permute-start | bytes 786440 | tf_op jit(solution)/shard_map/ppermute | solution.py:36
  67.2 10.2 %collective-permute-start.29 = (bf16[256,512]{1,0:T(8,128)(2,1)S(1)}, bf16[256,512]{1,0:T(8,128)(2,1)S(1)}, u32[]{:S(2)}, u32[]{:S(2)}) collective-permute-start(bf16[256,512]{1,0:T(8,128)(2,1)S(1)} %add_convert_fusion), channel_id=1, source_target_pairs={{0,2},{1,7},{2,0},{3,5},{4,6},{5,3},{6,4},{7,1},{8,10},{9,15},{10,... | collective-permute-start | bytes 786440 | tf_op jit(solution)/shard_map/ppermute | solution.py:36
  68.7 9.0 %collective-permute-start.27 = (bf16[256,512]{1,0:T(8,128)(2,1)S(1)}, bf16[256,512]{1,0:T(8,128)(2,1)S(1)}, u32[]{:S(2)}, u32[]{:S(2)}) collective-permute-start(bf16[256,512]{1,0:T(8,128)(2,1)S(1)} %add_convert_fusion.1), channel_id=1, source_target_pairs={{0,6},{1,3},{2,4},{3,1},{4,2},{5,7},{6,0},{7,5},{8,14},{9,11},{10,... | collective-permute-start | bytes 786440 | tf_op jit(solution)/shard_map/ppermute | solution.py:36
  (14 other events, 58.1 us)

commit v7 on v5

--- a/solution.py
+++ b/solution.py
@@ -379,16 +379,16 @@
 
     everything = (tokens, own_s, near1, near3, near1_s, near3_s, tuple(across), across_s)
     order = ((0, 1), (0, 0), (1, 1), (3, 1), (1, 0), (3, 0), (2, 1), (2, 0))
-    (query_sum,) = project(order, everything, (w_query,), None, "queries", after=[keys])
+    (gates,) = project(order, everything, (w_gate,), None, "gates", after=[keys], gated=True)
     (line,) = call(
         line_body, [((MSG, DV), BF)], [VM] * 5, [mine, factor, *messages], "line", moved=MSG * DV * 8,
-        after=[query_sum],
+        after=[gates],
     )
     lines = [x_flip(line, k) for k in range(1, SIDE)]
-    (gates,) = project(order, everything, (w_gate,), None, "gates", after=[line], gated=True)
+    (query_sum,) = project(order, everything, (w_query,), None, "queries", after=[line])
     e0, e1, e2, e3 = call(
         entry_body, [((CUT, DV), BF)] * 4, [VM] * 8, [mine, factor, *messages, *lines], "entry",
-        moved=MSG * DV * 16, after=[gates],
+        moved=MSG * DV * 16, after=[query_sum],
     )
     queries, local = call(
         local_body,

time: 78.5 us -> 78.5 us (level)
  no operation moved by 1% of the time
where the time goes in v7:
time: 78.5 us; the launch traced here: 78.3 us
  starting transfers between devices  29.6 us (38%)
  waiting for transfers between devices  28.8 us (37%)
  Pallas kernels  16.7 us (21%)
  local copies, waits for them, and re-layouts  2.66 us (3%)
    ppermute x12, waiting for transfers between devices, y_flip(): lax.ppermute(value, 'tp', [(i, i ^ 2 * turn(k, i % 2)) for i in range(8)])  19.2 us
    pallas_call x22, Pallas kernels, call(): pl.pallas_call(whole, out_shape=shapes, in_specs=list(in_specs) + [ANY] *...  16.7 us
    ppermute x12, starting transfers between devices, y_flip(): lax.ppermute(value, 'tp', [(i, i ^ 2 * turn(k, i % 2)) for i in range(8)])  14.6 us
    ppermute x9, starting transfers between devices, ctx_flip(): return lax.ppermute(value, ('ctx', 'tp'), pairs)  13.1 us
    ppermute x9, waiting for transfers between devices, ctx_flip(): return lax.ppermute(value, ('ctx', 'tp'), pairs)  9.19 us
    unnamed x16, local copies, waits for them, and re-layouts  2.66 us
    ppermute x9, starting transfers between devices, tp_swap(): return lax.ppermute(value, 'tp', [(i, i ^ 1) for i in range(8)])  1.94 us
  transfers between devices with their start and end apart: 30, of which 17 were waited for; matrix products, arithmetic and copies ran while one was open for 0% of the time, Pallas kernels for 20%

profile of v7, /device:TPU:0, one launch (start us, length us, event | category | flops | bytes accessed | tf_op | source)
XLA Modules:
  0.0 78.3 jit_solution(5862756478718607817)
XLA Ops:
  1.1 3.2 %collective-permute-start.1 = (bf16[256,512]{1,0:T(8,128)(2,1)S(1)}, bf16[256,512]{1,0:T(8,128)(2,1)S(1)}, u32[]{:S(2)}, u32[]{:S(2)}) collective-permute-start(bf16[256,512]{1,0:T(8,128)(2,1)S(1)} %get-tuple-element.47), channel_id=1, source_target_pairs={{0,6},{1,3},{2,4},{3,1},{4,2},{5,7},{6,0},{7,5},{8,14},{9,11},{10,... | collective-permute-start | bytes 786440 | tf_op jit(solution)/shard_map/ppermute | solution.py:36
  6.3 2.2 %pick.1 = (bf16[512,512]{1,0:T(8,128)(2,1)S(1)}, bf16[512,1536]{1,0:T(8,128)(2,1)S(1)}, bf16[512,512]{1,0:T(8,128)(2,1)S(1)}, bf16[512,1536]{1,0:T(8,128)(2,1)S(1)}) custom-call(bf16[512,4096]{1,0:T(8,128)(2,1)} %refs_0_.7), custom_call_target="tpu_custom_call" | custom-call | bytes 1 | tf_op jit(solution)/shard_map/pick/pallas_call | solution.py:76
  9.1 1.6 %copy-done.1 = bf16[4096,256]{1,0:T(8,128)(2,1)S(1)} copy-done((bf16[4096,256]{1,0:T(8,128)(2,1)S(1)}, bf16[4096,256]{1,0:T(8,128)(2,1)}, u32[]{:S(2)}) %copy-start.1) | copy-done | bytes 2097176
  11.7 1.5 %collective-permute-done.2.refs_1_ = bf16[256,512]{1,0:T(8,128)(2,1)S(1)} collective-permute-done((bf16[256,512]{1,0:T(8,128)(2,1)S(1)}, bf16[256,512]{1,0:T(8,128)(2,1)S(1)}, u32[]{:S(2)}, u32[]{:S(2)}) %collective-permute-start.2) | collective-permute-done | bytes 262176 | tf_op jit(solution)/shard_map/ppermute | solution.py:36
  13.7 1.5 %collective-permute-start.8 = (bf16[256,512]{1,0:T(8,128)(2,1)S(1)}, bf16[256,512]{1,0:T(8,128)(2,1)S(1)}, u32[]{:S(2)}, u32[]{:S(2)}) collective-permute-start(bf16[256,512]{1,0:T(8,128)(2,1)S(1)} %get-tuple-element.53.refs_3_), channel_id=1, source_target_pairs={{0,6},{1,3},{2,4},{3,1},{4,2},{5,7},{6,0},{7,5},{8,14},{9,11},{10,... | collective-permute-start | bytes 786440 | tf_op jit(solution)/shard_map/ppermute | solution.py:36
  15.1 1.5 %collective-permute-done.3.refs_1_ = bf16[256,512]{1,0:T(8,128)(2,1)S(1)} collective-permute-done((bf16[256,512]{1,0:T(8,128)(2,1)S(1)}, bf16[256,512]{1,0:T(8,128)(2,1)S(1)}, u32[]{:S(2)}, u32[]{:S(2)}) %collective-permute-start.3) | collective-permute-done | bytes 262176 | tf_op jit(solution)/shard_map/ppermute | solution.py:36
  18.3 3.7 %collective-permute-done.7.refs_0_ = bf16[256,512]{1,0:T(8,128)(2,1)S(1)} collective-permute-done((bf16[256,512]{1,0:T(8,128)(2,1)S(1)}, bf16[256,512]{1,0:T(8,128)(2,1)S(1)}, u32[]{:S(2)}, u32[]{:S(2)}) %collective-permute-start.7) | collective-permute-done | bytes 262176 | tf_op jit(solution)/shard_map/ppermute | solution.py:36
  26.1 4.0 %collective-permute-start.11 = (bf16[80,512]{1,0:T(8,128)(2,1)S(1)}, bf16[80,512]{1,0:T(8,128)(2,1)S(1)}, u32[]{:S(2)}, u32[]{:S(2)}) collective-permute-start(bf16[80,512]{1,0:T(8,128)(2,1)S(1)} %get-tuple-element.68), channel_id=1, source_target_pairs={{0,16},{1,17},{2,18},{3,19},{4,20},{5,21},{6,22},{7,23},{8,24},{9,... | collective-permute-start | bytes 245768 | tf_op jit(solution)/shard_map/ppermute | solution.py:53
  31.1 2.5 %gates.1.refs_5_.refs_7_ = f32[512,512]{1,0:T(8,128)S(1)} custom-call(bf16[512,512]{1,0:T(8,128)(2,1)S(1)} %copy-done.4, bf16[512,512]{1,0:T(8,128)(2,1)S(1)} %collective-permute-done.refs_1_, bf16[512,512]{1,0:T(8,128)(2,1)S(1)} %get-tuple-element.54.refs_0_.refs_2_, bf16[512,512]{1,0:T(8,128)(2,1)S(1)} %get-tuple-element.55.refs_1_.refs_3_, ...), custom_call_target="tpu_custom_call" | custom-call | flops 2147483648 | bytes 4194305 | tf_op jit(solution)/shard_map/gates/pallas_call | solution.py:76
  33.6 3.0 %collective-permute-done.12.refs_3_ = bf16[80,512]{1,0:T(8,128)(2,1)S(1)} collective-permute-done((bf16[80,512]{1,0:T(8,128)(2,1)S(1)}, bf16[80,512]{1,0:T(8,128)(2,1)S(1)}, u32[]{:S(2)}, u32[]{:S(2)}) %collective-permute-start.12) | collective-permute-done | bytes 81952 | tf_op jit(solution)/shard_map/ppermute | solution.py:53
  36.7 3.1 %collective-permute-start.14 = (bf16[80,512]{1,0:T(8,128)(2,1)S(1)}, bf16[80,512]{1,0:T(8,128)(2,1)S(1)}, u32[]{:S(2)}, u32[]{:S(2)}) collective-permute-start(bf16[80,512]{1,0:T(8,128)(2,1)S(1)} %line.1.refs_11_), channel_id=1, source_target_pairs={{0,64},{1,65},{2,66},{3,67},{4,68},{5,69},{6,70},{7,71},{8,72},{9,... | collective-permute-start | bytes 245768 | tf_op jit(solution)/shard_map/ppermute | solution.py:53
  39.8 1.1 %collective-permute-start.15 = (bf16[80,512]{1,0:T(8,128)(2,1)S(1)}, bf16[80,512]{1,0:T(8,128)(2,1)S(1)}, u32[]{:S(2)}, u32[]{:S(2)}) collective-permute-start(bf16[80,512]{1,0:T(8,128)(2,1)S(1)} %line.1.refs_11_), channel_id=1, source_target_pairs={{0,96},{1,33},{2,98},{3,35},{4,100},{5,37},{6,102},{7,39},{8,104},... | collective-permute-start | bytes 245768 | tf_op jit(solution)/shard_map/ppermute | solution.py:53
  40.9 1.3 %queries.1.refs_8_.refs_0_ = f32[512,256]{1,0:T(8,128)S(1)} custom-call(bf16[512,512]{1,0:T(8,128)(2,1)S(1)} %copy-done.4, bf16[512,512]{1,0:T(8,128)(2,1)S(1)} %collective-permute-done.refs_1_, bf16[512,512]{1,0:T(8,128)(2,1)S(1)} %get-tuple-element.54.refs_0_.refs_2_, bf16[512,512]{1,0:T(8,128)(2,1)S(1)} %get-tuple-element.55.refs_1_.refs_3_, ...), custom_call_target="tpu_custom_call" | custom-call | flops 1073741824 | bytes 2097153 | tf_op jit(solution)/shard_map/queries/pallas_call | solution.py:76
  42.7 2.7 %collective-permute-done.15.refs_6_ = bf16[80,512]{1,0:T(8,128)(2,1)S(1)} collective-permute-done((bf16[80,512]{1,0:T(8,128)(2,1)S(1)}, bf16[80,512]{1,0:T(8,128)(2,1)S(1)}, u32[]{:S(2)}, u32[]{:S(2)}) %collective-permute-start.15) | collective-permute-done | bytes 81952 | tf_op jit(solution)/shard_map/ppermute | solution.py:53
  45.8 1.9 %collective-permute-start.17 = (bf16[64,512]{1,0:T(8,128)(2,1)S(1)}, bf16[64,512]{1,0:T(8,128)(2,1)S(1)}, u32[]{:S(2)}, u32[]{:S(2)}) collective-permute-start(bf16[64,512]{1,0:T(8,128)(2,1)S(1)} %get-tuple-element.75), channel_id=1, source_target_pairs={{0,16},{1,17},{2,18},{3,19},{4,20},{5,21},{6,22},{7,23},{8,24},{9,... | collective-permute-start | bytes 196616 | tf_op jit(solution)/shard_map/ppermute | solution.py:53
  50.1 1.8 %collective-permute-done.17.refs_2_ = bf16[64,512]{1,0:T(8,128)(2,1)S(1)} collective-permute-done((bf16[64,512]{1,0:T(8,128)(2,1)S(1)}, bf16[64,512]{1,0:T(8,128)(2,1)S(1)}, u32[]{:S(2)}, u32[]{:S(2)}) %collective-permute-start.17) | collective-permute-done | bytes 65568 | tf_op jit(solution)/shard_map/ppermute | solution.py:53
  51.9 1.2 %collective-permute-done.18.refs_3_ = bf16[64,512]{1,0:T(8,128)(2,1)S(1)} collective-permute-done((bf16[64,512]{1,0:T(8,128)(2,1)S(1)}, bf16[64,512]{1,0:T(8,128)(2,1)S(1)}, u32[]{:S(2)}, u32[]{:S(2)}) %collective-permute-start.18) | collective-permute-done | bytes 65568 | tf_op jit(solution)/shard_map/ppermute | solution.py:53
  56.1 3.1 %collective-permute-start.28 = (bf16[256,512]{1,0:T(8,128)(2,1)S(1)}, bf16[256,512]{1,0:T(8,128)(2,1)S(1)}, u32[]{:S(2)}, u32[]{:S(2)}) collective-permute-start(bf16[256,512]{1,0:T(8,128)(2,1)S(1)} %far1.1.refs_7_), channel_id=1, source_target_pairs={{0,6},{1,3},{2,4},{3,1},{4,2},{5,7},{6,0},{7,5},{8,14},{9,11},{10,... | collective-permute-start | bytes 786440 | tf_op jit(solution)/shard_map/ppermute | solution.py:36
  59.2 1.2 %beside.1 = (f32[256,512]{1,0:T(8,128)S(1)}, bf16[256,512]{1,0:T(8,128)(2,1)S(1)}, bf16[256,512]{1,0:T(8,128)(2,1)S(1)}, f32[256,512]{1,0:T(8,128)S(1)}) custom-call(bf16[256,512]{1,0:T(8,128)(2,1)S(1)} %hidden0.1.refs_8_.refs_0_, bf16[256,512]{1,0:T(8,128)(2,1)S(1)} %hidden1.1.refs_1_, bf16[256,512]{1,0:T(8,128)(2,1)S(1)} %collective-permute-done.20.refs_1_.refs_2_, ...), custom_call_target="tpu_custom_call" | custom-call | flops 1073741824 | bytes 2097152 | tf_op jit(solution)/shard_map/beside/pallas_call | solution.py:76
  60.5 2.1 %collective-permute-start.24 = (bf16[256,512]{1,0:T(8,128)(2,1)S(1)}, bf16[256,512]{1,0:T(8,128)(2,1)S(1)}, u32[]{:S(2)}, u32[]{:S(2)}) collective-permute-start(bf16[256,512]{1,0:T(8,128)(2,1)S(1)} %get-tuple-element.83), channel_id=1, source_target_pairs={{0,2},{1,7},{2,0},{3,5},{4,6},{5,3},{6,4},{7,1},{8,10},{9,15},{10,... | collective-permute-start | bytes 786440 | tf_op jit(solution)/shard_map/ppermute | solution.py:36
  62.8 3.7 %collective-permute-done.28 = bf16[256,512]{1,0:T(8,128)(2,1)S(1)} collective-permute-done((bf16[256,512]{1,0:T(8,128)(2,1)S(1)}, bf16[256,512]{1,0:T(8,128)(2,1)S(1)}, u32[]{:S(2)}, u32[]{:S(2)}) %collective-permute-start.28) | collective-permute-done | bytes 262176 | tf_op jit(solution)/shard_map/ppermute | solution.py:36
  67.9 2.0 %collective-permute-start.27 = (bf16[256,512]{1,0:T(8,128)(2,1)S(1)}, bf16[256,512]{1,0:T(8,128)(2,1)S(1)}, u32[]{:S(2)}, u32[]{:S(2)}) collective-permute-start(bf16[256,512]{1,0:T(8,128)(2,1)S(1)} %add_convert_fusion.1), channel_id=1, source_target_pairs={{0,6},{1,3},{2,4},{3,1},{4,2},{5,7},{6,0},{7,5},{8,14},{9,11},{10,... | collective-permute-start | bytes 786440 | tf_op jit(solution)/shard_map/ppermute | solution.py:36
  69.9 2.7 %collective-permute-done.24.refs_6_ = bf16[256,512]{1,0:T(8,128)(2,1)S(1)} collective-permute-done((bf16[256,512]{1,0:T(8,128)(2,1)S(1)}, bf16[256,512]{1,0:T(8,128)(2,1)S(1)}, u32[]{:S(2)}, u32[]{:S(2)}) %collective-permute-start.24) | collective-permute-done | bytes 262176 | tf_op jit(solution)/shard_map/ppermute | solution.py:36
  73.8 3.1 %collective-permute-done.29.refs_3_ = bf16[256,512]{1,0:T(8,128)(2,1)S(1)} collective-permute-done((bf16[256,512]{1,0:T(8,128)(2,1)S(1)}, bf16[256,512]{1,0:T(8,128)(2,1)S(1)}, u32[]{:S(2)}, u32[]{:S(2)}) %collective-permute-start.29) | collective-permute-done | bytes 262176 | tf_op jit(solution)/shard_map/ppermute | solution.py:36
  (78 shorter events, 22.3 us)
Async XLA Ops:
  0.0 8.6 %collective-permute-start = (bf16[512,512]{1,0:T(8,128)(2,1)}, bf16[512,512]{1,0:T(8,128)(2,1)S(1)}, u32[]{:S(2)}, u32[]{:S(2)}) collective-permute-start(bf16[512,512]{1,0:T(8,128)(2,1)} %refs_0_.11), channel_id=1, source_target_pairs={{0,1},{1,0},{2,3},{3,2},{4,5},{5,4},{6,7},{7,6},{8,9},{9,8},{10,11... | collective-permute-start | bytes 1572872 | tf_op jit(solution)/shard_map/ppermute | solution.py:40
  1.1 10.5 %collective-permute-start.1 = (bf16[256,512]{1,0:T(8,128)(2,1)S(1)}, bf16[256,512]{1,0:T(8,128)(2,1)S(1)}, u32[]{:S(2)}, u32[]{:S(2)}) collective-permute-start(bf16[256,512]{1,0:T(8,128)(2,1)S(1)} %get-tuple-element.47), channel_id=1, source_target_pairs={{0,6},{1,3},{2,4},{3,1},{4,2},{5,7},{6,0},{7,5},{8,14},{9,11},{10,... | collective-permute-start | bytes 786440 | tf_op jit(solution)/shard_map/ppermute | solution.py:36
  4.3 8.9 %collective-permute-start.2 = (bf16[256,512]{1,0:T(8,128)(2,1)S(1)}, bf16[256,512]{1,0:T(8,128)(2,1)S(1)}, u32[]{:S(2)}, u32[]{:S(2)}) collective-permute-start(bf16[256,512]{1,0:T(8,128)(2,1)S(1)} %get-tuple-element.48), channel_id=1, source_target_pairs={{0,2},{1,7},{2,0},{3,5},{4,6},{5,3},{6,4},{7,1},{8,10},{9,15},{10,... | collective-permute-start | bytes 786440 | tf_op jit(solution)/shard_map/ppermute | solution.py:36
  4.4 12.2 %collective-permute-start.3 = (bf16[256,512]{1,0:T(8,128)(2,1)S(1)}, bf16[256,512]{1,0:T(8,128)(2,1)S(1)}, u32[]{:S(2)}, u32[]{:S(2)}) collective-permute-start(bf16[256,512]{1,0:T(8,128)(2,1)S(1)} %get-tuple-element.48), channel_id=1, source_target_pairs={{0,6},{1,3},{2,4},{3,1},{4,2},{5,7},{6,0},{7,5},{8,14},{9,11},{10,... | collective-permute-start | bytes 786440 | tf_op jit(solution)/shard_map/ppermute | solution.py:36
  5.5 11.1 %collective-permute-start.4 = (bf16[256,512]{1,0:T(8,128)(2,1)S(1)}, bf16[256,512]{1,0:T(8,128)(2,1)S(1)}, u32[]{:S(2)}, u32[]{:S(2)}) collective-permute-start(bf16[256,512]{1,0:T(8,128)(2,1)S(1)} %get-tuple-element.47), channel_id=1, source_target_pairs={{0,2},{1,7},{2,0},{3,5},{4,6},{5,3},{6,4},{7,1},{8,10},{9,15},{10,... | collective-permute-start | bytes 786440 | tf_op jit(solution)/shard_map/ppermute | solution.py:36
  8.6 50.7 %collective-permute-start.22 = (bf16[512,1536]{1,0:T(8,128)(2,1)S(1)}, bf16[512,1536]{1,0:T(8,128)(2,1)S(1)}, u32[]{:S(2)}, u32[]{:S(2)}) collective-permute-start(bf16[512,1536]{1,0:T(8,128)(2,1)S(1)} %get-tuple-element.81), channel_id=1, source_target_pairs={{0,1},{1,0},{2,3},{3,2},{4,5},{5,4},{6,7},{7,6},{8,9},{9,8},{10,11... | collective-permute-start | bytes 4718600 | tf_op jit(solution)/shard_map/ppermute | solution.py:40
  13.2 8.8 %collective-permute-start.7 = (bf16[256,512]{1,0:T(8,128)(2,1)S(1)}, bf16[256,512]{1,0:T(8,128)(2,1)S(1)}, u32[]{:S(2)}, u32[]{:S(2)}) collective-permute-start(bf16[256,512]{1,0:T(8,128)(2,1)S(1)} %get-tuple-element.52.refs_0_), channel_id=1, source_target_pairs={{0,2},{1,7},{2,0},{3,5},{4,6},{5,3},{6,4},{7,1},{8,10},{9,15},{10,... | collective-permute-start | bytes 786440 | tf_op jit(solution)/shard_map/ppermute | solution.py:36
  13.7 9.1 %collective-permute-start.8 = (bf16[256,512]{1,0:T(8,128)(2,1)S(1)}, bf16[256,512]{1,0:T(8,128)(2,1)S(1)}, u32[]{:S(2)}, u32[]{:S(2)}) collective-permute-start(bf16[256,512]{1,0:T(8,128)(2,1)S(1)} %get-tuple-element.53.refs_3_), channel_id=1, source_target_pairs={{0,6},{1,3},{2,4},{3,1},{4,2},{5,7},{6,0},{7,5},{8,14},{9,11},{10,... | collective-permute-start | bytes 786440 | tf_op jit(solution)/shard_map/ppermute | solution.py:36
  16.7 7.2 %collective-permute-start.5 = (bf16[512,512]{1,0:T(8,128)(2,1)S(1)}, bf16[512,512]{1,0:T(8,128)(2,1)S(1)}, u32[]{:S(2)}, u32[]{:S(2)}) collective-permute-start(bf16[512,512]{1,0:T(8,128)(2,1)S(1)} %get-tuple-element.54.refs_0_.refs_2_), channel_id=1, source_target_pairs={{0,1},{1,0},{2,3},{3,2},{4,5},{5,4},{6,7},{7,6},{8,9},{9,8},{10,11... | collective-permute-start | bytes 1572872 | tf_op jit(solution)/shard_map/ppermute | solution.py:40
  17.2 6.9 %collective-permute-start.6 = (bf16[512,512]{1,0:T(8,128)(2,1)S(1)}, bf16[512,512]{1,0:T(8,128)(2,1)S(1)}, u32[]{:S(2)}, u32[]{:S(2)}) collective-permute-start(bf16[512,512]{1,0:T(8,128)(2,1)S(1)} %get-tuple-element.55.refs_1_.refs_3_), channel_id=1, source_target_pairs={{0,1},{1,0},{2,3},{3,2},{4,5},{5,4},{6,7},{7,6},{8,9},{9,8},{10,11... | collective-permute-start | bytes 1572872 | tf_op jit(solution)/shard_map/ppermute | solution.py:40
  23.9 31.2 %collective-permute-start.23 = (bf16[512,512]{1,0:T(8,128)(2,1)S(1)}, bf16[512,512]{1,0:T(8,128)(2,1)S(1)}, u32[]{:S(2)}, u32[]{:S(2)}) collective-permute-start(bf16[512,512]{1,0:T(8,128)(2,1)S(1)} %get-tuple-element.82), channel_id=1, source_target_pairs={{0,1},{1,0},{2,3},{3,2},{4,5},{5,4},{6,7},{7,6},{8,9},{9,8},{10,11... | collective-permute-start | bytes 1572872 | tf_op jit(solution)/shard_map/ppermute | solution.py:40
  26.1 7.6 %collective-permute-start.11 = (bf16[80,512]{1,0:T(8,128)(2,1)S(1)}, bf16[80,512]{1,0:T(8,128)(2,1)S(1)}, u32[]{:S(2)}, u32[]{:S(2)}) collective-permute-start(bf16[80,512]{1,0:T(8,128)(2,1)S(1)} %get-tuple-element.68), channel_id=1, source_target_pairs={{0,16},{1,17},{2,18},{3,19},{4,20},{5,21},{6,22},{7,23},{8,24},{9,... | collective-permute-start | bytes 245768 | tf_op jit(solution)/shard_map/ppermute | solution.py:53
  30.1 6.5 %collective-permute-start.12 = (bf16[80,512]{1,0:T(8,128)(2,1)S(1)}, bf16[80,512]{1,0:T(8,128)(2,1)S(1)}, u32[]{:S(2)}, u32[]{:S(2)}) collective-permute-start(bf16[80,512]{1,0:T(8,128)(2,1)S(1)} %get-tuple-element.69), channel_id=1, source_target_pairs={{0,24},{1,9},{2,26},{3,11},{4,28},{5,13},{6,30},{7,15},{8,16},{9,1... | collective-permute-start | bytes 245768 | tf_op jit(solution)/shard_map/ppermute | solution.py:53
  30.8 5.8 %collective-permute-start.13 = (bf16[80,512]{1,0:T(8,128)(2,1)S(1)}, bf16[80,512]{1,0:T(8,128)(2,1)S(1)}, u32[]{:S(2)}, u32[]{:S(2)}) collective-permute-start(bf16[80,512]{1,0:T(8,128)(2,1)S(1)} %get-tuple-element.70), channel_id=1, source_target_pairs={{0,8},{1,25},{2,10},{3,27},{4,12},{5,29},{6,14},{7,31},{8,0},{9,17... | collective-permute-start | bytes 245768 | tf_op jit(solution)/shard_map/ppermute | solution.py:53
  36.7 6.0 %collective-permute-start.14 = (bf16[80,512]{1,0:T(8,128)(2,1)S(1)}, bf16[80,512]{1,0:T(8,128)(2,1)S(1)}, u32[]{:S(2)}, u32[]{:S(2)}) collective-permute-start(bf16[80,512]{1,0:T(8,128)(2,1)S(1)} %line.1.refs_11_), channel_id=1, source_target_pairs={{0,64},{1,65},{2,66},{3,67},{4,68},{5,69},{6,70},{7,71},{8,72},{9,... | collective-permute-start | bytes 245768 | tf_op jit(solution)/shard_map/ppermute | solution.py:53
  39.8 5.7 %collective-permute-start.15 = (bf16[80,512]{1,0:T(8,128)(2,1)S(1)}, bf16[80,512]{1,0:T(8,128)(2,1)S(1)}, u32[]{:S(2)}, u32[]{:S(2)}) collective-permute-start(bf16[80,512]{1,0:T(8,128)(2,1)S(1)} %line.1.refs_11_), channel_id=1, source_target_pairs={{0,96},{1,33},{2,98},{3,35},{4,100},{5,37},{6,102},{7,39},{8,104},... | collective-permute-start | bytes 245768 | tf_op jit(solution)/shard_map/ppermute | solution.py:53
  45.8 6.1 %collective-permute-start.17 = (bf16[64,512]{1,0:T(8,128)(2,1)S(1)}, bf16[64,512]{1,0:T(8,128)(2,1)S(1)}, u32[]{:S(2)}, u32[]{:S(2)}) collective-permute-start(bf16[64,512]{1,0:T(8,128)(2,1)S(1)} %get-tuple-element.75), channel_id=1, source_target_pairs={{0,16},{1,17},{2,18},{3,19},{4,20},{5,21},{6,22},{7,23},{8,24},{9,... | collective-permute-start | bytes 196616 | tf_op jit(solution)/shard_map/ppermute | solution.py:53
  47.6 5.5 %collective-permute-start.18 = (bf16[64,512]{1,0:T(8,128)(2,1)S(1)}, bf16[64,512]{1,0:T(8,128)(2,1)S(1)}, u32[]{:S(2)}, u32[]{:S(2)}) collective-permute-start(bf16[64,512]{1,0:T(8,128)(2,1)S(1)} %get-tuple-element.76), channel_id=1, source_target_pairs={{0,24},{1,9},{2,26},{3,11},{4,28},{5,13},{6,30},{7,15},{8,16},{9,1... | collective-permute-start | bytes 196616 | tf_op jit(solution)/shard_map/ppermute | solution.py:53
  56.1 10.4 %collective-permute-start.28 = (bf16[256,512]{1,0:T(8,128)(2,1)S(1)}, bf16[256,512]{1,0:T(8,128)(2,1)S(1)}, u32[]{:S(2)}, u32[]{:S(2)}) collective-permute-start(bf16[256,512]{1,0:T(8,128)(2,1)S(1)} %far1.1.refs_7_), channel_id=1, source_target_pairs={{0,6},{1,3},{2,4},{3,1},{4,2},{5,7},{6,0},{7,5},{8,14},{9,11},{10,... | collective-permute-start | bytes 786440 | tf_op jit(solution)/shard_map/ppermute | solution.py:36
  59.2 8.6 %collective-permute-start.26 = (bf16[256,512]{1,0:T(8,128)(2,1)S(1)}, bf16[256,512]{1,0:T(8,128)(2,1)S(1)}, u32[]{:S(2)}, u32[]{:S(2)}) collective-permute-start(bf16[256,512]{1,0:T(8,128)(2,1)S(1)} %far0.1.refs_3_.refs_6_), channel_id=1, source_target_pairs={{0,2},{1,7},{2,0},{3,5},{4,6},{5,3},{6,4},{7,1},{8,10},{9,15},{10,... | collective-permute-start | bytes 786440 | tf_op jit(solution)/shard_map/ppermute | solution.py:36
  60.5 12.1 %collective-permute-start.24 = (bf16[256,512]{1,0:T(8,128)(2,1)S(1)}, bf16[256,512]{1,0:T(8,128)(2,1)S(1)}, u32[]{:S(2)}, u32[]{:S(2)}) collective-permute-start(bf16[256,512]{1,0:T(8,128)(2,1)S(1)} %get-tuple-element.83), channel_id=1, source_target_pairs={{0,2},{1,7},{2,0},{3,5},{4,6},{5,3},{6,4},{7,1},{8,10},{9,15},{10,... | collective-permute-start | bytes 786440 | tf_op jit(solution)/shard_map/ppermute | solution.py:36
  62.6 10.5 %collective-permute-start.25 = (bf16[256,512]{1,0:T(8,128)(2,1)S(1)}, bf16[256,512]{1,0:T(8,128)(2,1)S(1)}, u32[]{:S(2)}, u32[]{:S(2)}) collective-permute-start(bf16[256,512]{1,0:T(8,128)(2,1)S(1)} %get-tuple-element.84), channel_id=1, source_target_pairs={{0,6},{1,3},{2,4},{3,1},{4,2},{5,7},{6,0},{7,5},{8,14},{9,11},{10,... | collective-permute-start | bytes 786440 | tf_op jit(solution)/shard_map/ppermute | solution.py:36
  66.6 10.2 %collective-permute-start.29 = (bf16[256,512]{1,0:T(8,128)(2,1)S(1)}, bf16[256,512]{1,0:T(8,128)(2,1)S(1)}, u32[]{:S(2)}, u32[]{:S(2)}) collective-permute-start(bf16[256,512]{1,0:T(8,128)(2,1)S(1)} %add_convert_fusion), channel_id=1, source_target_pairs={{0,2},{1,7},{2,0},{3,5},{4,6},{5,3},{6,4},{7,1},{8,10},{9,15},{10,... | collective-permute-start | bytes 786440 | tf_op jit(solution)/shard_map/ppermute | solution.py:36
  67.9 9.5 %collective-permute-start.27 = (bf16[256,512]{1,0:T(8,128)(2,1)S(1)}, bf16[256,512]{1,0:T(8,128)(2,1)S(1)}, u32[]{:S(2)}, u32[]{:S(2)}) collective-permute-start(bf16[256,512]{1,0:T(8,128)(2,1)S(1)} %add_convert_fusion.1), channel_id=1, source_target_pairs={{0,6},{1,3},{2,4},{3,1},{4,2},{5,7},{6,0},{7,5},{8,14},{9,11},{10,... | collective-permute-start | bytes 786440 | tf_op jit(solution)/shard_map/ppermute | solution.py:36
  (14 other events, 58.0 us)
